TPU v7x, 32 devices: a whole 2x2x4 slice. The times are simulated.
32 devices in a mesh: seq: 8 (over y, x, core), head: 4 (over z).
Axes of the slice: x: 2, y: 2, z: 4, core: 2. Of those that a mesh axis runs over, the one named last changes fastest.
Arguments:
- hidden_in: bfloat16 [4096, 1536], P('seq'), may hold values from -6 to 6
- cond: float32 [1024], replicated, may hold values from -6 to 6
- captions: bfloat16 [4, 128, 4096], replicated, may hold values from -6 to 6
- clip_lengths: int32 [4], replicated, may hold values from 1 to 3585, 4096 in all
- ada_weight: bfloat16 [1024, 6144], P(None, ('seq', 'head')), may hold values from -0.1875 to 0.1875
- norm_gains: float32 [4, 1536], replicated, may hold values from 0.5 to 1.5
- qk_gains: float32 [2, 64], replicated, may hold values from 0.1 to 1.9
- w_query: bfloat16 [1536, 1536], P('seq', 'head'), may hold values from -0.15625 to 0.15625
- w_key: bfloat16 [1536, 1536], P('seq', 'head'), may hold values from -0.15625 to 0.15625
- w_value: bfloat16 [1536, 1536], P('seq', 'head'), may hold values from -0.15625 to 0.15625
- w_out: bfloat16 [1536, 1536], P('head', 'seq'), may hold values from -0.15625 to 0.15625
- cross_gate: float32 [24], P('head'), may hold values from 0.3 to 1.5
- w_text_key: bfloat16 [4096, 1536], P('seq', 'head'), may hold values from -0.09375 to 0.09375
- w_text_value: bfloat16 [4096, 1536], P('seq', 'head'), may hold values from -0.09375 to 0.09375
- w_gate: bfloat16 [1536, 4096], P('seq', 'head'), may hold values from -0.15625 to 0.15625
- w_up: bfloat16 [1536, 4096], P('seq', 'head'), may hold values from -0.15625 to 0.15625
- w_down: bfloat16 [4096, 1536], P('head', 'seq'), may hold values from -0.09375 to 0.09375
- out_cotangent: bfloat16 [4096, 1536], P('seq'), may hold values from -6 to 6
Outputs:
- hidden_out: bfloat16 [4096, 1536], P('seq')
- input_grad: float32 [4096, 1536], P('seq')
- ada_grad: float32 [1024, 6144], P(None, ('seq', 'head'))
- norm_gains_grad: float32 [4, 1536], replicated
- qk_gains_grad: float32 [2, 64], replicated
- query_grad: float32 [1536, 1536], P('seq', 'head')
- key_grad: float32 [1536, 1536], P('seq', 'head')
- value_grad: float32 [1536, 1536], P('seq', 'head')
- out_grad: float32 [1536, 1536], P('head', 'seq')
- cross_gate_grad: float32 [24], P('head')
- text_key_grad: float32 [4096, 1536], P('seq', 'head')
- text_value_grad: float32 [4096, 1536], P('seq', 'head')
- gate_grad: float32 [1536, 4096], P('seq', 'head')
- up_grad: float32 [1536, 4096], P('seq', 'head')
- down_grad: float32 [4096, 1536], P('head', 'seq')
Inputs may be any that keep to these rules, and one draw needn't show every extreme that they name: `clip_lengths`: the lengths sum to 4096; the longest clip has exactly 3585 tokens.
All inputs are finite; a program needn't handle non-finite values.
Results may differ from a plain program's by a relative error of at most 0.024.
Values may be sent and summed in bfloat16 or wider, within the bound.
No kernel may reach another device: no remote copies, remote signals or barrier semaphores. Data moves between devices by JAX's collectives and lax.ppermute only.
A program may use at most 192 MiB of HBM per device.

v0:
```python
import jax
import jax.numpy as jnp
from jax import lax
from jax.sharding import PartitionSpec as P

HD = 64


def mean_norm(value):
    return value * lax.rsqrt(jnp.mean(value * value, axis=-1, keepdims=True) + 1e-06)


def clip_places(clip_lengths, first, count):
    clip_ends = jnp.cumsum(clip_lengths, dtype=jnp.int32)
    starts = clip_ends - clip_lengths
    places = first + jnp.arange(count, dtype=jnp.int32)
    segment = jnp.sum(
        (places[:, None] >= clip_ends[None, :]).astype(jnp.int32), axis=1, dtype=jnp.int32
    )
    onehot = segment[:, None] == jnp.arange(clip_lengths.shape[0], dtype=jnp.int32)[None, :]
    position = places - jnp.sum(jnp.where(onehot, starts[None, :], 0), axis=1, dtype=jnp.int32)
    return (segment, position)


def rotate_pairs(value, position):
    half_dim = value.shape[-1] // 2
    frequency = 10000.0 ** (-jnp.arange(half_dim, dtype=jnp.float32) / half_dim)
    angles = position.astype(jnp.float32)[:, None] * frequency[None, :]
    cosine = jnp.cos(angles)[:, None, :]
    sine_value = jnp.sin(angles)[:, None, :]
    first_half = value[..., :half_dim]
    second_half = value[..., half_dim:]
    return jnp.concatenate(
        [
            first_half * cosine - second_half * sine_value,
            second_half * cosine + first_half * sine_value,
        ],
        axis=-1,
    )


def head_norm(flat, gain):
    shaped = flat.reshape(flat.shape[0], -1, HD)
    return (mean_norm(shaped) * gain).reshape(flat.shape)


def attn_input(x_value, gain_value, scale_value):
    return mean_norm(x_value) * gain_value * (1.0 + scale_value)


def branch_tail(x_value, branch, gain_value, gate_value):
    return x_value + jnp.tanh(gate_value) * mean_norm(branch) * gain_value


def swiglu_units(gate_pre, up_pre):
    return jax.nn.silu(gate_pre) * up_pre


def matmul(left, right):
    return jnp.dot(left, right, preferred_element_type=jnp.float32)


def per_device(
    hidden_in,
    cond,
    captions,
    clip_lengths,
    ada_weight,
    norm_gains,
    qk_gains,
    w_query,
    w_key,
    w_value,
    w_out,
    cross_gate,
    w_text_key,
    w_text_value,
    w_gate,
    w_up,
    w_down,
    out_cotangent,
):
    local_rows = hidden_in.shape[0]
    model_width = hidden_in.shape[1]
    seq_count = lax.axis_size("seq")
    all_rows = local_rows * seq_count
    seq_index = lax.axis_index("seq")
    head_index = lax.axis_index("head")
    score_scale = HD ** (-0.5)
    bf16 = jnp.bfloat16
    f32 = jnp.float32
    query_w, key_w, value_w, out_w, gate_w, up_w, down_w, text_key_w, text_value_w = (
        lax.all_gather(w_query, "seq", axis=0, tiled=True),
        lax.all_gather(w_key, "seq", axis=0, tiled=True),
        lax.all_gather(w_value, "seq", axis=0, tiled=True),
        lax.all_gather(w_out, "seq", axis=1, tiled=True),
        lax.all_gather(w_gate, "seq", axis=0, tiled=True),
        lax.all_gather(w_up, "seq", axis=0, tiled=True),
        lax.all_gather(w_down, "seq", axis=1, tiled=True),
        lax.all_gather(w_text_key, "seq", axis=0, tiled=True),
        lax.all_gather(w_text_value, "seq", axis=0, tiled=True),
    )
    cond_act = jax.nn.silu(cond).astype(bf16)
    mod_piece = matmul(cond_act[None, :], ada_weight)[0]
    modulation = lax.all_gather(mod_piece, ("seq", "head"), axis=0, tiled=True)
    scale_a = modulation[:model_width]
    gate_a = modulation[model_width : 2 * model_width]
    scale_f = modulation[2 * model_width : 3 * model_width]
    gate_f = modulation[3 * model_width :]
    segment, position = clip_places(clip_lengths, seq_index * local_rows, local_rows)
    all_segment, all_position = clip_places(clip_lengths, 0, all_rows)
    x_float = hidden_in.astype(f32)
    normed_a, pull_in_a = jax.vjp(attn_input, x_float, norm_gains[0], scale_a)
    act_a = normed_a.astype(bf16)
    query_pre = matmul(act_a, query_w)
    key_pre = matmul(act_a, key_w)
    value_pre = matmul(act_a, value_w)

    def rotary_norm(flat, gain):
        shaped = flat.reshape(flat.shape[0], -1, HD)
        return rotate_pairs(mean_norm(shaped) * gain, position).reshape(flat.shape)

    query_value, query_pull = jax.vjp(rotary_norm, query_pre, qk_gains[0])
    key_value, key_pull = jax.vjp(rotary_norm, key_pre, qk_gains[1])
    queries = query_value.astype(bf16)
    keys_local = key_value.astype(bf16)
    values_local = value_pre.astype(bf16)
    all_keys, all_values = (
        lax.all_gather(keys_local, "seq", axis=0, tiled=True),
        lax.all_gather(values_local, "seq", axis=0, tiled=True),
    )
    text_rows = captions.reshape(-1, captions.shape[2])
    text_count = text_rows.shape[0]
    text_key_pre = matmul(text_rows, text_key_w)
    text_value_pre = matmul(text_rows, text_value_w)
    text_key_value, text_pull = jax.vjp(head_norm, text_key_pre, qk_gains[1])
    local_heads = query_w.shape[1] // HD
    text_keys3 = text_key_value.astype(bf16).reshape(text_count, local_heads, HD)
    text_values3 = text_value_pre.astype(bf16).reshape(text_count, local_heads, HD)
    query3 = queries.reshape(local_rows, local_heads, HD)
    block_rows = min(512, all_rows)
    block_count = all_rows // block_rows
    segment_blocks = all_segment.reshape(block_count, block_rows)

    def block_scores(key_block, segment_block):
        raw = jnp.einsum("qhd,khd->hqk", query3, key_block, preferred_element_type=f32)
        allowed = (segment[:, None] == segment_block[None, :])[None]
        return (jnp.where(allowed, score_scale * raw, -1e30), allowed)

    def stat_step(carry, blocks_in):
        run_max, run_sum = carry
        scores, allowed = block_scores(blocks_in[0], blocks_in[1])
        new_max = jnp.maximum(run_max, jnp.max(scores, axis=2))
        weights = jnp.where(allowed, jnp.exp(scores - new_max[..., None]), 0.0)
        return ((new_max, run_sum * jnp.exp(run_max - new_max) + jnp.sum(weights, axis=2)), None)

    key_blocks = all_keys.reshape(block_count, block_rows, local_heads, HD)
    value_blocks = all_values.reshape(block_count, block_rows, local_heads, HD)
    start_max = jnp.full((local_heads, local_rows), -1e30, f32)
    start_sum = jnp.zeros((local_heads, local_rows), f32)
    (row_max, row_sum), unused = lax.scan(
        stat_step, (start_max, start_sum), (key_blocks, segment_blocks)
    )
    log_total = row_max + jnp.log(row_sum)

    def value_step(carry, blocks_in):
        scores, allowed = block_scores(blocks_in[0], blocks_in[2])
        probs = jnp.where(allowed, jnp.exp(scores - log_total[..., None]), 0.0).astype(bf16)
        return (
            carry + jnp.einsum("hqk,khd->qhd", probs, blocks_in[1], preferred_element_type=f32),
            None,
        )

    self_out, unused = lax.scan(
        value_step,
        jnp.zeros((local_rows, local_heads, HD), f32),
        (key_blocks, value_blocks, segment_blocks),
    )
    key_clip = jnp.arange(text_count, dtype=jnp.int32) // captions.shape[1]
    cross_allowed = (segment[:, None] == key_clip[None, :])[None]
    cross_raw = jnp.einsum("qhd,khd->hqk", query3, text_keys3, preferred_element_type=f32)
    cross_scores = jnp.where(cross_allowed, score_scale * cross_raw, -1e30)
    cross_max = jnp.max(cross_scores, axis=2, keepdims=True)
    cross_exp = jnp.exp(cross_scores - cross_max)
    cross_probs = cross_exp / jnp.sum(cross_exp, axis=2, keepdims=True)
    cross_low = cross_probs.astype(bf16)
    cross_out = jnp.einsum("hqk,khd->qhd", cross_low, text_values3, preferred_element_type=f32)
    gate_local = jnp.tanh(cross_gate)
    mixed = (self_out + gate_local[None, :, None] * cross_out).reshape(local_rows, -1).astype(bf16)
    attn_sum = lax.psum(matmul(mixed, out_w).astype(jnp.bfloat16), "head").astype(jnp.float32)
    x_mid, pull_tail_a = jax.vjp(branch_tail, x_float, attn_sum, norm_gains[1], gate_a)
    normed_f, pull_in_f = jax.vjp(attn_input, x_mid, norm_gains[2], scale_f)
    act_f = normed_f.astype(bf16)
    gate_pre = matmul(act_f, gate_w)
    up_pre = matmul(act_f, up_w)
    unit_value, unit_pull = jax.vjp(swiglu_units, gate_pre, up_pre)
    hidden_units = unit_value.astype(bf16)
    ffn_sum = lax.psum(matmul(hidden_units, down_w).astype(jnp.bfloat16), "head").astype(
        jnp.float32
    )
    out_value, pull_tail_f = jax.vjp(branch_tail, x_mid, ffn_sum, norm_gains[3], gate_f)
    hidden_out = out_value.astype(bf16)
    grad_mid, grad_ffn, grad_gain_fo, grad_gate_f = pull_tail_f(out_cotangent.astype(f32))
    grad_ffn_low = grad_ffn.astype(bf16)
    grad_units = matmul(grad_ffn_low, down_w.T)
    down_part = matmul(hidden_units.T, grad_ffn_low)
    grad_gate_pre, grad_up_pre = unit_pull(grad_units)
    grad_gate_low = grad_gate_pre.astype(bf16)
    grad_up_low = grad_up_pre.astype(bf16)
    gate_part = matmul(act_f.T, grad_gate_low)
    up_part = matmul(act_f.T, grad_up_low)
    grad_act_f = lax.psum(
        (matmul(grad_gate_low, gate_w.T) + matmul(grad_up_low, up_w.T)).astype(jnp.bfloat16), "head"
    ).astype(jnp.float32)
    grad_mid_f, grad_gain_fi, grad_scale_f = pull_in_f(grad_act_f)
    grad_x_tail, grad_attn, grad_gain_ao, grad_gate_a = pull_tail_a(grad_mid + grad_mid_f)
    grad_attn_low = grad_attn.astype(bf16)
    grad_mixed = matmul(grad_attn_low, out_w.T).reshape(local_rows, local_heads, HD)
    out_part = matmul(mixed.T, grad_attn_low)
    grad_self = grad_mixed.astype(bf16)
    grad_cross = (gate_local[None, :, None] * grad_mixed).astype(bf16)
    cross_gate_part = jnp.sum(grad_mixed * cross_out, axis=(0, 2)) * (1.0 - gate_local * gate_local)
    cross_delta = jnp.sum(grad_cross.astype(f32) * cross_out, axis=2).T
    cross_dprob = jnp.einsum("qhd,khd->hqk", grad_cross, text_values3, preferred_element_type=f32)
    cross_raw_grad = (cross_probs * (cross_dprob - cross_delta[..., None]) * score_scale).astype(
        bf16
    )
    grad_query_cross = jnp.einsum(
        "hqk,khd->qhd", cross_raw_grad, text_keys3, preferred_element_type=f32
    )
    text_key_part = jnp.einsum("hqk,qhd->khd", cross_raw_grad, query3, preferred_element_type=f32)
    text_value_part = jnp.einsum("hqk,qhd->khd", cross_low, grad_cross, preferred_element_type=f32)
    self_delta = jnp.sum(grad_self.astype(f32) * self_out, axis=2).T

    def score_grads(
        query_block,
        grad_block,
        segment_query,
        segment_key,
        key_block,
        value_block,
        total_block,
        delta_block,
    ):
        raw = jnp.einsum("qhd,khd->hqk", query_block, key_block, preferred_element_type=f32)
        allowed = (segment_query[:, None] == segment_key[None, :])[None]
        scores = jnp.where(allowed, score_scale * raw, -1e30)
        probs = jnp.where(allowed, jnp.exp(scores - total_block[..., None]), 0.0)
        dprob = jnp.einsum("qhd,khd->hqk", grad_block, value_block, preferred_element_type=f32)
        raw_grad = (probs * (dprob - delta_block[..., None]) * score_scale).astype(bf16)
        return (probs, raw_grad)

    def grad_step(carry, blocks_in):
        key_block, value_block, segment_block = blocks_in
        probs, raw_grad = score_grads(
            query3, grad_self, segment, segment_block, key_block, value_block, log_total, self_delta
        )
        carry = carry + jnp.einsum("hqk,khd->qhd", raw_grad, key_block, preferred_element_type=f32)
        key_block_grad = jnp.einsum("hqk,qhd->khd", raw_grad, query3, preferred_element_type=f32)
        value_block_grad = jnp.einsum(
            "hqk,qhd->khd", probs.astype(bf16), grad_self, preferred_element_type=f32
        )
        return (carry, (key_block_grad, value_block_grad))

    grad_query_self, (key_grad_blocks, value_grad_blocks) = lax.scan(
        grad_step,
        jnp.zeros((local_rows, local_heads, HD), f32),
        (key_blocks, value_blocks, segment_blocks),
    )
    own_key_grad, own_value_grad = (
        lax.psum_scatter(
            key_grad_blocks.reshape(all_rows, -1).astype(jnp.bfloat16),
            "seq",
            scatter_dimension=0,
            tiled=True,
        ).astype(jnp.float32),
        lax.psum_scatter(
            value_grad_blocks.reshape(all_rows, -1).astype(jnp.bfloat16),
            "seq",
            scatter_dimension=0,
            tiled=True,
        ).astype(jnp.float32),
    )
    grad_query_total = (grad_query_self + grad_query_cross).reshape(local_rows, -1)
    grad_query_pre, grad_query_gain = query_pull(grad_query_total)
    grad_key_pre, grad_key_gain = key_pull(own_key_grad)
    text_key_pre_grad, text_gain_grad = text_pull(text_key_part.reshape(text_count, -1))
    query_low = grad_query_pre.astype(bf16)
    key_low = grad_key_pre.astype(bf16)
    value_low = own_value_grad.astype(bf16)
    query_part = matmul(act_a.T, query_low)
    key_part = matmul(act_a.T, key_low)
    value_part = matmul(act_a.T, value_low)
    grad_act_a = lax.psum(
        (
            matmul(query_low, query_w.T) + matmul(key_low, key_w.T) + matmul(value_low, value_w.T)
        ).astype(jnp.bfloat16),
        "head",
    ).astype(jnp.float32)
    grad_x_in, grad_gain_ai, grad_scale_a = pull_in_a(grad_act_a)
    input_grad = grad_x_tail + grad_x_in
    query_grad, key_grad, value_grad, out_grad, gate_grad, up_grad, down_grad = (
        lax.psum_scatter(
            query_part.astype(jnp.bfloat16), "seq", scatter_dimension=0, tiled=True
        ).astype(jnp.float32),
        lax.psum_scatter(
            key_part.astype(jnp.bfloat16), "seq", scatter_dimension=0, tiled=True
        ).astype(jnp.float32),
        lax.psum_scatter(
            value_part.astype(jnp.bfloat16), "seq", scatter_dimension=0, tiled=True
        ).astype(jnp.float32),
        lax.psum_scatter(
            out_part.astype(jnp.bfloat16), "seq", scatter_dimension=1, tiled=True
        ).astype(jnp.float32),
        lax.psum_scatter(
            gate_part.astype(jnp.bfloat16), "seq", scatter_dimension=0, tiled=True
        ).astype(jnp.float32),
        lax.psum_scatter(
            up_part.astype(jnp.bfloat16), "seq", scatter_dimension=0, tiled=True
        ).astype(jnp.float32),
        lax.psum_scatter(
            down_part.astype(jnp.bfloat16), "seq", scatter_dimension=1, tiled=True
        ).astype(jnp.float32),
    )
    mod_grad_part = jnp.concatenate([grad_scale_a, grad_gate_a, grad_scale_f, grad_gate_f])
    mod_grad = lax.psum_scatter(mod_grad_part, "seq", scatter_dimension=0, tiled=True)
    piece_width = ada_weight.shape[1]
    own_mod = lax.dynamic_slice_in_dim(mod_grad, head_index * piece_width, piece_width)
    ada_grad = cond_act.astype(f32)[:, None] * own_mod[None, :]
    gains_part = jnp.stack([grad_gain_ai, grad_gain_ao, grad_gain_fi, grad_gain_fo])
    text_total_key, text_total_value, norm_gains_grad, cross_gate_grad = (
        lax.psum(text_key_pre_grad.astype(jnp.bfloat16), "seq").astype(jnp.float32),
        lax.psum(text_value_part.reshape(text_count, -1).astype(jnp.bfloat16), "seq").astype(
            jnp.float32
        ),
        lax.psum(gains_part.astype(jnp.bfloat16), "seq").astype(jnp.float32),
        lax.psum(cross_gate_part.astype(jnp.bfloat16), "seq").astype(jnp.float32),
    )
    qk_gains_grad = lax.psum(
        jnp.stack([grad_query_gain, grad_key_gain + text_gain_grad]), ("seq", "head")
    )
    slab_width = text_rows.shape[1] // seq_count
    own_text = lax.dynamic_slice_in_dim(text_rows, seq_index * slab_width, slab_width, 1)
    text_key_grad = matmul(own_text.T, text_total_key.astype(bf16))
    text_value_grad = matmul(own_text.T, text_total_value.astype(bf16))
    return (
        hidden_out,
        input_grad,
        ada_grad,
        norm_gains_grad,
        qk_gains_grad,
        query_grad,
        key_grad,
        value_grad,
        out_grad,
        cross_gate_grad,
        text_key_grad,
        text_value_grad,
        gate_grad,
        up_grad,
        down_grad,
    )


def solution(mesh):
    in_specs = (
        P("seq", None),
        P(),
        P(),
        P(),
        P(None, ("seq", "head")),
        P(),
        P(),
        P("seq", "head"),
        P("seq", "head"),
        P("seq", "head"),
        P("head", "seq"),
        P("head"),
        P("seq", "head"),
        P("seq", "head"),
        P("seq", "head"),
        P("seq", "head"),
        P("head", "seq"),
        P("seq", None),
    )
    out_specs = (
        P("seq", None),
        P("seq", None),
        P(None, ("seq", "head")),
        P(),
        P(),
        P("seq", "head"),
        P("seq", "head"),
        P("seq", "head"),
        P("head", "seq"),
        P("head"),
        P("seq", "head"),
        P("seq", "head"),
        P("seq", "head"),
        P("seq", "head"),
        P("head", "seq"),
    )
    return jax.shard_map(
        per_device, mesh=mesh, in_specs=in_specs, out_specs=out_specs, check_vma=False
    )
```

profile of v0, /device:TPU:0, one launch (start us, length us, event | category | flops | bytes accessed | tf_op | source)
XLA Modules:
  0.0 1395.6 jit_solution(17392019799253216461)
XLA Ops:
  12.4 42.2 %all-reduce.4 = f32[6144]{0:T(1024)S(1)} all-reduce(f32[6144]{0:T(1024)S(1)} %dynamic-update-slice), channel_id=1, replica_groups=mesh['seq'=8,'head'=4] {'seq','head'}, use_global_device_ids=true, to_apply=%add.4 | all-reduce | flops 6144 | bytes 49152
  65.5 23.6 %all-gather.20.cloned.1.call-done = bf16[1536,384]{1,0:T(8,128)(2,1)} async-done(((bf16[192,384]{1,0:T(8,128)(2,1)}), bf16[1536,384]{1,0:T(8,128)(2,1)}) %all-gather.20.cloned.1.call-update) | async-done | bytes 1179664 | tf_op jit(solution)/shard_map/all_gather | solution.py:93
  92.4 30.8 %all-gather.24.cloned.1.call-done = bf16[4096,384]{1,0:T(8,128)(2,1)} async-done(((bf16[512,384]{1,0:T(8,128)(2,1)}), bf16[4096,384]{1,0:T(8,128)(2,1)}) %all-gather.24.cloned.1.call-update) | async-done | bytes 3145744 | tf_op jit(solution)/shard_map/all_gather | solution.py:100
  127.8 5.0 multiply_reduce_fusion.10
  138.2 6.2 fusion.149
  144.4 5.7 fusion.108
  150.2 7.1 all-gather.22.cloned.1.call-done
  157.3 5.7 convolution_convert_fusion.11
  163.0 28.9 %all-gather.14.cloned.1.call-done = bf16[4096,384]{1,0:T(8,128)(2,1)} async-done(((bf16[512,384]{1,0:T(8,128)(2,1)}), bf16[4096,384]{1,0:T(8,128)(2,1)}) %all-gather.14.cloned.1.call-update) | async-done | bytes 3145744 | tf_op jit(solution)/shard_map/all_gather | solution.py:130
  202.6 24.6 %all-gather.18.cloned.1.call-done = bf16[4096,384]{0,1:T(8,128)(2,1)} async-done(((bf16[512,384]{0,1:T(8,128)(2,1)}), bf16[4096,384]{0,1:T(8,128)(2,1)}) %all-gather.18.cloned.1.call-update) | async-done | bytes 3145744 | tf_op jit(solution)/shard_map/all_gather | solution.py:129
  233.3 75.8 %while.39 = (s32[]{:T(128)}, f32[6,512]{1,0:T(8,128)S(1)}, f32[6,512]{1,0:T(8,128)S(1)}, s32[512]{0:T(512)S(1)}, s32[8,512]{1,0:T(8,128)S(1)}, /*index=5*/bf16[8...) while((s32[]{:T(128)}, f32[6,512]{1,0:T(8,128)S(1)}, ...), condition=%wide.region_10.11_spmd.clone, body=%wide.region_7.10_spmd.clone.sunk | while | flops 214187008 | bytes 14324332 | solution.py:161
  243.0 4.9 fusion.240
  309.1 41.1 %while.40 = (s32[]{:T(128)}, f32[512,6,64]{0,2,1:T(8,128)S(1)}, bf16[8,512,6,64]{1,3,2,0:T(8,128)(2,1)}, s32[512]{0:T(512)S(1)}, s32[8,512]{1,0:T(8,128)S(1)}, /...) while((s32[]{:T(128)}, f32[512,6,64]{0,2,1:T(8,128)S(1)}, ...), condition=%wide.region_12.13_spmd.clone, body=%wide.region_11.12_spmd.clone.sunk | while | flops 411172864 | bytes 3298419 | solution.py:174
  360.0 67.3 %all-reduce.14.cloned.1.call-done = bf16[512,1536]{1,0:T(8,128)(2,1)} async-done(((bf16[512,1536]{1,0:T(8,128)(2,1)}), bf16[512,1536]{1,0:T(8,128)(2,1)}) %all-reduce.14.cloned.1.call-update) | async-done | bytes 1572880 | tf_op jit(solution)/shard_map/psum | solution.py:190
  436.4 24.0 %all-gather.28.cloned.1.call-done = bf16[1536,1024]{1,0:T(8,128)(2,1)} async-done(((bf16[192,1024]{1,0:T(8,128)(2,1)}), bf16[1536,1024]{1,0:T(8,128)(2,1)}) %all-gather.28.cloned.1.call-update) | async-done | bytes 3145744 | tf_op jit(solution)/shard_map/all_gather | solution.py:97
  460.4 5.5 fusion.151
  465.9 28.8 %all-gather.30.cloned.1.call-done = bf16[1536,1024]{1,0:T(8,128)(2,1)} async-done(((bf16[192,1024]{1,0:T(8,128)(2,1)}), bf16[1536,1024]{1,0:T(8,128)(2,1)}) %all-gather.30.cloned.1.call-update) | async-done | bytes 3145744 | tf_op jit(solution)/shard_map/all_gather | solution.py:98
  494.7 6.6 multiply_convert_fusion.3
  501.3 27.5 %all-gather.32.cloned.1.call-done = bf16[1024,1536]{0,1:T(8,128)(2,1)} async-done(((bf16[1024,192]{0,1:T(8,128)(2,1)}), bf16[1024,1536]{0,1:T(8,128)(2,1)}) %all-gather.32.cloned.1.call-update) | async-done | bytes 3145744 | tf_op jit(solution)/shard_map/all_gather | solution.py:99
  528.7 5.2 convolution_convert_fusion.3
  534.0 69.2 %all-reduce.16.cloned.1.call-done = bf16[512,1536]{1,0:T(8,128)(2,1)} async-done(((bf16[512,1536]{1,0:T(8,128)(2,1)}), bf16[512,1536]{1,0:T(8,128)(2,1)}) %all-reduce.16.cloned.1.call-update) | async-done | bytes 1572880 | tf_op jit(solution)/shard_map/psum | solution.py:198
  609.3 5.6 multiply_convert_fusion.2
  620.7 68.2 %all-reduce.18.cloned.1.call-done = bf16[512,1536]{1,0:T(8,128)(2,1)} async-done(((bf16[512,1536]{1,0:T(8,128)(2,1)}), bf16[512,1536]{1,0:T(8,128)(2,1)}) %all-reduce.18.cloned.1.call-update) | async-done | bytes 1572880 | tf_op jit(solution)/shard_map/psum | solution.py:212
  689.0 5.5 fusion.90
  695.2 6.4 fusion.83
  707.7 138.2 %while.41 = (s32[]{:T(128)}, f32[512,6,64]{0,2,1:T(8,128)}, bf16[8,512,6,64]{1,3,2,0:T(8,128)(2,1)}, bf16[8,512,6,64]{1,3,2,0:T(8,128)(2,1)}, bf16[8,512,6,64]{1...) while((s32[]{:T(128)}, f32[512,6,64]{0,2,1:T(8,128)}, ...), condition=%wide.region_27.28_spmd.clone, body=%wide.region_26.27_spmd.clone.sunk | while | flops 1027735552 | bytes 65600368 | solution.py:265
  719.4 5.3 fusion.261
  736.7 5.3 fusion.261
  754.0 5.3 fusion.261
  771.2 5.4 fusion.261
  788.5 5.3 fusion.261
  805.8 5.3 fusion.261
  823.1 5.3 fusion.261
  840.4 5.3 fusion.261
  864.7 5.3 convolution_convert_fusion
  889.5 8.7 reduce-scatter.10.cloned.1.call-done
  910.3 37.7 %reduce-scatter.12.cloned.1.call-done = bf16[512,384]{0,1:T(8,128)(2,1)} async-done(((bf16[4096,384]{0,1:T(8,128)(2,1)}), bf16[512,384]{0,1:T(8,128)(2,1)}) %reduce-scatter.12.cloned.1.call-update) | async-done | bytes 393232 | tf_op jit(solution)/shard_map/reduce_scatter | solution.py:277
  962.0 25.9 %reduce-scatter.20.cloned.1.call-done = bf16[384,192]{0,1:T(8,128)(2,1)} async-done(((bf16[384,1536]{0,1:T(8,128)(2,1)}), bf16[384,192]{0,1:T(8,128)(2,1)}) %reduce-scatter.20.cloned.1.call-update) | async-done | bytes 147472 | tf_op jit(solution)/shard_map/reduce_scatter | solution.py:312
  989.6 48.3 %reduce-scatter.26.cloned.1.call-done = bf16[1024,192]{0,1:T(8,128)(2,1)} async-done(((bf16[1024,1536]{0,1:T(8,128)(2,1)}), bf16[1024,192]{0,1:T(8,128)(2,1)}) %reduce-scatter.26.cloned.1.call-update) | async-done | bytes 393232 | tf_op jit(solution)/shard_map/reduce_scatter | solution.py:321
  1039.8 47.7 %reduce-scatter.22.cloned.1.call-done = bf16[192,1024]{1,0:T(8,128)(2,1)} async-done(((bf16[1536,1024]{1,0:T(8,128)(2,1)}), bf16[192,1024]{1,0:T(8,128)(2,1)}) %reduce-scatter.22.cloned.1.call-update) | async-done | bytes 393232 | tf_op jit(solution)/shard_map/reduce_scatter | solution.py:315
  1089.4 47.9 %reduce-scatter.24.cloned.1.call-done = bf16[192,1024]{1,0:T(8,128)(2,1)} async-done(((bf16[1536,1024]{1,0:T(8,128)(2,1)}), bf16[192,1024]{1,0:T(8,128)(2,1)}) %reduce-scatter.24.cloned.1.call-update) | async-done | bytes 393232 | tf_op jit(solution)/shard_map/reduce_scatter | solution.py:318
  1139.4 39.4 %psum.68 = f32[2,64]{1,0:T(2,128)} all-reduce(f32[2,64]{1,0:T(2,128)S(1)} %pad_maximum_fusion.4), channel_id=1, replica_groups=mesh['seq'=8,'head'=4] {'seq','head'}, use_global_device_ids=true, to_apply=%region_48.49 | all-reduce | flops 128 | bytes 1024 | tf_op jit(solution)/shard_map/psum | solution.py:339
  1181.0 15.9 %all-reduce.22.cloned.1.call-done = (bf16[512,384]{0,1:T(8,128)(2,1)}, bf16[512,384]{0,1:T(8,128)(2,1)}) async-done(((bf16[512,384]{0,1:T(8,128)(2,1)}, bf16[512,384]{0,1:T(8,128)(2,1)}), (bf16[512,384]{0,1:T(8,128)(2,1)}, bf16[512,384]{0,1:T(8,128)(2,1)})) %all-reduce.22.cloned.1.call-update) | async-done | bytes 786448 | tf_op jit(solution)/shard_map/psum | solution.py:332
  1202.0 65.6 %all-reduce.20.cloned.1.call-done = bf16[512,1536]{1,0:T(8,128)(2,1)} async-done(((bf16[512,1536]{1,0:T(8,128)(2,1)}), bf16[512,1536]{1,0:T(8,128)(2,1)}) %all-reduce.20.cloned.1.call-update) | async-done | bytes 1572880 | tf_op jit(solution)/shard_map/psum | solution.py:294
  1271.1 23.0 %all-reduce.6 = (bf16[4,1536]{1,0:T(4,128)(2,1)S(1)}, bf16[6]{0:T(256)(128)(2,1)S(1)}) all-reduce(bf16[4,1536]{1,0:T(4,128)(2,1)S(1)} %pad_maximum_fusion.3, bf16[6]{0:T(256)(128)(2,1)S(1)} %copy-done.114), channel_id=1, replica_groups=mesh['seq'=8,'head'=4] {'seq'}, use_global_device_ids=true, to_apply=%region_44.45 | all-reduce | flops 6150 | bytes 24600 | tf_op jit(solution)/shard_map/psum | solution.py:336
  1295.2 22.5 %all-reduce.5 = f32[6144]{0:T(1024)S(1)} all-reduce(f32[6144]{0:T(1024)S(1)} %pad_maximum_fusion.2), channel_id=4, replica_groups=mesh['seq'=8,'head'=4] {'seq'}, use_global_device_ids=true, to_apply=%region_39.40.clone | all-reduce | flops 6144 | bytes 49152
  1325.8 21.2 %reduce-scatter.16.cloned.1.call-done = bf16[192,384]{1,0:T(8,128)(2,1)} async-done(((bf16[1536,384]{1,0:T(8,128)(2,1)}), bf16[192,384]{1,0:T(8,128)(2,1)}) %reduce-scatter.16.cloned.1.call-update) | async-done | bytes 147472 | tf_op jit(solution)/shard_map/reduce_scatter | solution.py:306
  1348.6 38.4 %reduce-scatter.18.cloned.1.call-done = bf16[192,384]{1,0:T(8,128)(2,1)} async-done(((bf16[1536,384]{1,0:T(8,128)(2,1)}), bf16[192,384]{1,0:T(8,128)(2,1)}) %reduce-scatter.18.cloned.1.call-update) | async-done | bytes 147472 | tf_op jit(solution)/shard_map/reduce_scatter | solution.py:309
  (661 shorter events, 372.1 us)
Async XLA Ops:
  7.2 51.3 %copy-start.3 = (bf16[512,1536]{1,0:T(8,128)(2,1)S(1)}, bf16[512,1536]{1,0:T(8,128)(2,1)}, u32[]{:S(2)}) copy-start(bf16[512,1536]{1,0:T(8,128)(2,1)} %param.24) | copy-start | bytes 4718596
  7.2 51.3 %all-gather.12.cloned.1.call-start = ((), (), s32[]{:S(2)}) async-start(), calls=%async_computation.9 | async-start | bytes 1327104 | tf_op jit(solution)/shard_map/all_gather | solution.py:95
  7.9 55.2 %all-gather.16.cloned.1.call-start = ((), (), s32[]{:S(2)}) async-start(), calls=%async_computation.11 | async-start | bytes 1327104 | tf_op jit(solution)/shard_map/all_gather | solution.py:94
  8.7 80.4 %all-gather.20.cloned.1.call-start = ((), (), s32[]{:S(2)}) async-start(), calls=%async_computation.13 | async-start | bytes 1327104 | tf_op jit(solution)/shard_map/all_gather | solution.py:93
  9.4 113.8 %all-gather.24.cloned.1.call-start = ((), (), s32[]{:S(2)}) async-start(), calls=%async_computation.15 | async-start | bytes 3538944 | tf_op jit(solution)/shard_map/all_gather | solution.py:100
  10.0 147.3 %all-gather.22.cloned.1.call-start = ((), (), s32[]{:S(2)}) async-start(), calls=%async_computation.14 | async-start | bytes 3538944 | tf_op jit(solution)/shard_map/all_gather | solution.py:101
  10.6 181.3 %all-gather.14.cloned.1.call-start = ((), (), s32[]{:S(2)}) async-start(), calls=%async_computation.10 | async-start | bytes 3538944 | tf_op jit(solution)/shard_map/all_gather | solution.py:130
  61.7 165.6 %all-gather.18.cloned.1.call-start = ((), (), s32[]{:S(2)}) async-start(), calls=%async_computation.12 | async-start | bytes 3538944 | tf_op jit(solution)/shard_map/all_gather | solution.py:129
  62.1 70.8 %copy-start.104 = (f32[64]{0:T(128)}, f32[64]{0:T(128)S(1)}, u32[]{:S(2)}) copy-start(f32[64]{0:T(128)S(1)} %get-tuple-element.474) | copy-start | bytes 772
  65.4 67.6 %copy-start.12 = (f32[512,384]{0,1:T(8,128)}, f32[512,384]{0,1:T(8,128)S(1)}, u32[]{:S(2)}) copy-start(f32[512,384]{0,1:T(8,128)S(1)} %fusion.145) | copy-start | bytes 2359300
  135.8 218.6 %all-gather.26.cloned.1.call-start = ((), (), s32[]{:S(2)}) async-start(), calls=%async_computation.16 | async-start | bytes 1327104 | tf_op jit(solution)/shard_map/all_gather | solution.py:96
  136.5 290.8 %all-reduce.14.cloned.1.call-start = ((), (), s32[]{:S(2)}) async-start(), calls=%async_computation.17 | async-start | bytes 3145728 | tf_op jit(solution)/shard_map/psum | solution.py:190
  137.2 213.6 %copy-start.106 = (f32[6]{0:T(128)}, f32[6]{0:T(128)S(1)}, u32[]{:S(2)}) copy-start(f32[6]{0:T(128)S(1)} %tanh.10) | copy-start | bytes 76
  358.0 102.4 %all-gather.28.cloned.1.call-start = ((), (), s32[]{:S(2)}) async-start(), calls=%async_computation.18 | async-start | bytes 3538944 | tf_op jit(solution)/shard_map/all_gather | solution.py:97
  358.6 136.1 %all-gather.30.cloned.1.call-start = ((), (), s32[]{:S(2)}) async-start(), calls=%async_computation.19 | async-start | bytes 3538944 | tf_op jit(solution)/shard_map/all_gather | solution.py:98
  359.3 169.4 %all-gather.32.cloned.1.call-start = ((), (), s32[]{:S(2)}) async-start(), calls=%async_computation.20 | async-start | bytes 3538944 | tf_op jit(solution)/shard_map/all_gather | solution.py:99
  359.9 243.3 %all-reduce.16.cloned.1.call-start = ((), (), s32[]{:S(2)}) async-start(), calls=%async_computation.21 | async-start | bytes 3145728 | tf_op jit(solution)/shard_map/psum | solution.py:198
  534.0 155.0 %all-reduce.18.cloned.1.call-start = ((), (), s32[]{:S(2)}) async-start(), calls=%async_computation.22 | async-start | bytes 3145728 | tf_op jit(solution)/shard_map/psum | solution.py:212
  620.6 277.5 %reduce-scatter.10.cloned.1.call-start = ((), (), s32[]{:S(2)}) async-start(), calls=%async_computation.23 | async-start | bytes 3538944 | tf_op jit(solution)/shard_map/reduce_scatter | solution.py:271
  852.7 95.3 %reduce-scatter.12.cloned.1.call-start = ((), (), s32[]{:S(2)}) async-start(), calls=%async_computation.24 | async-start | bytes 3538944 | tf_op jit(solution)/shard_map/reduce_scatter | solution.py:277
  859.7 128.3 %reduce-scatter.20.cloned.1.call-start = ((), (), s32[]{:S(2)}) async-start(), calls=%async_computation.29 | async-start | bytes 1327104 | tf_op jit(solution)/shard_map/reduce_scatter | solution.py:312
  864.6 173.3 %reduce-scatter.26.cloned.1.call-start = ((), (), s32[]{:S(2)}) async-start(), calls=%async_computation.32 | async-start | bytes 3538944 | tf_op jit(solution)/shard_map/reduce_scatter | solution.py:321
  870.0 217.5 %reduce-scatter.22.cloned.1.call-start = ((), (), s32[]{:S(2)}) async-start(), calls=%async_computation.30 | async-start | bytes 3538944 | tf_op jit(solution)/shard_map/reduce_scatter | solution.py:315
  875.3 262.1 %reduce-scatter.24.cloned.1.call-start = ((), (), s32[]{:S(2)}) async-start(), calls=%async_computation.31 | async-start | bytes 3538944 | tf_op jit(solution)/shard_map/reduce_scatter | solution.py:318
  880.1 316.9 %all-reduce.22.cloned.1.call-start = ((), (), s32[]{:S(2)}) async-start(), calls=%async_computation.33 | async-start | bytes 1572864 | tf_op jit(solution)/shard_map/psum | solution.py:332
  905.2 362.5 %all-reduce.20.cloned.1.call-start = ((), (), s32[]{:S(2)}) async-start(), calls=%async_computation.25 | async-start | bytes 3145728 | tf_op jit(solution)/shard_map/psum | solution.py:294
  910.3 42.3 %copy-start.4 = (bf16[512,1536]{1,0:T(8,128)(2,1)S(1)}, bf16[512,1536]{1,0:T(8,128)(2,1)}, u32[]{:S(2)}) copy-start(bf16[512,1536]{1,0:T(8,128)(2,1)} %param.24) | copy-start | bytes 4718596
  910.3 42.3 %copy-start.69 = (f32[1536]{0:T(1024)S(1)}, f32[1536]{0:T(1024)}, u32[]{:S(2)}) copy-start(f32[1536]{0:T(1024)} %copy-done.68) | copy-start | bytes 18436
  910.3 42.3 %copy-start.71 = (f32[1536]{0:T(1024)S(1)}, f32[1536]{0:T(1024)}, u32[]{:S(2)}) copy-start(f32[1536]{0:T(1024)} %copy-done.70) | copy-start | bytes 18436
  910.3 42.4 %copy-start.84 = (f32[512]{0:T(512)S(1)}, f32[512]{0:T(512)}, u32[]{:S(2)}) copy-start(f32[512]{0:T(512)} %copy-done.83) | copy-start | bytes 6148
  952.6 371.5 %reduce-scatter.14.cloned.1.call-start = ((), (), s32[]{:S(2)}) async-start(), calls=%async_computation.26 | async-start | bytes 1327104 | tf_op jit(solution)/shard_map/reduce_scatter | solution.py:303
  955.1 391.9 %reduce-scatter.16.cloned.1.call-start = ((), (), s32[]{:S(2)}) async-start(), calls=%async_computation.27 | async-start | bytes 1327104 | tf_op jit(solution)/shard_map/reduce_scatter | solution.py:306
  957.6 181.8 %copy-start.112 = (f32[64]{0:T(128)S(1)}, f32[64]{0:T(128)}, u32[]{:S(2)}) copy-start(f32[64]{0:T(128)} %get-tuple-element.372) | copy-start | bytes 772
  957.6 181.8 %copy-start.113 = (f32[64]{0:T(128)S(1)}, f32[64]{0:T(128)}, u32[]{:S(2)}) copy-start(f32[64]{0:T(128)} %get-tuple-element.380) | copy-start | bytes 772
  957.6 181.8 %copy-start.108 = (f32[64]{0:T(128)S(1)}, f32[64]{0:T(128)}, u32[]{:S(2)}) copy-start(f32[64]{0:T(128)} %get-tuple-element.370) | copy-start | bytes 772
  957.6 221.2 %copy-start.43 = (bf16[512,384]{0,1:T(8,128)(2,1)S(1)}, bf16[512,384]{0,1:T(8,128)(2,1)}, u32[]{:S(2)}) copy-start(bf16[512,384]{0,1:T(8,128)(2,1)} %reduce-scatter.12.cloned.1.call-done) | copy-start | bytes 1179652
  957.6 429.4 %reduce-scatter.18.cloned.1.call-start = ((), (), s32[]{:S(2)}) async-start(), calls=%async_computation.28 | async-start | bytes 1327104 | tf_op jit(solution)/shard_map/reduce_scatter | solution.py:309
  1181.0 86.7 %copy-start.85 = (f32[512]{0:T(512)S(1)}, f32[512]{0:T(512)}, u32[]{:S(2)}) copy-start(f32[512]{0:T(512)} %copy-done.83) | copy-start | bytes 6148
  1196.9 74.1 %copy-start.80 = (bf16[1,1536]{1,0:T(2,128)(2,1)S(1)}, bf16[1,1536]{1,0:T(2,128)(2,1)}, u32[]{:S(2)}) copy-start(bf16[1,1536]{1,0:T(2,128)(2,1)} %reshape.492) | copy-start | bytes 9220
  1196.9 74.1 %copy-start.81 = (bf16[1,1536]{1,0:T(2,128)(2,1)S(1)}, bf16[1,1536]{1,0:T(2,128)(2,1)}, u32[]{:S(2)}) copy-start(bf16[1,1536]{1,0:T(2,128)(2,1)} %reshape.490) | copy-start | bytes 9220
  1196.9 74.1 %copy-start.82 = (bf16[1,1536]{1,0:T(2,128)(2,1)S(1)}, bf16[1,1536]{1,0:T(2,128)(2,1)}, u32[]{:S(2)}) copy-start(bf16[1,1536]{1,0:T(2,128)(2,1)} %reshape.491) | copy-start | bytes 9220
  1196.9 74.2 %copy-start.114 = (bf16[6]{0:T(256)(128)(2,1)S(1)}, bf16[6]{0:T(256)(128)(2,1)}, u32[]{:S(2)}) copy-start(bf16[6]{0:T(256)(128)(2,1)} %multiply_convert_fusion.7) | copy-start | bytes 40
  1196.9 98.3 %copy-start.75 = (f32[1536]{0:T(1024)S(1)}, f32[1536]{0:T(1024)}, u32[]{:S(2)}) copy-start(f32[1536]{0:T(1024)} %get-tuple-element.358) | copy-start | bytes 18436
  1196.9 98.3 %copy-start.78 = (f32[1536]{0:T(1024)S(1)}, f32[1536]{0:T(1024)}, u32[]{:S(2)}) copy-start(f32[1536]{0:T(1024)} %get-tuple-element.465) | copy-start | bytes 18436
  1196.9 98.3 %copy-start.79 = (f32[1536]{0:T(1024)S(1)}, f32[1536]{0:T(1024)}, u32[]{:S(2)}) copy-start(f32[1536]{0:T(1024)} %get-tuple-element.466) | copy-start | bytes 18436
  1196.9 120.8 %copy-start.88 = (f32[512]{0:T(512)S(1)}, f32[512]{0:T(512)}, u32[]{:S(2)}) copy-start(f32[512]{0:T(512)} %copy-done.87) | copy-start | bytes 6148
  1267.7 51.8 %copy-start.24 = (bf16[512,1536]{1,0:T(8,128)(2,1)S(1)}, bf16[512,1536]{1,0:T(8,128)(2,1)}, u32[]{:S(2)}) copy-start(bf16[512,1536]{1,0:T(8,128)(2,1)} %all-reduce.20.cloned.1.call-done) | copy-start | bytes 4718596
  1317.8 70.9 %copy-start.1 = (bf16[1024,192]{0,1:T(8,128)(2,1)S(1)}, bf16[1024,192]{0,1:T(8,128)(2,1)}, u32[]{:S(2)}) copy-start(bf16[1024,192]{0,1:T(8,128)(2,1)} %param.28) | copy-start | bytes 1179652
  (158 other events, 834.0 us)
Sparse Core Ops, SparseCore 0:
  9.9 26.9 all-gather.11
  38.8 24.2 all-gather.15
  65.0 24.0 all-gather.19
  90.8 32.3 all-gather.23
  124.9 32.3 all-gather.21
  159.6 32.3 all-gather.13
  194.4 32.8 all-gather.17
  229.1 24.0 all-gather.25
  358.1 69.1 all-reduce.13
  429.0 31.3 all-gather.27
  462.3 32.3 all-gather.29
  496.4 32.3 all-gather.31
  534.1 69.1 all-reduce.15
  620.8 68.1 all-reduce.17
  852.8 45.2 reduce-scatter.9
  901.8 46.2 reduce-scatter.11
  951.1 36.7 reduce-scatter.19
  991.5 46.2 reduce-scatter.25
  1041.2 46.2 reduce-scatter.21
  1091.1 46.2 reduce-scatter.23
  1141.1 55.7 all-reduce.21
  1199.3 68.3 all-reduce.19
  1270.9 35.8 reduce-scatter.13
  1310.2 36.7 reduce-scatter.15
  1350.2 36.7 reduce-scatter.17
where the time goes:
time: 1410 us; the launch traced here: 1400 us
  waiting for transfers between devices  763 us (54%)
  matrix products  304 us (22%)
  blocking collectives  127 us (9%)
  other arithmetic  113 us (8%)
  local copies, waits for them, and re-layouts  57.9 us (4%)
  between operations  16.6 us (1%)
    dot_general x26, matrix products, matmul(): return jnp.dot(left, right, preferred_element_type=jnp.float32)  88.4 us
    psum x1, waiting for transfers between devices, per_device(): lax.psum(matmul(hidden_units, down_w).astype(jnp.bfloat16), 'head')  69.2 us
    psum x1, waiting for transfers between devices, per_device(): lax.psum((matmul(grad_gate_low, gate_w.T) + matmul(grad_up_low, up_w.T))....  68.2 us
    psum x1, waiting for transfers between devices, per_device(): lax.psum(matmul(mixed, out_w).astype(jnp.bfloat16), 'head')  67.3 us
    psum x1, waiting for transfers between devices, per_device(): lax.psum((matmul(query_low, query_w.T) + matmul(key_low, key_w.T) + matmu...  65.6 us
    unnamed x2, blocking collectives  64.6 us
    reduce_scatter x1, waiting for transfers between devices, per_device(): lax.psum_scatter(down_part.astype(jnp.bfloat16), 'seq', scatter_dimension...  48.3 us
    reduce_scatter x1, waiting for transfers between devices, per_device(): lax.psum_scatter(up_part.astype(jnp.bfloat16), 'seq', scatter_dimension=0...  47.9 us
  transfers between devices with their start and end apart: 25, of which 21 were waited for; matrix products, arithmetic and copies ran while one was open for 20% of the time, Pallas kernels for 0%

commit v1 on v0

v1 whole, which is shorter than its diff:
```python
import functools
import jax
import jax.numpy as jnp
from jax import lax
from jax.experimental import pallas as pl
from jax.experimental.pallas import tpu as pltpu
from jax.sharding import PartitionSpec as P

HD = 64
MASK = 8192.0


def dot(a, b):
    return lax.dot_general(a, b, (((1,), (0,)), ((), ())), preferred_element_type=jnp.float32)


def split3(v):
    hi = v.astype(jnp.bfloat16).astype(jnp.float32)
    mid = (v - hi).astype(jnp.bfloat16).astype(jnp.float32)
    return hi, mid, v - hi - mid


def bounds(info, base, clips, ids):
    start = jnp.full(ids.shape, 1 << 30, jnp.int32)
    end = jnp.zeros(ids.shape, jnp.int32)
    for c in range(clips):
        start = jnp.where(ids == c, info[base + c], start)
        end = jnp.where(ids == c, info[base + clips + c], end)
    return start, end


def query_ext(info, clips, width, scale):
    ids = lax.broadcasted_iota(jnp.int32, (16, width), 0)
    place = info[0] + lax.broadcasted_iota(jnp.int32, (16, width), 1)
    start, end = bounds(info, 1, clips, ids)
    return jnp.where((place >= start) & (place < end), scale, 0.0)


def key_ext(info, clips, first, rows):
    ids = lax.broadcasted_iota(jnp.int32, (rows, 128), 1)
    place = first + lax.broadcasted_iota(jnp.int32, (rows, 128), 0)
    start, end = bounds(info, 1 + 2 * clips, clips, ids)
    inside = (place >= start) & (place < end)
    value = jnp.where(ids < clips, jnp.where(inside, 0.0, -1.0), jnp.where(ids < clips + 3, 1.0, 0.0))
    return value.astype(jnp.bfloat16)


def fill_ext(dst, h, src, tail):
    width = src.shape[1]
    half = h % 2
    zero = jnp.zeros((HD, width), jnp.bfloat16)
    dst[h, half * HD : half * HD + HD, :] = src[h * HD : h * HD + HD, :]
    dst[h, (1 - half) * HD : (1 - half) * HD + HD, :] = zero
    dst[h, 128:144, :] = tail.astype(jnp.bfloat16)
    dst[h, 144:256, :] = jnp.zeros((112, width), jnp.bfloat16)


def stack_rows(heads, rows, clips, width):
    ids = lax.broadcasted_iota(jnp.int32, (16, width), 0)
    total = jnp.zeros((16, width), jnp.float32)
    for k, row in enumerate(rows):
        total = jnp.where(ids == clips + k, jnp.broadcast_to(row, (16, width)), total)
    return total


def load_pieces(pieces, kv, sem):
    rows = pieces[0].shape[0]
    return [
        pltpu.make_async_copy(piece, kv.at[pl.ds(k * rows, rows), :], sem.at[k])
        for k, piece in enumerate(pieces)
    ]


def fwd_kernel(heads, clips, count, tile, info, qt, *rest):
    pieces, (out, qx, kv, sem) = rest[:count], rest[count:]
    copies = load_pieces(pieces, kv, sem)
    for c in copies:
        c.start()
    width = qt.shape[1]
    wide = qt.shape[0]
    ext = query_ext(info, clips, width, MASK)
    for h in range(heads):
        fill_ext(qx, h, qt, ext)
        out[h] = jnp.zeros((80, width), jnp.float32)
    for c in copies:
        c.wait()
    per = pieces[0].shape[0] // tile
    ones = jnp.ones((16, tile), jnp.bfloat16)

    def step(t, carry):
        rows = pl.ds(pl.multiple_of(t * tile, tile), tile)
        first = info[1 + 4 * clips + t // per] + lax.rem(t, per) * tile
        extra = key_ext(info, clips, first, tile)
        for p in range((heads + 1) // 2):
            kx = jnp.concatenate([kv[rows, p * 128 : p * 128 + 128], extra], axis=1)
            vt = kv[rows, wide + p * 128 : wide + p * 128 + 128].T
            for h in range(2 * p, min(2 * p + 2, heads)):
                half = h % 2
                probs = jnp.exp(dot(kx, qx[h])).astype(jnp.bfloat16)
                vx = jnp.concatenate([vt[half * HD : half * HD + HD, :], ones], axis=0)
                out[h] += dot(vx, probs)
        return carry

    lax.fori_loop(0, per * count, step, 0)


def attend(info, qt, pieces, heads, clips, tile=512):
    count = len(pieces)
    wide, width = qt.shape
    rows = pieces[0].shape[0]
    tile = min(tile, rows)
    return pl.pallas_call(
        functools.partial(fwd_kernel, heads, clips, count, tile),
        out_shape=jax.ShapeDtypeStruct((heads, 80, width), jnp.float32),
        in_specs=[pl.BlockSpec(memory_space=pltpu.SMEM), pl.BlockSpec(memory_space=pltpu.VMEM)]
        + [pl.BlockSpec(memory_space=pl.ANY)] * count,
        out_specs=pl.BlockSpec(memory_space=pltpu.VMEM),
        scratch_shapes=[
            pltpu.VMEM((heads, 256, width), jnp.bfloat16),
            pltpu.VMEM((count * rows, 2 * wide), jnp.bfloat16),
            pltpu.SemaphoreType.DMA((count,)),
        ],
        compiler_params=pltpu.CompilerParams(vmem_limit_bytes=48 << 20),
        cost_estimate=pl.CostEstimate(
            flops=4 * heads * width * rows * count * 256,
            bytes_accessed=count * rows * wide * 4 + 4 * heads * 80 * width,
            transcendentals=heads * width * rows * count,
        ),
        name="attend",
    )(info, qt, *pieces)


def bwd_kernel(heads, clips, count, tile, info, qt, dot_t, q_tok, do_tok, lse, delta, *rest):
    pieces, rest = rest[:count], rest[count:]
    dqt, grads, (qx, dox, qpad, dopad, kv, sem) = rest[0], rest[1:-6], rest[-6:]
    copies = load_pieces(pieces, kv, sem)
    for c in copies:
        c.start()
    wide, width = qt.shape
    ext = query_ext(info, clips, width, MASK)
    for h in range(heads):
        p, half = h // 2, h % 2
        fill_ext(qx, h, qt, ext - stack_rows(heads, split3(lse[h : h + 1, :]), clips, width))
        fill_ext(dox, h, dot_t, -stack_rows(heads, split3(delta[h : h + 1, :]), clips, width))
        lane = lax.broadcasted_iota(jnp.int32, (width, 128), 1) // HD
        zero = jnp.zeros((width, 128), jnp.bfloat16)
        qpad[h] = jnp.where(lane == half, q_tok[:, p * 128 : p * 128 + 128], zero)
        dopad[h] = jnp.where(lane == half, do_tok[:, p * 128 : p * 128 + 128], zero)
    dqt[...] = jnp.zeros((wide, width), jnp.float32)
    for c in copies:
        c.wait()
    per = pieces[0].shape[0] // tile

    def step(t, carry):
        rows = pl.ds(pl.multiple_of(t * tile, tile), tile)
        first = info[1 + 4 * clips + t // per] + lax.rem(t, per) * tile
        extra = key_ext(info, clips, first, tile)
        for p in range((heads + 1) // 2):
            cols = slice(p * 128, p * 128 + 128)
            vcols = slice(wide + p * 128, wide + p * 128 + 128)
            k_tile = kv[rows, cols]
            kx = jnp.concatenate([k_tile, extra], axis=1)
            vx = jnp.concatenate([kv[rows, vcols], extra], axis=1)
            kt = k_tile.T
            dk = jnp.zeros((tile, 128), jnp.float32)
            dv = jnp.zeros((tile, 128), jnp.float32)
            for h in range(2 * p, min(2 * p + 2, heads)):
                half = h % 2
                probs = jnp.exp(dot(kx, qx[h]))
                ds = (probs * dot(vx, dox[h])).astype(jnp.bfloat16)
                dqt[h * HD : h * HD + HD, :] += dot(kt[half * HD : half * HD + HD, :], ds)
                dk = dk + dot(ds, qpad[h])
                dv = dv + dot(probs.astype(jnp.bfloat16), dopad[h])
            for g, grad in enumerate(grads):

                @pl.when(t // (per * count // len(grads)) == g)
                def store(g=g, grad=grad, dk=dk, dv=dv, cols=cols, vcols=vcols):
                    start = (t - g * (per * count // len(grads))) * tile
                    here = pl.ds(pl.multiple_of(start, tile), tile)
                    grad[here, cols] = dk.astype(grad.dtype)
                    grad[here, vcols] = dv.astype(grad.dtype)

        return carry

    lax.fori_loop(0, per * count, step, 0)


def attend_back(info, qt, dot_t, q_tok, do_tok, lse, delta, pieces, heads, clips, kind, parts=1, tile=512):
    count = len(pieces)
    wide, width = qt.shape
    rows = pieces[0].shape[0]
    tile = min(tile, rows)
    return pl.pallas_call(
        functools.partial(bwd_kernel, heads, clips, count, tile),
        out_shape=(
            jax.ShapeDtypeStruct((wide, width), jnp.float32),
        )
        + (jax.ShapeDtypeStruct((count * rows // parts, 2 * wide), kind),) * parts,
        in_specs=[pl.BlockSpec(memory_space=pltpu.SMEM)]
        + [pl.BlockSpec(memory_space=pltpu.VMEM)] * 6
        + [pl.BlockSpec(memory_space=pl.ANY)] * count,
        out_specs=(pl.BlockSpec(memory_space=pltpu.VMEM),) * (1 + parts),
        scratch_shapes=[
            pltpu.VMEM((heads, 256, width), jnp.bfloat16),
            pltpu.VMEM((heads, 256, width), jnp.bfloat16),
            pltpu.VMEM((heads, width, 128), jnp.bfloat16),
            pltpu.VMEM((heads, width, 128), jnp.bfloat16),
            pltpu.VMEM((count * rows, 2 * wide), jnp.bfloat16),
            pltpu.SemaphoreType.DMA((count,)),
        ],
        compiler_params=pltpu.CompilerParams(vmem_limit_bytes=56 << 20),
        cost_estimate=pl.CostEstimate(
            flops=10 * heads * width * rows * count * 256,
            bytes_accessed=count * rows * wide * 8 + 4 * wide * width,
            transcendentals=heads * width * rows * count,
        ),
        name="attend_back",
    )(info, qt, dot_t, q_tok, do_tok, lse, delta, *pieces)


ROWS = (((1,), (1,)), ((), ()))
COLS = (((0,), (0,)), ((), ()))
f32 = jnp.float32
bf16 = jnp.bfloat16


def matmul(left, right, dims=None):
    if dims is None:
        return jnp.dot(left, right, preferred_element_type=f32)
    return lax.dot_general(left, right, dims, preferred_element_type=f32)


def first_way(i):
    return i ^ 2 if i % 2 == 0 else i ^ 4


def other_way(i):
    return i ^ 4 if i % 2 == 0 else i ^ 2


def swap(value, axis, count, to):
    return lax.ppermute(value, axis, [(i, to(i)) for i in range(count)])


def seq_roles(seq_index, seq_count):
    if seq_count != 8:
        return jnp.arange(seq_count, dtype=jnp.int32)
    peer = seq_index ^ 1

    def roles(i):
        even = i % 2 == 0
        return [i, jnp.where(even, i ^ 2, i ^ 4), jnp.where(even, i ^ 4, i ^ 2), i ^ 6]

    return jnp.stack(roles(seq_index) + roles(peer)).astype(jnp.int32)


def gather_pieces(block, seq_count):
    if seq_count != 8:
        whole = lax.all_gather(block, "seq", axis=0, tiled=False)
        return [whole[i] for i in range(seq_count)]
    near = swap(block, "seq", 8, first_way)
    next_ = swap(block, "seq", 8, other_way)
    far = swap(near, "seq", 8, other_way)
    mine = [block, near, next_, far]
    return mine + [swap(v, "seq", 8, lambda i: i ^ 1) for v in mine]


def place_kernel(count, rows, roles, *rest):
    pieces, out, sem = rest[:count], rest[count], rest[count + 1]
    copies = []
    for k in range(count):
        start = pl.multiple_of(roles[k] * rows, rows)
        copies.append(pltpu.make_async_copy(pieces[k], out.at[pl.ds(start, rows), :], sem.at[k]))
    for c in copies:
        c.start()
    for c in copies:
        c.wait()


def place(pieces, roles):
    count = len(pieces)
    rows, width = pieces[0].shape
    return pl.pallas_call(
        functools.partial(place_kernel, count, rows),
        out_shape=jax.ShapeDtypeStruct((count * rows, width), pieces[0].dtype),
        in_specs=[pl.BlockSpec(memory_space=pltpu.SMEM)]
        + [pl.BlockSpec(memory_space=pl.ANY)] * count,
        out_specs=pl.BlockSpec(memory_space=pltpu.VMEM),
        scratch_shapes=[pltpu.SemaphoreType.DMA((count,))],
        compiler_params=pltpu.CompilerParams(vmem_limit_bytes=32 << 20),
        cost_estimate=pl.CostEstimate(flops=0, bytes_accessed=4 * count * rows * width, transcendentals=0),
        name="place",
    )(roles, *pieces)


def scatter_sum(part, seq_index, seq_count):
    if seq_count != 8:
        return lax.psum_scatter(part, "seq", scatter_dimension=0, tiled=True).astype(f32)
    rows = part.shape[0] // 8
    blocks = part.reshape(4, 2, rows, part.shape[1])
    core, chip = seq_index % 2, seq_index // 2
    theirs = lax.dynamic_index_in_dim(blocks, 1 - core, 1, False)
    got = swap(theirs, "seq", 8, lambda i: i ^ 1)
    mine = (lax.dynamic_index_in_dim(blocks, core, 1, False).astype(f32) + got.astype(f32)).astype(bf16)
    pick = lambda c: lax.dynamic_index_in_dim(mine, c, 0, False)
    near = jnp.where(core == 0, chip ^ 1, chip ^ 2)
    next_ = jnp.where(core == 0, chip ^ 2, chip ^ 1)
    first = swap(jnp.stack([pick(chip ^ 3), pick(next_)]), "seq", 8, other_way)
    second = (pick(near).astype(f32) + first[0].astype(f32)).astype(bf16)
    second = swap(second, "seq", 8, first_way)
    return pick(chip).astype(f32) + first[1].astype(f32) + second.astype(f32)


def sum_all(value, axes):
    for axis, count in axes:
        if count & (count - 1):
            value = lax.psum(value, axis)
            continue
        bit = 1
        while bit < count:
            value = value + swap(value, axis, count, lambda i, bit=bit: i ^ bit)
            bit *= 2
    return value


def head_sum(chunks, head_index, head_count):
    if head_count != 4:
        return [lax.psum(c, "head") for c in chunks]
    end = (head_index == 0) | (head_index == 3)
    inner, middle, totals = [], [], []
    for k, chunk in enumerate(chunks):
        if k >= 2:
            chunk, _ = lax.optimization_barrier((chunk, middle[k - 2]))
        got = lax.ppermute(chunk, "head", [(0, 1), (3, 2)])
        middle.append((chunk.astype(f32) + got.astype(f32)).astype(bf16))
    for k, part in enumerate(middle):
        got = lax.ppermute(part, "head", [(1, 2), (2, 1)])
        total = (part.astype(f32) + got.astype(f32)).astype(bf16)
        back = lax.ppermute(total, "head", [(1, 0), (2, 3)])
        totals.append(jnp.where(end, back, total))
    return totals


def head_sum_rows(value, head_index, head_count, parts=4):
    rows = value.shape[0] // parts
    value = value.astype(bf16)
    chunks = [value[k * rows : (k + 1) * rows] for k in range(parts)]
    return jnp.concatenate(head_sum(chunks, head_index, head_count), axis=0)


def head_mean(value):
    row = lax.broadcasted_iota(jnp.int32, (128, 128), 0) // HD
    col = lax.broadcasted_iota(jnp.int32, (128, 128), 1) // HD
    ones = jnp.where(row == col, 1.0 / HD, 0.0).astype(bf16)
    hi, mid, lo = split3(value)
    return dot(hi.astype(bf16), ones) + dot(mid.astype(bf16), ones) + dot(lo.astype(bf16), ones)


def partner(value):
    lane = lax.broadcasted_iota(jnp.int32, value.shape, 1) % HD
    return jnp.where(lane < HD // 2, pltpu.roll(value, 128 - HD // 2, 1), pltpu.roll(value, HD // 2, 1))


def norm_kernel(pre, gain, cos, sin, out):
    for p in range(pre.shape[1] // 128):
        cols = slice(p * 128, p * 128 + 128)
        value = pre[:, cols]
        value = value * lax.rsqrt(head_mean(value * value) + 1e-6) * gain[...]
        out[:, cols] = (value * cos[...] + partner(value) * sin[...]).astype(out.dtype)


def norm_rope(pre, gain, cos, sin):
    return pl.pallas_call(
        norm_kernel,
        out_shape=jax.ShapeDtypeStruct(pre.shape, bf16),
        name="norm_rope",
        compiler_params=pltpu.CompilerParams(vmem_limit_bytes=32 << 20),
    )(pre, gain, cos, sin)


def norm_back_kernel(pre, gain, cos, sin, grad, out, gain_grad):
    total = jnp.zeros((1, 128), f32)
    for p in range(pre.shape[1] // 128):
        cols = slice(p * 128, p * 128 + 128)
        value = pre[:, cols]
        scale = lax.rsqrt(head_mean(value * value) + 1e-6)
        normed = value * scale
        g = grad[:, cols]
        g = g * cos[...] - partner(g) * sin[...]
        total = total + jnp.sum(g * normed, axis=0, keepdims=True)
        g = g * gain[...]
        out[:, cols] = (scale * (g - normed * head_mean(g * normed))).astype(out.dtype)
    gain_grad[...] = total


def norm_rope_back(pre, gain, cos, sin, grad, kind):
    return pl.pallas_call(
        norm_back_kernel,
        out_shape=(jax.ShapeDtypeStruct(pre.shape, kind), jax.ShapeDtypeStruct((1, 128), f32)),
        name="norm_rope_back",
        compiler_params=pltpu.CompilerParams(vmem_limit_bytes=32 << 20),
    )(pre, gain, cos, sin, grad)


def mean_norm(value):
    return value * lax.rsqrt(jnp.mean(value * value, axis=-1, keepdims=True) + 1e-06)


def attn_input(x_value, gain_value, scale_value):
    return mean_norm(x_value) * gain_value * (1.0 + scale_value)


def branch_tail(x_value, branch, gain_value, gate_value):
    return x_value + jnp.tanh(gate_value) * mean_norm(branch) * gain_value


def swiglu_units(gate_pre, up_pre):
    return jax.nn.silu(gate_pre) * up_pre


def per_device(
    seq_count,
    head_count,
    hidden_in,
    cond,
    captions,
    clip_lengths,
    ada_weight,
    norm_gains,
    qk_gains,
    w_query,
    w_key,
    w_value,
    w_out,
    cross_gate,
    w_text_key,
    w_text_value,
    w_gate,
    w_up,
    w_down,
    out_cotangent,
):
    local_rows, model_width = hidden_in.shape
    seq_index = lax.axis_index("seq")
    head_index = lax.axis_index("head")
    clips = clip_lengths.shape[0]
    cols = w_query.shape[1]
    heads = cols // HD
    wide = (cols + 127) // 128 * 128
    units = w_gate.shape[1]
    roles = seq_roles(seq_index, seq_count)
    pad = lambda v: jnp.pad(v, ((0, 0), (0, wide - cols))) if wide > cols else v
    cut = lambda v: v[:, :cols]

    cond_act = jax.nn.silu(cond).astype(bf16)
    piece_width = ada_weight.shape[1]
    mod_piece = matmul(cond_act[None, :], ada_weight)
    mine = lax.broadcasted_iota(jnp.int32, (seq_count * head_count, 1), 0) == seq_index * head_count + head_index
    modulation = sum_all(
        jnp.where(mine, mod_piece, 0.0), (("seq", seq_count), ("head", head_count))
    ).reshape(-1)
    scale_a, gate_a, scale_f, gate_f = jnp.split(modulation, 4)

    w_qkv = place(
        gather_pieces(jnp.concatenate([pad(w_query), pad(w_key), pad(w_value)], axis=1), seq_count), roles
    )
    text_rows = captions.reshape(-1, captions.shape[2])
    text_count = text_rows.shape[0]
    slab_width = text_rows.shape[1] // seq_count
    own_text = lax.dynamic_slice_in_dim(text_rows, seq_index * slab_width, slab_width, 1)
    w_text = jnp.concatenate([pad(w_text_key), pad(w_text_value)], axis=1)
    text_pre = lax.psum(matmul(own_text, w_text).astype(bf16), "seq")
    gate_w = lax.all_gather(w_gate, "seq", axis=0, tiled=True)
    up_w = lax.all_gather(w_up, "seq", axis=0, tiled=True)
    down_t = lax.all_gather(w_down.T, "seq", axis=0, tiled=True)

    clip_ends = jnp.cumsum(clip_lengths, dtype=jnp.int32)
    starts = clip_ends - clip_lengths
    text_ids = jnp.arange(clips, dtype=jnp.int32) * captions.shape[1]
    first_row = seq_index * local_rows
    place_info = jnp.concatenate([first_row[None], starts, clip_ends]).astype(jnp.int32)
    text_info = jnp.concatenate(
        [place_info, text_ids, text_ids + captions.shape[1], jnp.zeros((1,), jnp.int32)]
    )

    def self_info(which):
        return jnp.concatenate([place_info, starts, clip_ends, roles[which] * local_rows])

    places = first_row + jnp.arange(local_rows, dtype=jnp.int32)
    inside = (places[:, None] >= starts[None, :]) & (places[:, None] < clip_ends[None, :])
    position = places - jnp.sum(jnp.where(inside, starts[None, :], 0), axis=1, dtype=jnp.int32)
    lane = jnp.arange(128)
    frequency = 10000.0 ** (-(lane % (HD // 2)).astype(f32) / (HD // 2))
    angles = position.astype(f32)[:, None] * frequency[None, :]
    cos = jnp.cos(angles)
    sin = jnp.where(lane % HD < HD // 2, -1.0, 1.0)[None, :] * jnp.sin(angles)
    flat = (jnp.ones((text_count, 128), f32), jnp.zeros((text_count, 128), f32))
    query_gain = jnp.tile(qk_gains[0], 2)[None, :]
    key_gain = jnp.tile(qk_gains[1], 2)[None, :]

    x_float = hidden_in.astype(f32)
    normed_a, pull_in_a = jax.vjp(attn_input, x_float, norm_gains[0], scale_a)
    act_a = normed_a.astype(bf16)
    pre = matmul(act_a, w_qkv)
    query_pre, key_pre, value_pre = pre[:, :wide], pre[:, wide : 2 * wide], pre[:, 2 * wide :]
    queries = norm_rope(query_pre, query_gain, cos, sin) * jnp.asarray(HD**-0.5, bf16)
    keys = norm_rope(key_pre, key_gain, cos, sin)
    query_t = queries.T
    pieces = gather_pieces(jnp.concatenate([keys, value_pre.astype(bf16)], axis=1), seq_count)
    out_in, _ = lax.optimization_barrier((w_out.T, pieces[-1]))
    out_t = place(gather_pieces(out_in, seq_count), roles)
    text_key_pre = text_pre[:, :wide].astype(f32)
    text_keys = norm_rope(text_key_pre, key_gain, *flat)
    text_piece = jnp.concatenate([text_keys, text_pre[:, wide:]], axis=1)
    if seq_count == 8:
        groups = ((0, 4), (1, 2, 5, 6), (3, 7))
    else:
        groups = (tuple(range(seq_count)),)
    sums = 0.0
    for group in groups:
        sums = sums + attend(
            self_info(jnp.array(group)), query_t, [pieces[g] for g in group], heads, clips
        )
    cross_sums = attend(text_info, query_t, [text_piece], heads, clips)
    self_den, cross_den = sums[:, HD], cross_sums[:, HD]
    self_lse, cross_lse = jnp.log(self_den), jnp.log(cross_den)
    self_out = sums[:, :HD] / self_den[:, None]
    cross_out = cross_sums[:, :HD] / cross_den[:, None]
    gate_local = jnp.tanh(cross_gate)[:, None, None]
    mixed = (self_out + gate_local * cross_out).astype(bf16).reshape(cols, local_rows)
    attn_part = matmul(mixed, cut(out_t), (((0,), (1,)), ((), ())))
    attn_sum = head_sum_rows(attn_part, head_index, head_count).astype(f32)

    x_mid, pull_tail_a = jax.vjp(branch_tail, x_float, attn_sum, norm_gains[1], gate_a)
    normed_f, pull_in_f = jax.vjp(attn_input, x_mid, norm_gains[2], scale_f)
    act_f = normed_f.astype(bf16)
    gate_pre = matmul(act_f, gate_w)
    up_pre = matmul(act_f, up_w)
    unit_value, unit_pull = jax.vjp(swiglu_units, gate_pre, up_pre)
    hidden_units = unit_value.astype(bf16)
    ffn_sum = head_sum_rows(matmul(hidden_units, down_t, ROWS), head_index, head_count).astype(f32)
    out_value, pull_tail_f = jax.vjp(branch_tail, x_mid, ffn_sum, norm_gains[3], gate_f)
    hidden_out = out_value.astype(bf16)
    grad_mid, grad_ffn, grad_gain_fo, grad_gate_f = pull_tail_f(out_cotangent.astype(f32))
    grad_ffn_low = grad_ffn.astype(bf16)
    grad_units = matmul(grad_ffn_low, down_t)
    grad_gate_pre, grad_up_pre = unit_pull(grad_units)
    grad_gate_low = grad_gate_pre.astype(bf16)
    grad_up_low = grad_up_pre.astype(bf16)
    grad_act_f = head_sum_rows(
        matmul(grad_gate_low, gate_w, ROWS) + matmul(grad_up_low, up_w, ROWS), head_index, head_count
    ).astype(f32)
    down_part = matmul(grad_ffn_low, hidden_units, COLS).astype(bf16)
    gate_part = matmul(act_f, grad_gate_low, COLS).astype(bf16)
    up_part = matmul(act_f, grad_up_low, COLS).astype(bf16)
    down_grad = lax.psum_scatter(down_part, "seq", scatter_dimension=0, tiled=True).astype(f32).T
    gate_grad = lax.psum_scatter(gate_part, "seq", scatter_dimension=0, tiled=True).astype(f32)
    up_grad = lax.psum_scatter(up_part, "seq", scatter_dimension=0, tiled=True).astype(f32)

    grad_mid_f, grad_gain_fi, grad_scale_f = pull_in_f(grad_act_f)
    grad_x_tail, grad_attn, grad_gain_ao, grad_gate_a = pull_tail_a(grad_mid + grad_mid_f)
    grad_attn_low = grad_attn.astype(bf16)
    grad_mixed = matmul(out_t, grad_attn_low, (((0,), (1,)), ((), ())))[:cols]
    grad_mixed = grad_mixed.reshape(heads, HD, local_rows)
    out_part = matmul(grad_attn_low, mixed, (((0,), (1,)), ((), ()))).astype(bf16)
    grad_self = grad_mixed.astype(bf16)
    grad_cross = (gate_local * grad_mixed).astype(bf16)
    cross_gate_part = jnp.sum(grad_mixed * cross_out, axis=(1, 2)) * (1.0 - gate_local[:, 0, 0] ** 2)
    cross_delta = jnp.sum(grad_cross.astype(f32) * cross_out, axis=1)
    self_delta = jnp.sum(grad_self.astype(f32) * self_out, axis=1)
    pad_rows = lambda v: jnp.pad(v.reshape(cols, local_rows), ((0, wide - cols), (0, 0)))
    grad_self_t, grad_cross_t = pad_rows(grad_self), pad_rows(grad_cross)
    grad_self_tok, grad_cross_tok = grad_self_t.T, grad_cross_t.T
    cross_dq, cross_kv = attend_back(
        text_info, query_t, grad_cross_t, queries, grad_cross_tok, cross_lse, cross_delta,
        [text_piece], heads, clips, f32,
    )

    def back(group, parts):
        return attend_back(
            self_info(jnp.array(group)), query_t, grad_self_t, queries, grad_self_tok, self_lse, self_delta,
            [pieces[g] for g in group], heads, clips, bf16, parts,
        )

    if seq_count == 8:
        core = lambda v: swap(v, "seq", 8, lambda i: i ^ 1).astype(f32)
        dq1, kv_mine, kv_theirs = back((3, 2, 7, 6), 2)
        total = (kv_mine.astype(f32) + core(kv_theirs)).astype(bf16)
        first = swap(total, "seq", 8, other_way).astype(f32)
        dq2, kv_mine, kv_theirs = back((1, 5), 2)
        total = (kv_mine.astype(f32) + core(kv_theirs) + first[:local_rows]).astype(bf16)
        second = swap(total, "seq", 8, first_way).astype(f32)
        dq3, kv_mine, kv_theirs = back((0, 4), 2)
        own_kv = kv_mine.astype(f32) + core(kv_theirs) + first[local_rows:] + second
        query_grad_t = dq1 + dq2 + dq3
    else:
        query_grad_t, kv_all = back(tuple(range(seq_count)), 1)
        own_kv = lax.psum_scatter(kv_all, "seq", scatter_dimension=0, tiled=True).astype(f32)
    query_total = ((query_grad_t + cross_dq) * HD**-0.5).T
    query_low, grad_query_gain = norm_rope_back(query_pre, query_gain, cos, sin, query_total, bf16)
    key_low, grad_key_gain = norm_rope_back(key_pre, key_gain, cos, sin, own_kv[:, :wide], bf16)
    text_low, grad_text_gain = norm_rope_back(text_key_pre, key_gain, *flat, cross_kv[:, :wide], bf16)
    qkv_low = jnp.concatenate([query_low, key_low, own_kv[:, wide:].astype(bf16)], axis=1)
    act_part = matmul(qkv_low, w_qkv, ROWS)
    grad_act_a = head_sum_rows(act_part, head_index, head_count).astype(f32)
    qkv_part = matmul(act_a, qkv_low, COLS).astype(bf16)
    own_qkv = scatter_sum(jnp.concatenate([qkv_part, out_part], axis=1), seq_index, seq_count)
    grad_x_in, grad_gain_ai, grad_scale_a = pull_in_a(grad_act_a)
    input_grad = grad_x_tail + grad_x_in

    fold = lambda v: v[0, :HD] + v[0, HD:]
    gains = jnp.stack([fold(grad_query_gain), fold(grad_key_gain + grad_text_gain)])
    gains = sum_all(gains, (("head", head_count),))
    flat_sum = jnp.concatenate(
        [grad_scale_a, grad_gate_a, grad_scale_f, grad_gate_f, grad_gain_ai, grad_gain_ao, grad_gain_fi, grad_gain_fo]
        + [gains.reshape(-1), cross_gate_part]
    )
    flat_sum = sum_all(flat_sum, (("seq", seq_count),))
    mod_grad = flat_sum[: 4 * model_width]
    norm_gains_grad = flat_sum[4 * model_width : 8 * model_width].reshape(4, model_width)
    qk_gains_grad = flat_sum[8 * model_width : 8 * model_width + 2 * HD].reshape(2, HD)
    cross_gate_grad = flat_sum[8 * model_width + 2 * HD :]
    own_mod = lax.dynamic_slice_in_dim(
        mod_grad, (seq_index * head_count + head_index) * piece_width, piece_width
    )
    ada_grad = cond_act.astype(f32)[:, None] * own_mod[None, :]
    text_total = lax.psum(jnp.concatenate([text_low, cross_kv[:, wide:].astype(bf16)], axis=1), "seq")
    text_grad = matmul(own_text, text_total, COLS)
    return (
        hidden_out,
        input_grad,
        ada_grad,
        norm_gains_grad,
        qk_gains_grad,
        cut(own_qkv[:, :wide]),
        cut(own_qkv[:, wide : 2 * wide]),
        cut(own_qkv[:, 2 * wide : 3 * wide]),
        own_qkv[:, 3 * wide :].T,
        cross_gate_grad,
        cut(text_grad[:, :wide]),
        cut(text_grad[:, wide:]),
        gate_grad,
        up_grad,
        down_grad,
    )


def solution(mesh):
    in_specs = (
        P("seq", None),
        P(),
        P(),
        P(),
        P(None, ("seq", "head")),
        P(),
        P(),
        P("seq", "head"),
        P("seq", "head"),
        P("seq", "head"),
        P("head", "seq"),
        P("head"),
        P("seq", "head"),
        P("seq", "head"),
        P("seq", "head"),
        P("seq", "head"),
        P("head", "seq"),
        P("seq", None),
    )
    out_specs = (
        P("seq", None),
        P("seq", None),
        P(None, ("seq", "head")),
        P(),
        P(),
        P("seq", "head"),
        P("seq", "head"),
        P("seq", "head"),
        P("head", "seq"),
        P("head"),
        P("seq", "head"),
        P("seq", "head"),
        P("seq", "head"),
        P("seq", "head"),
        P("head", "seq"),
    )
    body = functools.partial(per_device, mesh.shape["seq"], mesh.shape["head"])
    return jax.shard_map(body, mesh=mesh, in_specs=in_specs, out_specs=out_specs, check_vma=False)
```

time: 1410 us -> 720 us (0.51)
  waiting for transfers between devices: 763 us -> 258 us
  matrix products: 304 us -> 54.6 us
  blocking collectives: 127 us -> 0 us
  starting transfers between devices: 1.73 us -> 119 us
  Pallas kernels: 0 us -> 100 us
    psum x5 -> x2, waiting for transfers between devices: 286 us -> 0.01 us  [the longest x1 0.01 us: per_device(): text_pre = lax.psum(matmul(own_text, w_text).astype(bf16), 'seq')]
    reduce_scatter x9 -> x3, waiting for transfers between devices: 276 us -> 0.02 us  [the longest x1 0.02 us: per_device(): lax.psum_scatter(down_part, 'seq', scatter_dimension=0, tiled=True)]
    ppermute x0 -> x87, waiting for transfers between devices: none -> 257 us  [the longest x16 120 us: head_sum(): back = lax.ppermute(total, 'head', [(1, 0), (2, 3)])]
    dot_general x87 -> x18, matrix products: 298 us -> 54.6 us  [the longest x12 32.9 us: matmul(): return lax.dot_general(left, right, dims, preferred_element_type=f32)]
    all_gather x11 -> x3, waiting for transfers between devices: 195 us -> 0.01 us  [the longest x1 0.01 us: per_device(): gate_w = lax.all_gather(w_gate, 'seq', axis=0, tiled=True)]
    ppermute x0 -> x87, starting transfers between devices: none -> 118 us  [the longest x16 57.2 us: head_sum(): got = lax.ppermute(chunk, 'head', [(0, 1), (3, 2)])]
    pallas_call x0 -> x16, Pallas kernels: none -> 100 us  [the longest x4 62.2 us: attend_back(): pl.pallas_call(functools.partial(bwd_kernel, heads, clips, count, tile),...]
    unnamed x2 -> x0, blocking collectives: 64.6 us -> none
  transfers between devices with their start and end apart: 25 -> 95, of which waited for: 21 -> 40; matrix products, arithmetic and copies ran while one was open for 20% -> 22% of each run, Pallas kernels for 0% -> 13%
where the time goes in v1:
time: 720 us; the launch traced here: 714 us
  waiting for transfers between devices  258 us (36%)
  starting transfers between devices  119 us (17%)
  other arithmetic  101 us (14%)
  Pallas kernels  100 us (14%)
  local copies, waits for them, and re-layouts  63.5 us (9%)
  matrix products  54.6 us (8%)
  between operations  17.6 us (2%)
    ppermute x16, waiting for transfers between devices, head_sum(): back = lax.ppermute(total, 'head', [(1, 0), (2, 3)])  120 us
    ppermute x39, waiting for transfers between devices, swap(): return lax.ppermute(value, axis, [(i, to(i)) for i in range(count)])  74 us
    ppermute x16, waiting for transfers between devices, head_sum(): got = lax.ppermute(chunk, 'head', [(0, 1), (3, 2)])  63.1 us
    pallas_call x4, Pallas kernels, attend_back(): pl.pallas_call(functools.partial(bwd_kernel, heads, clips, count, tile),...  62.2 us
    ppermute x16, starting transfers between devices, head_sum(): got = lax.ppermute(chunk, 'head', [(0, 1), (3, 2)])  57.2 us
    dot_general x12, matrix products, matmul(): return lax.dot_general(left, right, dims, preferred_element_type=f32)  32.9 us
    ppermute x39, starting transfers between devices, swap(): return lax.ppermute(value, axis, [(i, to(i)) for i in range(count)])  28.2 us
    pallas_call x4, Pallas kernels, attend(): pl.pallas_call(functools.partial(fwd_kernel, heads, clips, count, tile),...  26.2 us
  transfers between devices with their start and end apart: 95, of which 40 were waited for; matrix products, arithmetic and copies ran while one was open for 22% of the time, Pallas kernels for 13%

profile of v1, /device:TPU:0, one launch (start us, length us, event | category | flops | bytes accessed | tf_op | source)
XLA Modules:
  0.0 713.8 jit_solution(7810205703620068185)
XLA Ops:
  20.5 6.8 collective-permute-done.5.rest_1_
  30.5 5.8 collective-permute-done.2
  60.5 18.1 %collective-permute-done.13.rest_0_ = bf16[512,768]{1,0:T(8,128)(2,1)} collective-permute-done((bf16[512,768]{1,0:T(8,128)(2,1)}, bf16[512,768]{1,0:T(8,128)(2,1)}, u32[]{:S(2)}, u32[]{:S(2)}) %collective-permute-start.13) | collective-permute-done | bytes 786464 | tf_op jit(solution)/shard_map/ppermute | solution.py:242
  95.1 6.1 attend.4
  101.3 10.8 %attend.5 = f32[6,80,512]{2,1,0:T(8,128)S(1)} custom-call(s32[21]{0:T(128)S(1)} %concatenate.68.info, bf16[384,512]{1,0:T(8,128)(2,1)S(1)} %copy-done.9, bf16[512,768]{1,0:T(8,128)(2,1)} %collective-permute-done.13.rest_0_, bf16[512,768]{1,0:T(8,128)(2,1)} %collective-permute-done.14.rest_1_, bf16[512,768]{1,0:T(8,128)(2,1)} %collective-permute-done.15.rest_2_.rest_1_, ...), custom_call_target="tpu_custom_call" | custom-call | flops 6442450944 | bytes 4128768 | tf_op jit(solution)/shard_map/attend/pallas_call | solution.py:112
  116.4 6.4 attend.6
  139.6 8.1 %collective-permute-done.26 = bf16[128,1536]{1,0:T(8,128)(2,1)S(1)} collective-permute-done((bf16[128,1536]{1,0:T(8,128)(2,1)S(1)}, bf16[128,1536]{1,0:T(8,128)(2,1)S(1)}, u32[]{:S(2)}, u32[]{:S(2)}) %collective-permute-start.26) | collective-permute-done | bytes 393248 | tf_op jit(solution)/shard_map/ppermute | solution.py:334
  147.7 7.6 %collective-permute-done.29 = bf16[128,1536]{1,0:T(8,128)(2,1)S(1)} collective-permute-done((bf16[128,1536]{1,0:T(8,128)(2,1)S(1)}, bf16[128,1536]{1,0:T(8,128)(2,1)S(1)}, u32[]{:S(2)}, u32[]{:S(2)}) %collective-permute-start.29) | collective-permute-done | bytes 393248 | tf_op jit(solution)/shard_map/ppermute | solution.py:334
  156.4 5.2 collective-permute-start.35
  165.9 5.0 collective-permute-start.32
  172.8 5.7 collective-permute-done.32
  187.1 11.0 %collective-permute-done.28 = bf16[128,1536]{1,0:T(8,128)(2,1)S(1)} collective-permute-done((bf16[128,1536]{1,0:T(8,128)(2,1)S(1)}, bf16[128,1536]{1,0:T(8,128)(2,1)S(1)}, u32[]{:S(2)}, u32[]{:S(2)}) %collective-permute-start.28) | collective-permute-done | bytes 393248 | tf_op jit(solution)/shard_map/ppermute | solution.py:339
  198.2 8.4 %collective-permute-done.31 = bf16[128,1536]{1,0:T(8,128)(2,1)S(1)} collective-permute-done((bf16[128,1536]{1,0:T(8,128)(2,1)S(1)}, bf16[128,1536]{1,0:T(8,128)(2,1)S(1)}, u32[]{:S(2)}, u32[]{:S(2)}) %collective-permute-start.31) | collective-permute-done | bytes 393248 | tf_op jit(solution)/shard_map/ppermute | solution.py:339
  206.6 8.4 %collective-permute-done.37 = bf16[128,1536]{1,0:T(8,128)(2,1)S(1)} collective-permute-done((bf16[128,1536]{1,0:T(8,128)(2,1)S(1)}, bf16[128,1536]{1,0:T(8,128)(2,1)S(1)}, u32[]{:S(2)}, u32[]{:S(2)}) %collective-permute-start.37) | collective-permute-done | bytes 393248 | tf_op jit(solution)/shard_map/ppermute | solution.py:339
  215.0 4.8 collective-permute-done.34
  227.3 5.5 fusion.90
  232.8 6.5 multiply_convert_fusion.2
  247.1 8.1 %collective-permute-done.38 = bf16[128,1536]{1,0:T(8,128)(2,1)S(1)} collective-permute-done((bf16[128,1536]{1,0:T(8,128)(2,1)S(1)}, bf16[128,1536]{1,0:T(8,128)(2,1)S(1)}, u32[]{:S(2)}, u32[]{:S(2)}) %collective-permute-start.38) | collective-permute-done | bytes 393248 | tf_op jit(solution)/shard_map/ppermute | solution.py:334
  260.4 5.2 collective-permute-start.47
  268.5 5.0 collective-permute-start.44
  287.7 13.0 %collective-permute-done.40 = bf16[128,1536]{1,0:T(8,128)(2,1)S(1)} collective-permute-done((bf16[128,1536]{1,0:T(8,128)(2,1)S(1)}, bf16[128,1536]{1,0:T(8,128)(2,1)S(1)}, u32[]{:S(2)}, u32[]{:S(2)}) %collective-permute-start.40) | collective-permute-done | bytes 393248 | tf_op jit(solution)/shard_map/ppermute | solution.py:339
  300.7 8.0 %collective-permute-done.43 = bf16[128,1536]{1,0:T(8,128)(2,1)S(1)} collective-permute-done((bf16[128,1536]{1,0:T(8,128)(2,1)S(1)}, bf16[128,1536]{1,0:T(8,128)(2,1)S(1)}, u32[]{:S(2)}, u32[]{:S(2)}) %collective-permute-start.43) | collective-permute-done | bytes 393248 | tf_op jit(solution)/shard_map/ppermute | solution.py:339
  338.1 8.0 %collective-permute-done.53 = bf16[128,1536]{1,0:T(8,128)(2,1)S(1)} collective-permute-done((bf16[128,1536]{1,0:T(8,128)(2,1)S(1)}, bf16[128,1536]{1,0:T(8,128)(2,1)S(1)}, u32[]{:S(2)}, u32[]{:S(2)}) %collective-permute-start.53) | collective-permute-done | bytes 393248 | tf_op jit(solution)/shard_map/ppermute | solution.py:334
  347.2 5.1 collective-permute-start.59
  357.1 5.0 collective-permute-start.56
  376.6 9.3 %collective-permute-done.52 = bf16[128,1536]{1,0:T(8,128)(2,1)S(1)} collective-permute-done((bf16[128,1536]{1,0:T(8,128)(2,1)S(1)}, bf16[128,1536]{1,0:T(8,128)(2,1)S(1)}, u32[]{:S(2)}, u32[]{:S(2)}) %collective-permute-start.52) | collective-permute-done | bytes 393248 | tf_op jit(solution)/shard_map/ppermute | solution.py:339
  385.9 6.4 collective-permute-done.55
  404.1 5.9 fusion.20
  423.3 8.3 %attend_back.7 = (f32[384,512]{1,0:T(8,128)}, f32[512,768]{1,0:T(8,128)}) custom-call(s32[18]{0:T(128)} %copy-done.13, bf16[384,512]{1,0:T(8,128)(2,1)} %copy.120.qt, bf16[384,512]{1,0:T(8,128)(2,1)} %copy.143.dot_t, bf16[512,384]{1,0:T(8,128)(2,1)} %get-tuple-element.126.q_tok, bf16[512,384]{1,0:T(8,128)(2,1)} %bitcast.92, f32[6,512]{1,0:T(8,128)} %fusion.67.lse, ...), custom_call_target="tpu_custom_call" | custom-call | flops 4026531840 | bytes 2359296 | tf_op jit(solution)/shard_map/attend_back/pallas_call | solution.py:193
  436.5 5.6 convolution_convert_fusion.1
  443.3 4.9 convolution_convert_fusion.2
  452.8 6.4 fusion.22
  461.2 25.4 %attend_back.4 = (f32[384,512]{1,0:T(8,128)}, bf16[1024,768]{1,0:T(8,128)(2,1)}, bf16[1024,768]{1,0:T(8,128)(2,1)}) custom-call(s32[21]{0:T(128)} %concatenate.76.info, bf16[384,512]{1,0:T(8,128)(2,1)} %copy.120.qt, bf16[384,512]{1,0:T(8,128)(2,1)} %copy.132.dot_t, bf16[512,384]{1,0:T(8,128)(2,1)} %get-tuple-element.126.q_tok, bf16[512,384]{1,0:T(8,128)(2,1)} %bitcast.89, ...), custom_call_target="tpu_custom_call" | custom-call | flops 16106127360 | bytes 7077888 | tf_op jit(solution)/shard_map/attend_back/pallas_call | solution.py:193
  492.5 14.4 %attend_back.6 = (f32[384,512]{1,0:T(8,128)}, bf16[512,768]{1,0:T(8,128)(2,1)}, bf16[512,768]{1,0:T(8,128)(2,1)}) custom-call(s32[19]{0:T(128)} %copy-done.12, bf16[384,512]{1,0:T(8,128)(2,1)} %copy.120.qt, bf16[384,512]{1,0:T(8,128)(2,1)} %copy.132.dot_t, bf16[512,384]{1,0:T(8,128)(2,1)} %get-tuple-element.126.q_tok, bf16[512,384]{1,0:T(8,128)(2,1)} %bitcast.90, ...), custom_call_target="tpu_custom_call" | custom-call | flops 8053063680 | bytes 3932160 | tf_op jit(solution)/shard_map/attend_back/pallas_call | solution.py:193
  511.4 14.2 %attend_back.5 = (f32[384,512]{1,0:T(8,128)}, bf16[512,768]{1,0:T(8,128)(2,1)}, bf16[512,768]{1,0:T(8,128)(2,1)}) custom-call(s32[19]{0:T(128)} %concatenate.77.info, bf16[384,512]{1,0:T(8,128)(2,1)} %copy.120.qt, bf16[384,512]{1,0:T(8,128)(2,1)} %copy.132.dot_t, bf16[512,384]{1,0:T(8,128)(2,1)} %get-tuple-element.126.q_tok, bf16[512,384]{1,0:T(8,128)(2,1)} %bitcast.91, ...), custom_call_target="tpu_custom_call" | custom-call | flops 8053063680 | bytes 3932160 | tf_op jit(solution)/shard_map/attend_back/pallas_call | solution.py:193
  533.9 5.1 fusion.28
  540.8 4.7 fusion.27
  545.5 9.1 %collective-permute-done.64 = bf16[1024,768]{1,0:T(8,128)(2,1)S(1)} collective-permute-done((bf16[1024,768]{1,0:T(8,128)(2,1)S(1)}, bf16[1024,768]{1,0:T(8,128)(2,1)S(1)}, u32[]{:S(2)}, u32[]{:S(2)}) %collective-permute-start.64) | collective-permute-done | bytes 1572896 | tf_op jit(solution)/shard_map/ppermute | solution.py:242
  561.1 11.4 %collective-permute-done.66 = bf16[512,768]{1,0:T(8,128)(2,1)S(1)} collective-permute-done((bf16[512,768]{1,0:T(8,128)(2,1)}, bf16[512,768]{1,0:T(8,128)(2,1)S(1)}, u32[]{:S(2)}, u32[]{:S(2)}) %collective-permute-start.66) | collective-permute-done | bytes 786464 | tf_op jit(solution)/shard_map/ppermute | solution.py:242
  590.3 6.9 copy.146
  601.9 4.6 collective-permute-start.76
  611.3 5.9 collective-permute-start.73
  618.0 7.6 %collective-permute-done.73 = bf16[128,1536]{1,0:T(8,128)(2,1)S(1)} collective-permute-done((bf16[128,1536]{1,0:T(8,128)(2,1)S(1)}, bf16[128,1536]{1,0:T(8,128)(2,1)S(1)}, u32[]{:S(2)}, u32[]{:S(2)}) %collective-permute-start.73) | collective-permute-done | bytes 393248 | tf_op jit(solution)/shard_map/ppermute | solution.py:334
  632.6 10.4 %collective-permute-done.69 = bf16[128,1536]{1,0:T(8,128)(2,1)S(1)} collective-permute-done((bf16[128,1536]{1,0:T(8,128)(2,1)S(1)}, bf16[128,1536]{1,0:T(8,128)(2,1)S(1)}, u32[]{:S(2)}, u32[]{:S(2)}) %collective-permute-start.69) | collective-permute-done | bytes 393248 | tf_op jit(solution)/shard_map/ppermute | solution.py:339
  643.1 8.3 %collective-permute-done.72 = bf16[128,1536]{1,0:T(8,128)(2,1)S(1)} collective-permute-done((bf16[128,1536]{1,0:T(8,128)(2,1)S(1)}, bf16[128,1536]{1,0:T(8,128)(2,1)S(1)}, u32[]{:S(2)}, u32[]{:S(2)}) %collective-permute-start.72) | collective-permute-done | bytes 393248 | tf_op jit(solution)/shard_map/ppermute | solution.py:339
  651.5 8.4 %collective-permute-done.78 = bf16[128,1536]{1,0:T(8,128)(2,1)S(1)} collective-permute-done((bf16[128,1536]{1,0:T(8,128)(2,1)S(1)}, bf16[128,1536]{1,0:T(8,128)(2,1)S(1)}, u32[]{:S(2)}, u32[]{:S(2)}) %collective-permute-start.78) | collective-permute-done | bytes 393248 | tf_op jit(solution)/shard_map/ppermute | solution.py:339
  659.9 7.1 collective-permute-done.75
  682.3 4.7 collective-permute-done.82
  (707 shorter events, 313.6 us)
Async XLA Ops:
  7.2 73.2 %all-reduce.3.cloned.1.call-start = ((), (), s32[]{:S(2)}) async-start(), calls=%async_computation.3 | async-start | bytes 1572864 | tf_op jit(solution)/shard_map/psum | solution.py:472
  10.2 217.1 %all-gather.4.cloned.1.call-start = ((), (), s32[]{:S(2)}) async-start(), calls=%async_computation.4 | async-start | bytes 3538944 | tf_op jit(solution)/shard_map/all_gather | solution.py:473
  11.0 221.8 %all-gather.6.cloned.1.call-start = ((), (), s32[]{:S(2)}) async-start(), calls=%async_computation.5 | async-start | bytes 3538944 | tf_op jit(solution)/shard_map/all_gather | solution.py:474
  11.1 34.8 %collective-permute-start.8 = (bf16[192,1152]{1,0:T(8,128)(2,1)S(1)}, bf16[192,1152]{1,0:T(8,128)(2,1)S(1)}, u32[]{:S(2)}, u32[]{:S(2)}) collective-permute-start(bf16[192,1152]{1,0:T(8,128)(2,1)S(1)} %constant_dynamic-update-slice_fusion.rest_0_), channel_id=1, source_target_pairs={{0,4},{4,0},{8,12},{12,8},{16,20},{20,16},{24,28},{28,24},{1,5},{5... | collective-permute-start | bytes 1327112 | tf_op jit(solution)/shard_map/ppermute | solution.py:242
  11.6 26.7 %collective-permute-start.6 = (bf16[192,1152]{1,0:T(8,128)(2,1)S(1)}, bf16[192,1152]{1,0:T(8,128)(2,1)S(1)}, u32[]{:S(2)}, u32[]{:S(2)}) collective-permute-start(bf16[192,1152]{1,0:T(8,128)(2,1)S(1)} %constant_dynamic-update-slice_fusion.rest_0_), channel_id=1, source_target_pairs={{0,16},{4,12},{8,24},{12,4},{16,0},{20,28},{24,8},{28,20},{1,17},{... | collective-permute-start | bytes 1327112 | tf_op jit(solution)/shard_map/ppermute | solution.py:242
  16.7 222.6 %all-gather.8.cloned.1.call-start = ((), (), s32[]{:S(2)}) async-start(), calls=%async_computation.6 | async-start | bytes 3538944 | tf_op jit(solution)/shard_map/all_gather | solution.py:475
  54.6 23.9 %collective-permute-start.13 = (bf16[512,768]{1,0:T(8,128)(2,1)}, bf16[512,768]{1,0:T(8,128)(2,1)}, u32[]{:S(2)}, u32[]{:S(2)}) collective-permute-start(bf16[512,768]{1,0:T(8,128)(2,1)} %pad_maximum_fusion.7.rest_0_), channel_id=1, source_target_pairs={{0,8},{4,20},{8,0},{12,28},{16,24},{20,4},{24,16},{28,12},{1,9},{5... | collective-permute-start | bytes 2359304 | tf_op jit(solution)/shard_map/ppermute | solution.py:242
  57.6 25.0 %collective-permute-start.14 = (bf16[512,768]{1,0:T(8,128)(2,1)}, bf16[512,768]{1,0:T(8,128)(2,1)}, u32[]{:S(2)}, u32[]{:S(2)}) collective-permute-start(bf16[512,768]{1,0:T(8,128)(2,1)} %pad_maximum_fusion.7.rest_0_), channel_id=1, source_target_pairs={{0,16},{4,12},{8,24},{12,4},{16,0},{20,28},{24,8},{28,20},{1,17},{... | collective-permute-start | bytes 2359304 | tf_op jit(solution)/shard_map/ppermute | solution.py:242
  60.5 34.6 %collective-permute-start.12 = (bf16[512,768]{1,0:T(8,128)(2,1)}, bf16[512,768]{1,0:T(8,128)(2,1)}, u32[]{:S(2)}, u32[]{:S(2)}) collective-permute-start(bf16[512,768]{1,0:T(8,128)(2,1)} %pad_maximum_fusion.7.rest_0_), channel_id=1, source_target_pairs={{0,4},{4,0},{8,12},{12,8},{16,20},{20,16},{24,28},{28,24},{1,5},{5... | collective-permute-start | bytes 2359304 | tf_op jit(solution)/shard_map/ppermute | solution.py:242
  78.5 16.5 %collective-permute-start.17 = (bf16[512,768]{1,0:T(8,128)(2,1)}, bf16[512,768]{1,0:T(8,128)(2,1)}, u32[]{:S(2)}, u32[]{:S(2)}) collective-permute-start(bf16[512,768]{1,0:T(8,128)(2,1)} %collective-permute-done.13.rest_0_), channel_id=1, source_target_pairs={{0,16},{4,12},{8,24},{12,4},{16,0},{20,28},{24,8},{28,20},{1,17},{... | collective-permute-start | bytes 2359304 | tf_op jit(solution)/shard_map/ppermute | solution.py:242
  82.5 18.7 %collective-permute-start.15 = (bf16[512,768]{1,0:T(8,128)(2,1)}, bf16[512,768]{1,0:T(8,128)(2,1)}, u32[]{:S(2)}, u32[]{:S(2)}) collective-permute-start(bf16[512,768]{1,0:T(8,128)(2,1)} %collective-permute-done.13.rest_0_), channel_id=1, source_target_pairs={{0,4},{4,0},{8,12},{12,8},{16,20},{20,16},{24,28},{28,24},{1,5},{5... | collective-permute-start | bytes 2359304 | tf_op jit(solution)/shard_map/ppermute | solution.py:242
  82.6 18.6 %collective-permute-start.16 = (bf16[512,768]{1,0:T(8,128)(2,1)}, bf16[512,768]{1,0:T(8,128)(2,1)}, u32[]{:S(2)}, u32[]{:S(2)}) collective-permute-start(bf16[512,768]{1,0:T(8,128)(2,1)} %collective-permute-done.14.rest_1_), channel_id=1, source_target_pairs={{0,4},{4,0},{8,12},{12,8},{16,20},{20,16},{24,28},{28,24},{1,5},{5... | collective-permute-start | bytes 2359304 | tf_op jit(solution)/shard_map/ppermute | solution.py:242
  95.1 17.2 %collective-permute-start.18 = (bf16[512,768]{1,0:T(8,128)(2,1)}, bf16[512,768]{1,0:T(8,128)(2,1)S(1)}, u32[]{:S(2)}, u32[]{:S(2)}) collective-permute-start(bf16[512,768]{1,0:T(8,128)(2,1)} %collective-permute-done.17.rest_0_), channel_id=1, source_target_pairs={{0,4},{4,0},{8,12},{12,8},{16,20},{20,16},{24,28},{28,24},{1,5},{5... | collective-permute-start | bytes 2359304 | tf_op jit(solution)/shard_map/ppermute | solution.py:242
  112.3 17.5 %collective-permute-start.22 = (bf16[192,384]{1,0:T(8,128)(2,1)S(1)}, bf16[192,384]{1,0:T(8,128)(2,1)S(1)}, u32[]{:S(2)}, u32[]{:S(2)}) collective-permute-start(bf16[192,384]{1,0:T(8,128)(2,1)S(1)} %bitcast.78), channel_id=1, source_target_pairs={{0,4},{4,0},{8,12},{12,8},{16,20},{20,16},{24,28},{28,24},{1,5},{5... | collective-permute-start | bytes 442376 | tf_op jit(solution)/shard_map/ppermute | solution.py:242
  138.3 17.1 %collective-permute-start.29 = (bf16[128,1536]{1,0:T(8,128)(2,1)S(1)}, bf16[128,1536]{1,0:T(8,128)(2,1)S(1)}, u32[]{:S(2)}, u32[]{:S(2)}) collective-permute-start(bf16[128,1536]{1,0:T(8,128)(2,1)S(1)} %get-tuple-element.117), channel_id=1, source_target_pairs={{0,1},{3,2},{4,5},{7,6},{8,9},{11,10},{12,13},{15,14},{16,17},{19,... | collective-permute-start | bytes 1179656 | tf_op jit(solution)/shard_map/ppermute | solution.py:334
  161.6 396.2 %all-reduce.5.cloned.1.call-start = ((), (), s32[]{:S(2)}) async-start(), calls=%async_computation.7 | async-start | bytes 1572864 | tf_op jit(solution)/shard_map/psum | solution.py:627
  164.4 18.3 %collective-permute-start.30 = (bf16[128,1536]{1,0:T(8,128)(2,1)}, bf16[128,1536]{1,0:T(8,128)(2,1)S(1)}, u32[]{:S(2)}, u32[]{:S(2)}) collective-permute-start(bf16[128,1536]{1,0:T(8,128)(2,1)} %get-tuple-element.113), channel_id=1, source_target_pairs={{1,2},{2,1},{5,6},{6,5},{9,10},{10,9},{13,14},{14,13},{17,18},{18,... | collective-permute-start | bytes 1179656 | tf_op jit(solution)/shard_map/ppermute | solution.py:337
  181.4 16.7 %collective-permute-start.28 = (bf16[128,1536]{1,0:T(8,128)(2,1)S(1)}, bf16[128,1536]{1,0:T(8,128)(2,1)S(1)}, u32[]{:S(2)}, u32[]{:S(2)}) collective-permute-start(bf16[128,1536]{1,0:T(8,128)(2,1)S(1)} %add_convert_fusion.33), channel_id=1, source_target_pairs={{1,0},{2,3},{5,4},{6,7},{9,8},{10,11},{13,12},{14,15},{17,16},{18,... | collective-permute-start | bytes 1179656 | tf_op jit(solution)/shard_map/ppermute | solution.py:339
  182.8 23.7 %collective-permute-start.31 = (bf16[128,1536]{1,0:T(8,128)(2,1)S(1)}, bf16[128,1536]{1,0:T(8,128)(2,1)S(1)}, u32[]{:S(2)}, u32[]{:S(2)}) collective-permute-start(bf16[128,1536]{1,0:T(8,128)(2,1)S(1)} %add_convert_fusion.31), channel_id=1, source_target_pairs={{1,0},{2,3},{5,4},{6,7},{9,8},{10,11},{13,12},{14,15},{17,16},{18,... | collective-permute-start | bytes 1179656 | tf_op jit(solution)/shard_map/ppermute | solution.py:339
  184.2 30.7 %collective-permute-start.37 = (bf16[128,1536]{1,0:T(8,128)(2,1)S(1)}, bf16[128,1536]{1,0:T(8,128)(2,1)S(1)}, u32[]{:S(2)}, u32[]{:S(2)}) collective-permute-start(bf16[128,1536]{1,0:T(8,128)(2,1)S(1)} %add_convert_fusion.27), channel_id=1, source_target_pairs={{1,0},{2,3},{5,4},{6,7},{9,8},{10,11},{13,12},{14,15},{17,16},{18,... | collective-permute-start | bytes 1179656 | tf_op jit(solution)/shard_map/ppermute | solution.py:339
  185.7 34.2 %collective-permute-start.34 = (bf16[128,1536]{1,0:T(8,128)(2,1)S(1)}, bf16[128,1536]{1,0:T(8,128)(2,1)S(1)}, u32[]{:S(2)}, u32[]{:S(2)}) collective-permute-start(bf16[128,1536]{1,0:T(8,128)(2,1)S(1)} %add_convert_fusion.29), channel_id=1, source_target_pairs={{1,0},{2,3},{5,4},{6,7},{9,8},{10,11},{13,12},{14,15},{17,16},{18,... | collective-permute-start | bytes 1179656 | tf_op jit(solution)/shard_map/ppermute | solution.py:339
  267.0 16.3 %collective-permute-start.42 = (bf16[128,1536]{1,0:T(8,128)(2,1)}, bf16[128,1536]{1,0:T(8,128)(2,1)S(1)}, u32[]{:S(2)}, u32[]{:S(2)}) collective-permute-start(bf16[128,1536]{1,0:T(8,128)(2,1)} %get-tuple-element.107), channel_id=1, source_target_pairs={{1,2},{2,1},{5,6},{6,5},{9,10},{10,9},{13,14},{14,13},{17,18},{18,... | collective-permute-start | bytes 1179656 | tf_op jit(solution)/shard_map/ppermute | solution.py:337
  281.9 18.7 %collective-permute-start.40 = (bf16[128,1536]{1,0:T(8,128)(2,1)S(1)}, bf16[128,1536]{1,0:T(8,128)(2,1)S(1)}, u32[]{:S(2)}, u32[]{:S(2)}) collective-permute-start(bf16[128,1536]{1,0:T(8,128)(2,1)S(1)} %add_convert_fusion.25), channel_id=1, source_target_pairs={{1,0},{2,3},{5,4},{6,7},{9,8},{10,11},{13,12},{14,15},{17,16},{18,... | collective-permute-start | bytes 1179656 | tf_op jit(solution)/shard_map/ppermute | solution.py:339
  283.4 25.4 %collective-permute-start.43 = (bf16[128,1536]{1,0:T(8,128)(2,1)S(1)}, bf16[128,1536]{1,0:T(8,128)(2,1)S(1)}, u32[]{:S(2)}, u32[]{:S(2)}) collective-permute-start(bf16[128,1536]{1,0:T(8,128)(2,1)S(1)} %add_convert_fusion.23), channel_id=1, source_target_pairs={{1,0},{2,3},{5,4},{6,7},{9,8},{10,11},{13,12},{14,15},{17,16},{18,... | collective-permute-start | bytes 1179656 | tf_op jit(solution)/shard_map/ppermute | solution.py:339
  284.8 28.2 %collective-permute-start.49 = (bf16[128,1536]{1,0:T(8,128)(2,1)S(1)}, bf16[128,1536]{1,0:T(8,128)(2,1)S(1)}, u32[]{:S(2)}, u32[]{:S(2)}) collective-permute-start(bf16[128,1536]{1,0:T(8,128)(2,1)S(1)} %add_convert_fusion.19), channel_id=1, source_target_pairs={{1,0},{2,3},{5,4},{6,7},{9,8},{10,11},{13,12},{14,15},{17,16},{18,... | collective-permute-start | bytes 1179656 | tf_op jit(solution)/shard_map/ppermute | solution.py:339
  286.2 31.0 %collective-permute-start.46 = (bf16[128,1536]{1,0:T(8,128)(2,1)S(1)}, bf16[128,1536]{1,0:T(8,128)(2,1)S(1)}, u32[]{:S(2)}, u32[]{:S(2)}) collective-permute-start(bf16[128,1536]{1,0:T(8,128)(2,1)S(1)} %add_convert_fusion.21), channel_id=1, source_target_pairs={{1,0},{2,3},{5,4},{6,7},{9,8},{10,11},{13,12},{14,15},{17,16},{18,... | collective-permute-start | bytes 1179656 | tf_op jit(solution)/shard_map/ppermute | solution.py:339
  355.7 16.2 %collective-permute-start.54 = (bf16[128,1536]{1,0:T(8,128)(2,1)}, bf16[128,1536]{1,0:T(8,128)(2,1)S(1)}, u32[]{:S(2)}, u32[]{:S(2)}) collective-permute-start(bf16[128,1536]{1,0:T(8,128)(2,1)} %get-tuple-element.101), channel_id=1, source_target_pairs={{1,2},{2,1},{5,6},{6,5},{9,10},{10,9},{13,14},{14,13},{17,18},{18,... | collective-permute-start | bytes 1179656 | tf_op jit(solution)/shard_map/ppermute | solution.py:337
  372.1 20.2 %collective-permute-start.55 = (bf16[128,1536]{1,0:T(8,128)(2,1)S(1)}, bf16[128,1536]{1,0:T(8,128)(2,1)S(1)}, u32[]{:S(2)}, u32[]{:S(2)}) collective-permute-start(bf16[128,1536]{1,0:T(8,128)(2,1)S(1)} %add_convert_fusion.15), channel_id=1, source_target_pairs={{1,0},{2,3},{5,4},{6,7},{9,8},{10,11},{13,12},{14,15},{17,16},{18,... | collective-permute-start | bytes 1179656 | tf_op jit(solution)/shard_map/ppermute | solution.py:339
  373.6 22.9 %collective-permute-start.61 = (bf16[128,1536]{1,0:T(8,128)(2,1)S(1)}, bf16[128,1536]{1,0:T(8,128)(2,1)S(1)}, u32[]{:S(2)}, u32[]{:S(2)}) collective-permute-start(bf16[128,1536]{1,0:T(8,128)(2,1)S(1)} %add_convert_fusion.11), channel_id=1, source_target_pairs={{1,0},{2,3},{5,4},{6,7},{9,8},{10,11},{13,12},{14,15},{17,16},{18,... | collective-permute-start | bytes 1179656 | tf_op jit(solution)/shard_map/ppermute | solution.py:339
  375.2 25.5 %collective-permute-start.58 = (bf16[128,1536]{1,0:T(8,128)(2,1)S(1)}, bf16[128,1536]{1,0:T(8,128)(2,1)S(1)}, u32[]{:S(2)}, u32[]{:S(2)}) collective-permute-start(bf16[128,1536]{1,0:T(8,128)(2,1)S(1)} %add_convert_fusion.13), channel_id=1, source_target_pairs={{1,0},{2,3},{5,4},{6,7},{9,8},{10,11},{13,12},{14,15},{17,16},{18,... | collective-permute-start | bytes 1179656 | tf_op jit(solution)/shard_map/ppermute | solution.py:339
  436.4 239.8 %reduce-scatter.8.cloned.1.call-start = ((), (), s32[]{:S(2)}) async-start(), calls=%async_computation.10 | async-start | bytes 3538944 | tf_op jit(solution)/shard_map/reduce_scatter | solution.py:556
  442.1 236.0 %reduce-scatter.6.cloned.1.call-start = ((), (), s32[]{:S(2)}) async-start(), calls=%async_computation.9 | async-start | bytes 3538944 | tf_op jit(solution)/shard_map/reduce_scatter | solution.py:558
  448.4 231.7 %reduce-scatter.4.cloned.1.call-start = ((), (), s32[]{:S(2)}) async-start(), calls=%async_computation.8 | async-start | bytes 3538944 | tf_op jit(solution)/shard_map/reduce_scatter | solution.py:557
  486.5 41.4 %collective-permute-start.63 = (bf16[1024,768]{1,0:T(8,128)(2,1)}, bf16[1024,768]{1,0:T(8,128)(2,1)}, u32[]{:S(2)}, u32[]{:S(2)}) collective-permute-start(bf16[1024,768]{1,0:T(8,128)(2,1)} %get-tuple-element.56), channel_id=1, source_target_pairs={{0,4},{4,0},{8,12},{12,8},{16,20},{20,16},{24,28},{28,24},{1,5},{5... | collective-permute-start | bytes 4718600 | tf_op jit(solution)/shard_map/ppermute | solution.py:242
  530.5 24.1 %collective-permute-start.64 = (bf16[1024,768]{1,0:T(8,128)(2,1)S(1)}, bf16[1024,768]{1,0:T(8,128)(2,1)S(1)}, u32[]{:S(2)}, u32[]{:S(2)}) collective-permute-start(bf16[1024,768]{1,0:T(8,128)(2,1)S(1)} %add_convert_fusion), channel_id=1, source_target_pairs={{0,16},{4,12},{8,24},{12,4},{16,0},{20,28},{24,8},{28,20},{1,17},{... | collective-permute-start | bytes 4718600 | tf_op jit(solution)/shard_map/ppermute | solution.py:242
  533.3 21.5 %collective-permute-start.65 = (bf16[512,768]{1,0:T(8,128)(2,1)S(1)}, bf16[512,768]{1,0:T(8,128)(2,1)S(1)}, u32[]{:S(2)}, u32[]{:S(2)}) collective-permute-start(bf16[512,768]{1,0:T(8,128)(2,1)S(1)} %copy-done.147), channel_id=1, source_target_pairs={{0,4},{4,0},{8,12},{12,8},{16,20},{20,16},{24,28},{28,24},{1,5},{5... | collective-permute-start | bytes 2359304 | tf_op jit(solution)/shard_map/ppermute | solution.py:242
  533.4 27.8 %collective-permute-start.62 = (bf16[512,768]{1,0:T(8,128)(2,1)}, bf16[512,768]{1,0:T(8,128)(2,1)S(1)}, u32[]{:S(2)}, u32[]{:S(2)}) collective-permute-start(bf16[512,768]{1,0:T(8,128)(2,1)} %get-tuple-element.54), channel_id=1, source_target_pairs={{0,4},{4,0},{8,12},{12,8},{16,20},{20,16},{24,28},{28,24},{1,5},{5... | collective-permute-start | bytes 2359304 | tf_op jit(solution)/shard_map/ppermute | solution.py:242
  580.9 16.3 %collective-permute-start.79 = (f32[2,64]{1,0:T(2,128)S(1)}, f32[2,64]{1,0:T(2,128)S(1)}, u32[]{:S(2)}, u32[]{:S(2)}) collective-permute-start(f32[2,64]{1,0:T(2,128)S(1)} %pad_maximum_fusion.12), channel_id=1, source_target_pairs={{0,1},{1,0},{2,3},{3,2},{4,5},{5,4},{6,7},{7,6},{8,9},{9,8},{10,11... | collective-permute-start | bytes 1544 | tf_op jit(solution)/shard_map/ppermute | solution.py:242
  581.9 15.5 %collective-permute-start.67 = (bf16[128,1536]{1,0:T(8,128)(2,1)}, bf16[128,1536]{1,0:T(8,128)(2,1)S(1)}, u32[]{:S(2)}, u32[]{:S(2)}) collective-permute-start(bf16[128,1536]{1,0:T(8,128)(2,1)} %get-tuple-element.96), channel_id=1, source_target_pairs={{0,1},{3,2},{4,5},{7,6},{8,9},{11,10},{12,13},{15,14},{16,17},{19,... | collective-permute-start | bytes 1179656 | tf_op jit(solution)/shard_map/ppermute | solution.py:334
  601.9 15.3 %collective-permute-start.76 = (bf16[128,1536]{1,0:T(8,128)(2,1)S(1)}, bf16[128,1536]{1,0:T(8,128)(2,1)S(1)}, u32[]{:S(2)}, u32[]{:S(2)}) collective-permute-start(bf16[128,1536]{1,0:T(8,128)(2,1)S(1)} %get-tuple-element.61), channel_id=1, source_target_pairs={{0,1},{3,2},{4,5},{7,6},{8,9},{11,10},{12,13},{15,14},{16,17},{19,... | collective-permute-start | bytes 1179656 | tf_op jit(solution)/shard_map/ppermute | solution.py:334
  609.8 60.2 %collective-permute-start.84 = (bf16[4,192,1536]{2,1,0:T(8,128)(2,1)}, bf16[4,192,1536]{2,1,0:T(8,128)(2,1)}, u32[]{:S(2)}, u32[]{:S(2)}) collective-permute-start(bf16[4,192,1536]{2,1,0:T(8,128)(2,1)} %dynamic-slice_bitcast_fusion), channel_id=1, source_target_pairs={{0,4},{4,0},{8,12},{12,8},{16,20},{20,16},{24,28},{28,24},{1,5},{5... | collective-permute-start | bytes 7077896 | tf_op jit(solution)/shard_map/ppermute | solution.py:242
  609.9 18.2 %collective-permute-start.71 = (bf16[128,1536]{1,0:T(8,128)(2,1)S(1)}, bf16[128,1536]{1,0:T(8,128)(2,1)S(1)}, u32[]{:S(2)}, u32[]{:S(2)}) collective-permute-start(bf16[128,1536]{1,0:T(8,128)(2,1)S(1)} %get-tuple-element.95), channel_id=1, source_target_pairs={{1,2},{2,1},{5,6},{6,5},{9,10},{10,9},{13,14},{14,13},{17,18},{18,... | collective-permute-start | bytes 1179656 | tf_op jit(solution)/shard_map/ppermute | solution.py:337
  610.6 16.0 %collective-permute-start.68 = (bf16[128,1536]{1,0:T(8,128)(2,1)S(1)}, bf16[128,1536]{1,0:T(8,128)(2,1)S(1)}, u32[]{:S(2)}, u32[]{:S(2)}) collective-permute-start(bf16[128,1536]{1,0:T(8,128)(2,1)S(1)} %get-tuple-element.94), channel_id=1, source_target_pairs={{1,2},{2,1},{5,6},{6,5},{9,10},{10,9},{13,14},{14,13},{17,18},{18,... | collective-permute-start | bytes 1179656 | tf_op jit(solution)/shard_map/ppermute | solution.py:337
  626.7 16.3 %collective-permute-start.69 = (bf16[128,1536]{1,0:T(8,128)(2,1)S(1)}, bf16[128,1536]{1,0:T(8,128)(2,1)S(1)}, u32[]{:S(2)}, u32[]{:S(2)}) collective-permute-start(bf16[128,1536]{1,0:T(8,128)(2,1)S(1)} %add_convert_fusion.9), channel_id=1, source_target_pairs={{1,0},{2,3},{5,4},{6,7},{9,8},{10,11},{13,12},{14,15},{17,16},{18,... | collective-permute-start | bytes 1179656 | tf_op jit(solution)/shard_map/ppermute | solution.py:339
  628.2 23.2 %collective-permute-start.72 = (bf16[128,1536]{1,0:T(8,128)(2,1)S(1)}, bf16[128,1536]{1,0:T(8,128)(2,1)S(1)}, u32[]{:S(2)}, u32[]{:S(2)}) collective-permute-start(bf16[128,1536]{1,0:T(8,128)(2,1)S(1)} %add_convert_fusion.7), channel_id=1, source_target_pairs={{1,0},{2,3},{5,4},{6,7},{9,8},{10,11},{13,12},{14,15},{17,16},{18,... | collective-permute-start | bytes 1179656 | tf_op jit(solution)/shard_map/ppermute | solution.py:339
  629.6 30.2 %collective-permute-start.78 = (bf16[128,1536]{1,0:T(8,128)(2,1)S(1)}, bf16[128,1536]{1,0:T(8,128)(2,1)S(1)}, u32[]{:S(2)}, u32[]{:S(2)}) collective-permute-start(bf16[128,1536]{1,0:T(8,128)(2,1)S(1)} %add_convert_fusion.3), channel_id=1, source_target_pairs={{1,0},{2,3},{5,4},{6,7},{9,8},{10,11},{13,12},{14,15},{17,16},{18,... | collective-permute-start | bytes 1179656 | tf_op jit(solution)/shard_map/ppermute | solution.py:339
  631.2 35.8 %collective-permute-start.75 = (bf16[128,1536]{1,0:T(8,128)(2,1)S(1)}, bf16[128,1536]{1,0:T(8,128)(2,1)S(1)}, u32[]{:S(2)}, u32[]{:S(2)}) collective-permute-start(bf16[128,1536]{1,0:T(8,128)(2,1)S(1)} %add_convert_fusion.5), channel_id=1, source_target_pairs={{1,0},{2,3},{5,4},{6,7},{9,8},{10,11},{13,12},{14,15},{17,16},{18,... | collective-permute-start | bytes 1179656 | tf_op jit(solution)/shard_map/ppermute | solution.py:339
  675.2 16.5 %collective-permute-start.85 = (bf16[2,192,1536]{2,1,0:T(8,128)(2,1)}, bf16[2,192,1536]{2,1,0:T(8,128)(2,1)}, u32[]{:S(2)}, u32[]{:S(2)}) collective-permute-start(bf16[2,192,1536]{2,1,0:T(8,128)(2,1)} %pad_maximum_fusion.6), channel_id=1, source_target_pairs={{0,16},{4,12},{8,24},{12,4},{16,0},{20,28},{24,8},{28,20},{1,17},{... | collective-permute-start | bytes 3538952 | tf_op jit(solution)/shard_map/ppermute | solution.py:242
  (206 other events, 2629.1 us)
Sparse Core Ops, SparseCore 0:
  11.8 59.8 all-reduce.2
  73.6 34.2 all-gather.3
  109.7 32.6 all-gather.5
  161.7 30.4 all-gather.7
  436.5 53.3 all-reduce.4
  493.1 47.8 reduce-scatter.7
  544.7 46.3 reduce-scatter.5
  594.5 49.0 reduce-scatter.3

commit v2 on v1

v2 whole, which is shorter than its diff:
```python
import functools
import jax
import jax.numpy as jnp
from jax import lax
from jax.experimental import pallas as pl
from jax.experimental.pallas import tpu as pltpu
from jax.sharding import PartitionSpec as P

HD = 64
MASK = 8192.0
CHEAP = pl.CostEstimate(flops=1, bytes_accessed=1, transcendentals=0)
ATTEND_MIB = 60
BACK_MIB = 60
SMALL_MIB = 16


def dot(a, b):
    return lax.dot_general(a, b, (((1,), (0,)), ((), ())), preferred_element_type=jnp.float32)


def split3(v):
    hi = v.astype(jnp.bfloat16).astype(jnp.float32)
    mid = (v - hi).astype(jnp.bfloat16).astype(jnp.float32)
    return hi, mid, v - hi - mid


def bounds(info, base, clips, ids):
    start = jnp.full(ids.shape, 1 << 30, jnp.int32)
    end = jnp.zeros(ids.shape, jnp.int32)
    for c in range(clips):
        start = jnp.where(ids == c, info[base + c], start)
        end = jnp.where(ids == c, info[base + clips + c], end)
    return start, end


def query_ext(info, clips, width, scale):
    ids = lax.broadcasted_iota(jnp.int32, (16, width), 0)
    place = info[0] + lax.broadcasted_iota(jnp.int32, (16, width), 1)
    start, end = bounds(info, 1, clips, ids)
    return jnp.where((place >= start) & (place < end), scale, 0.0)


def key_ext(info, clips, row, rows, piece):
    ids = lax.broadcasted_iota(jnp.int32, (rows, 128), 1)
    step = min(rows, piece)
    parts = []
    for k in range(rows // step):
        at = row + k * step
        first = info[1 + 4 * clips + at // piece] + lax.rem(at, piece)
        parts.append(first + lax.broadcasted_iota(jnp.int32, (step, 128), 0))
    place = parts[0] if len(parts) == 1 else jnp.concatenate(parts, axis=0)
    start, end = bounds(info, 1 + 2 * clips, clips, ids)
    inside = (place >= start) & (place < end)
    value = jnp.where(ids < clips, jnp.where(inside, 0.0, -1.0), jnp.where(ids < clips + 3, 1.0, 0.0))
    return value.astype(jnp.bfloat16)


def fill_ext(dst, h, src, tail):
    width = src.shape[1]
    half = h % 2
    zero = jnp.zeros((HD, width), jnp.bfloat16)
    dst[h, half * HD : half * HD + HD, :] = src[h * HD : h * HD + HD, :]
    dst[h, (1 - half) * HD : (1 - half) * HD + HD, :] = zero
    dst[h, 128:144, :] = tail.astype(jnp.bfloat16)
    dst[h, 144:256, :] = jnp.zeros((112, width), jnp.bfloat16)


def stack_rows(heads, rows, clips, width):
    ids = lax.broadcasted_iota(jnp.int32, (16, width), 0)
    total = jnp.zeros((16, width), jnp.float32)
    for k, row in enumerate(rows):
        total = jnp.where(ids == clips + k, jnp.broadcast_to(row, (16, width)), total)
    return total


def load_pieces(pieces, kv, sem):
    rows = pieces[0].shape[0]
    return [
        pltpu.make_async_copy(piece, kv.at[pl.ds(k * rows, rows), :], sem.at[k])
        for k, piece in enumerate(pieces)
    ]


def fwd_kernel(heads, clips, count, tile, again, info, qt, *rest):
    before, pieces, (out, qx, kv, sem) = rest[:again], rest[again : again + count], rest[again + count :]
    copies = load_pieces(pieces, kv, sem)
    for c in copies:
        c.start()
    width = qt.shape[1]
    wide = qt.shape[0]
    ext = query_ext(info, clips, width, MASK)
    for h in range(heads):
        fill_ext(qx, h, qt, ext)
        out[h] = before[0][h] if again else jnp.zeros((80, width), jnp.float32)
    for c in copies:
        c.wait()
    steps = count * pieces[0].shape[0] // tile
    ones = jnp.ones((16, tile), jnp.bfloat16)

    def step(t, carry):
        rows = pl.ds(pl.multiple_of(t * tile, tile), tile)
        extra = key_ext(info, clips, t * tile, tile, pieces[0].shape[0])
        for p in range((heads + 1) // 2):
            kx = jnp.concatenate([kv[rows, p * 128 : p * 128 + 128], extra], axis=1)
            vt = kv[rows, wide + p * 128 : wide + p * 128 + 128].T
            for h in range(2 * p, min(2 * p + 2, heads)):
                half = h % 2
                probs = jnp.exp(dot(kx, qx[h])).astype(jnp.bfloat16)
                vx = jnp.concatenate([vt[half * HD : half * HD + HD, :], ones], axis=0)
                out[h] += dot(vx, probs)
        return carry

    lax.fori_loop(0, steps, step, 0)


def attend(info, qt, pieces, heads, clips, before=None, tile=1024):
    count = len(pieces)
    before = [] if before is None else [before]
    wide, width = qt.shape
    rows = pieces[0].shape[0]
    tile = min(tile, rows * count)
    return pl.pallas_call(
        functools.partial(fwd_kernel, heads, clips, count, tile, len(before)),
        out_shape=jax.ShapeDtypeStruct((heads, 80, width), jnp.float32),
        in_specs=[pl.BlockSpec(memory_space=pltpu.SMEM)]
        + [pl.BlockSpec(memory_space=pltpu.VMEM)] * (1 + len(before))
        + [pl.BlockSpec(memory_space=pltpu.HBM)] * count,
        out_specs=pl.BlockSpec(memory_space=pltpu.VMEM),
        scratch_shapes=[
            pltpu.VMEM((heads, 256, width), jnp.bfloat16),
            pltpu.VMEM((count * rows, 2 * wide), jnp.bfloat16),
            pltpu.SemaphoreType.DMA((count,)),
        ],
        compiler_params=pltpu.CompilerParams(vmem_limit_bytes=ATTEND_MIB << 20),
        cost_estimate=CHEAP,
        name="attend",
    )(info, qt, *before, *pieces)


def bwd_kernel(heads, clips, count, tile, again, info, qt, dot_t, q_tok, do_tok, lse, delta, *rest):
    before, pieces, rest = rest[:again], rest[again : again + count], rest[again + count :]
    dqt, kdot, grads, (qx, dox, qpad, dopad, kv, sem) = rest[0], rest[1], rest[2:-6], rest[-6:]
    copies = load_pieces(pieces, kv, sem)
    for c in copies:
        c.start()
    wide, width = qt.shape
    ext = query_ext(info, clips, width, MASK)
    for h in range(heads):
        p, half = h // 2, h % 2
        fill_ext(qx, h, qt, ext - stack_rows(heads, split3(lse[h : h + 1, :]), clips, width))
        fill_ext(dox, h, dot_t, -stack_rows(heads, split3(delta[h : h + 1, :]), clips, width))
        lane = lax.broadcasted_iota(jnp.int32, (width, 128), 1) // HD
        zero = jnp.zeros((width, 128), jnp.bfloat16)
        qpad[h] = jnp.where(lane == half, q_tok[:, p * 128 : p * 128 + 128], zero)
        dopad[h] = jnp.where(lane == half, do_tok[:, p * 128 : p * 128 + 128], zero)
    kdot[...] = jnp.zeros((1, 128), jnp.float32)
    dqt[...] = before[0][...] if again else jnp.zeros((wide, width), jnp.float32)
    for c in copies:
        c.wait()
    steps = count * pieces[0].shape[0] // tile

    def step(t, carry):
        rows = pl.ds(pl.multiple_of(t * tile, tile), tile)
        extra = key_ext(info, clips, t * tile, tile, pieces[0].shape[0])
        for p in range((heads + 1) // 2):
            cols = slice(p * 128, p * 128 + 128)
            vcols = slice(wide + p * 128, wide + p * 128 + 128)
            k_tile = kv[rows, cols]
            kx = jnp.concatenate([k_tile, extra], axis=1)
            vx = jnp.concatenate([kv[rows, vcols], extra], axis=1)
            kt = k_tile.T
            dk = jnp.zeros((tile, 128), jnp.float32)
            dv = jnp.zeros((tile, 128), jnp.float32)
            for h in range(2 * p, min(2 * p + 2, heads)):
                half = h % 2
                probs = jnp.exp(dot(kx, qx[h]))
                ds = (probs * dot(vx, dox[h])).astype(jnp.bfloat16)
                dqt[h * HD : h * HD + HD, :] += dot(kt[half * HD : half * HD + HD, :], ds)
                dk = dk + dot(ds, qpad[h])
                dv = dv + dot(probs.astype(jnp.bfloat16), dopad[h])
            kdot[...] += jnp.sum(dk * k_tile.astype(jnp.float32), axis=0, keepdims=True)
            for g, grad in enumerate(grads):

                @pl.when(t // (steps // len(grads)) == g)
                def store(g=g, grad=grad, dk=dk, dv=dv, cols=cols, vcols=vcols):
                    start = (t - g * (steps // len(grads))) * tile
                    here = pl.ds(pl.multiple_of(start, tile), tile)
                    grad[here, cols] = dk.astype(grad.dtype)
                    grad[here, vcols] = dv.astype(grad.dtype)

        return carry

    lax.fori_loop(0, steps, step, 0)


def attend_back(info, qt, dot_t, q_tok, do_tok, lse, delta, pieces, heads, clips, kind, parts=1, before=None, tile=1024):
    count = len(pieces)
    before = [] if before is None else [before]
    wide, width = qt.shape
    rows = pieces[0].shape[0]
    tile = min(tile, rows * count // parts)
    return pl.pallas_call(
        functools.partial(bwd_kernel, heads, clips, count, tile, len(before)),
        out_shape=(
            jax.ShapeDtypeStruct((wide, width), jnp.float32),
            jax.ShapeDtypeStruct((1, 128), jnp.float32),
        )
        + (jax.ShapeDtypeStruct((count * rows // parts, 2 * wide), kind),) * parts,
        in_specs=[pl.BlockSpec(memory_space=pltpu.SMEM)]
        + [pl.BlockSpec(memory_space=pltpu.VMEM)] * (6 + len(before))
        + [pl.BlockSpec(memory_space=pltpu.HBM)] * count,
        out_specs=(pl.BlockSpec(memory_space=pltpu.VMEM),) * (2 + parts),
        scratch_shapes=[
            pltpu.VMEM((heads, 256, width), jnp.bfloat16),
            pltpu.VMEM((heads, 256, width), jnp.bfloat16),
            pltpu.VMEM((heads, width, 128), jnp.bfloat16),
            pltpu.VMEM((heads, width, 128), jnp.bfloat16),
            pltpu.VMEM((count * rows, 2 * wide), jnp.bfloat16),
            pltpu.SemaphoreType.DMA((count,)),
        ],
        compiler_params=pltpu.CompilerParams(vmem_limit_bytes=BACK_MIB << 20),
        cost_estimate=CHEAP,
        name="attend_back",
    )(info, qt, dot_t, q_tok, do_tok, lse, delta, *before, *pieces)


ROWS = (((1,), (1,)), ((), ()))
COLS = (((0,), (0,)), ((), ()))
f32 = jnp.float32
bf16 = jnp.bfloat16


def matmul(left, right, dims=None):
    if dims is None:
        return jnp.dot(left, right, preferred_element_type=f32)
    return lax.dot_general(left, right, dims, preferred_element_type=f32)


def first_way(i):
    return i ^ 2 if i % 2 == 0 else i ^ 4


def other_way(i):
    return i ^ 4 if i % 2 == 0 else i ^ 2


def swap(value, axis, count, to):
    return lax.ppermute(value, axis, [(i, to(i)) for i in range(count)])


def seq_roles(seq_index, seq_count):
    if seq_count != 8:
        return jnp.arange(seq_count, dtype=jnp.int32)
    peer = seq_index ^ 1

    def roles(i):
        even = i % 2 == 0
        return [i, jnp.where(even, i ^ 2, i ^ 4), jnp.where(even, i ^ 4, i ^ 2), i ^ 6]

    return jnp.stack(roles(seq_index) + roles(peer)).astype(jnp.int32)


def gather_pieces(block, seq_count):
    if seq_count != 8:
        whole = lax.all_gather(block, "seq", axis=0, tiled=False)
        return [whole[i] for i in range(seq_count)]
    near = swap(block, "seq", 8, first_way)
    next_ = swap(block, "seq", 8, other_way)
    far = swap(near, "seq", 8, other_way)
    mine = [block, near, next_, far]
    return mine + [swap(v, "seq", 8, lambda i: i ^ 1) for v in mine]


def place_kernel(count, rows, widths, roles, *rest):
    pieces, outs, sem = rest[:count], rest[count:-1], rest[-1]
    copies = []
    for k in range(count):
        to = pl.ds(pl.multiple_of(roles[k] * rows, rows), rows)
        first = 0
        for n, width in enumerate(widths):
            piece = pieces[k].at[:, first : first + width]
            copies.append(pltpu.make_async_copy(piece, outs[n].at[to, :], sem.at[k, n]))
            first += width
    for c in copies:
        c.start()
    for c in copies:
        c.wait()


def place(pieces, roles, widths=None, limit=SMALL_MIB):
    count = len(pieces)
    rows, width = pieces[0].shape
    outs = widths or (width,)
    placed = pl.pallas_call(
        functools.partial(place_kernel, count, rows, outs),
        out_shape=[jax.ShapeDtypeStruct((count * rows, w), pieces[0].dtype) for w in outs],
        in_specs=[pl.BlockSpec(memory_space=pltpu.SMEM)]
        + [pl.BlockSpec(memory_space=pltpu.HBM)] * count,
        out_specs=[pl.BlockSpec(memory_space=pltpu.VMEM)] * len(outs),
        scratch_shapes=[pltpu.SemaphoreType.DMA((count, len(outs)))],
        compiler_params=pltpu.CompilerParams(vmem_limit_bytes=limit << 20),
        cost_estimate=CHEAP,
        name="place",
    )(roles, *pieces)
    return placed if widths else placed[0]


def scatter_start(part, seq_index):
    blocks = part.reshape(4, 2, part.shape[0] // 8, part.shape[1])
    theirs = lax.dynamic_index_in_dim(blocks, 1 - seq_index % 2, 1, False)
    return part, swap(theirs, "seq", 8, lambda i: i ^ 1)


def scatter_first(pair, seq_index):
    part, got = pair
    blocks = part.reshape(4, 2, part.shape[0] // 8, part.shape[1])
    mine = add_low(lax.dynamic_index_in_dim(blocks, seq_index % 2, 1, False), got)
    chip = seq_index // 2
    next_ = jnp.where(seq_index % 2 == 0, chip ^ 2, chip ^ 1)
    pick = lambda c: lax.dynamic_index_in_dim(mine, c, 0, False)
    return mine, swap(jnp.stack([pick(chip ^ 3), pick(next_)]), "seq", 8, other_way)


def scatter_second(pair, seq_index):
    mine, got = pair
    chip = seq_index // 2
    near = jnp.where(seq_index % 2 == 0, chip ^ 1, chip ^ 2)
    pick = lambda c: lax.dynamic_index_in_dim(mine, c, 0, False)
    return add_low(pick(chip), got[1]), swap(add_low(pick(near), got[0]), "seq", 8, first_way)


def scatter_last(pair):
    return pair[0].astype(f32) + pair[1].astype(f32)


def scatter_sum(part, seq_index, seq_count):
    if seq_count != 8:
        return lax.psum_scatter(part, "seq", scatter_dimension=0, tiled=True).astype(f32)
    pair = scatter_first(scatter_start(part, seq_index), seq_index)
    return scatter_last(scatter_second(pair, seq_index))


def hops(axis, count):
    return [(axis, 1 << k) for k in range(count.bit_length() - 1)]


def sum_all(value, axes, order, beside=()):
    if any(count & (count - 1) for _, count in axes):
        return lax.psum(value, [axis for axis, _ in axes]), list(beside)
    counts, beside = dict(axes), list(beside)
    for k, (axis, bit) in enumerate(order):
        got = swap(value, axis, counts[axis], lambda i: i ^ bit)
        if k < len(beside):
            got, beside[k] = lax.optimization_barrier((got, beside[k]))
        value = value + got
    return value, beside


def add_low(a, b):
    return (a.astype(f32) + b.astype(f32)).astype(bf16)


def relay_kernel(names, end, *refs):
    ins = dict(zip(names, refs))
    outs = list(refs[len(names) :])
    add = lambda a, b: (ins[a][...].astype(f32) + ins[b][...].astype(f32)).astype(bf16)
    if "part" in ins:
        outs.pop(0)[...] = add("part", "part_got")
    if "total" in ins:
        total = add("total", "total_got")
        outs.pop(0)[...] = total
        if "own" in ins:
            send = outs.pop(0)
            rows, own_rows = total.shape[0], ins["own"].shape[0]
            both = min(rows, own_rows)
            send[:both, :] = jnp.where(end[0] == 1, ins["own"][:both, :], total[:both, :])
            if own_rows > both:
                send[both:, :] = ins["own"][both:, :]
            if rows > both:
                send[both:, :] = total[both:, :]


def relay(end, part, total, own):
    ins = {}
    shapes = []
    if part is not None:
        ins.update(part=part[0], part_got=part[1])
        shapes.append(part[0].shape)
    if total is not None:
        ins.update(total=total[0], total_got=total[1])
        shapes.append(total[0].shape)
        if own is not None:
            ins["own"] = own
            shapes.append((max(own.shape[0], total[0].shape[0]), own.shape[1]))
    if not shapes:
        return None, None, own
    outs = pl.pallas_call(
        functools.partial(relay_kernel, tuple(ins)),
        out_shape=[jax.ShapeDtypeStruct(shape, bf16) for shape in shapes],
        in_specs=[pl.BlockSpec(memory_space=pltpu.SMEM)] + [pl.BlockSpec(memory_space=pltpu.VMEM)] * len(ins),
        out_specs=[pl.BlockSpec(memory_space=pltpu.VMEM)] * len(shapes),
        compiler_params=pltpu.CompilerParams(vmem_limit_bytes=SMALL_MIB << 20),
        cost_estimate=CHEAP,
        name="relay",
    )(end, *ins.values())
    outs = list(outs)
    part = outs.pop(0) if part is not None else None
    total = outs.pop(0) if total is not None else None
    return part, total, outs.pop(0) if outs else own


def fused(kernel, outs, scalars, arrays, name, limit=40, **static):
    return pl.pallas_call(
        functools.partial(kernel, **static) if static else kernel,
        out_shape=[jax.ShapeDtypeStruct(shape, kind) for shape, kind in outs],
        in_specs=[pl.BlockSpec(memory_space=pltpu.SMEM)] * len(scalars)
        + [pl.BlockSpec() if limit == 60 else pl.BlockSpec(memory_space=pltpu.VMEM)] * len(arrays),
        out_specs=[pl.BlockSpec() if limit == 60 else pl.BlockSpec(memory_space=pltpu.VMEM)] * len(outs),
        compiler_params=pltpu.CompilerParams(vmem_limit_bytes=limit << 20),
        cost_estimate=CHEAP,
        name=name,
    )(*scalars, *arrays)


def rms(value):
    return lax.rsqrt(jnp.mean(value * value, axis=-1, keepdims=True) + 1e-06)


def rms_back(grad, normed, scale):
    return scale * (grad - normed * jnp.mean(grad * normed, axis=-1, keepdims=True))


def dot_rows(a, b):
    return lax.dot_general(a, b, ROWS, preferred_element_type=f32)


def picked(end, total, got):
    return jnp.where(end[0] == 1, got[...], total[...]).astype(f32)


def forward_kernel(
    end, total, got, x, gain_a, gain_in, gate_w, up_w, down_t, ra, na, mid, rm, act, gate, up, units, part
):
    attn = picked(end, total, got)
    scale = rms(attn)
    normed = attn * scale
    ra[...] = scale
    na[...] = normed
    middle = x[...].astype(f32) + normed * gain_a[...]
    mid[...] = middle
    scale = rms(middle)
    rm[...] = scale
    low = (middle * scale * gain_in[...]).astype(bf16)
    act[...] = low
    gated = dot(low, gate_w[...])
    upper = dot(low, up_w[...])
    gate[...] = gated
    up[...] = upper
    low = (gated * jax.nn.sigmoid(gated) * upper).astype(bf16)
    units[...] = low
    part[...] = dot_rows(low, down_t[...]).astype(bf16)


def backward_kernel(
    end, total, got, mid, cot, gate, up, gain_f, gate_w, up_w, down_t, out, uf, dffn, dgate, dup, part
):
    ffn = picked(end, total, got)
    scale = rms(ffn)
    normed = ffn * scale
    out[...] = (mid[...] + normed * gain_f[...]).astype(bf16)
    grad = cot[...].astype(f32)
    uf[...] = jnp.sum(grad * normed, axis=0, keepdims=True)
    low = rms_back(grad * gain_f[...], normed, scale).astype(bf16)
    dffn[...] = low
    grad_units = dot(low, down_t[...])
    gated = gate[...]
    sig = jax.nn.sigmoid(gated)
    low_gate = (grad_units * up[...] * sig * (1.0 + gated * (1.0 - sig))).astype(bf16)
    low_up = (grad_units * gated * sig).astype(bf16)
    dgate[...] = low_gate
    dup[...] = low_up
    part[...] = (dot_rows(low_gate, gate_w[...]) + dot_rows(low_up, up_w[...])).astype(bf16)


def attn_back_kernel(end, total, got, mid, rm, na, ra, cot, gain_in, gain_a, sf, ua, dmid, dattn):
    grad = picked(end, total, got)
    normed = mid[...] * rm[...]
    sf[...] = jnp.sum(grad * normed, axis=0, keepdims=True)
    middle = cot[...].astype(f32) + rms_back(grad * gain_in[...], normed, rm[...])
    dmid[...] = middle
    ua[...] = jnp.sum(middle * na[...], axis=0, keepdims=True)
    dattn[...] = rms_back(middle * gain_a[...], na[...], ra[...]).astype(bf16)


def weight_grad_kernel(*refs, count):
    left = jnp.concatenate([ref[...] for ref in refs[:count]], axis=0)
    right = jnp.concatenate([ref[...] for ref in refs[count : 2 * count]], axis=0)
    refs[2 * count][...] = lax.dot_general(left, right, COLS, preferred_element_type=f32).astype(bf16)


def weight_grad(left, right):
    shape = (left[0].shape[1], right[0].shape[1])
    return fused(weight_grad_kernel, [(shape, bf16)], [], [*left, *right], "weight_grad", 60, count=len(left))[0]


def run_ticks(parts, computes, head_index, head_count, fill):
    carry = []
    stages = 4 * len(computes)
    ticks = stages + len(parts) - 1
    if head_count != 4:
        for n, compute in enumerate(computes):
            sums = [lax.psum(part, "head") for part in parts]
            parts = [compute(k, jnp.zeros((1,), jnp.int32), part, part) for k, part in enumerate(sums)]
        for t in range(ticks):
            carry = fill[t](carry) if t in fill else carry
        return parts, carry
    end = jnp.where((head_index == 0) | (head_index == 3), 1, 0).astype(jnp.int32).reshape(1)
    states = [(part,) for part in parts]
    for t in range(ticks):
        at = {(t - k) % 4: k for k in range(len(parts)) if 0 <= t - k < stages}
        live = [k for k in range(len(parts)) if t - k < stages]
        own = states[at[0]][0] if 0 in at else None
        part, total, send = relay(
            end, states[at[1]] if 1 in at else None, states[at[2]] if 2 in at else None, own
        )
        if 1 in at:
            states[at[1]] = (part, lax.ppermute(part, "head", [(1, 2), (2, 1)]))
        if 0 in at and 2 in at:
            got = lax.ppermute(send, "head", [(0, 1), (3, 2), (1, 0), (2, 3)])
            states[at[0]] = (own, got[: own.shape[0]])
            states[at[2]] = (total, got[: total.shape[0]])
        elif 0 in at:
            states[at[0]] = (own, lax.ppermute(own, "head", [(0, 1), (3, 2)]))
        elif 2 in at:
            states[at[2]] = (total, lax.ppermute(total, "head", [(1, 0), (2, 3)]))
        if 3 in at:
            k = at[3]
            states[k] = (computes[(t - k) // 4](k, end, *states[k]),)
        if t in fill:
            carry = fill[t](carry)
        held, carry = lax.optimization_barrier(([states[k] for k in live], carry))
        for k, state in zip(live, held):
            states[k] = state
    return [state[0] for state in states], carry


def head_mean(value):
    row = lax.broadcasted_iota(jnp.int32, (128, 128), 0) // HD
    col = lax.broadcasted_iota(jnp.int32, (128, 128), 1) // HD
    ones = jnp.where(row == col, 1.0 / HD, 0.0).astype(bf16)
    hi, mid, lo = split3(value)
    return dot(hi.astype(bf16), ones) + dot(mid.astype(bf16), ones) + dot(lo.astype(bf16), ones)


def partner(value):
    lane = lax.broadcasted_iota(jnp.int32, value.shape, 1) % HD
    return jnp.where(lane < HD // 2, pltpu.roll(value, 128 - HD // 2, 1), pltpu.roll(value, HD // 2, 1))


def text_norm_kernel(pre, gain, out):
    wide = pre.shape[1] // 2
    for p in range(wide // 128):
        cols = slice(p * 128, p * 128 + 128)
        value = pre[:, cols]
        out[:, cols] = (value * lax.rsqrt(head_mean(value * value) + 1e-6) * gain[...]).astype(bf16)
    out[:, wide:] = pre[:, wide:].astype(bf16)


def text_norm(pre, gain):
    return pl.pallas_call(
        text_norm_kernel, out_shape=jax.ShapeDtypeStruct(pre.shape, bf16), name="text_norm", cost_estimate=CHEAP
    )(pre, gain)


def qkv_kernel(count, rows, wide, roles, x, gain, qgain, kgain, cos, sin, *rest):
    pieces, (act, scale, pre, kv, query, query_t, weight, sem) = rest[:count], rest[count:]
    copies = []
    for k in range(count):
        start = pl.multiple_of(roles[k] * rows, rows)
        copies.append(pltpu.make_async_copy(pieces[k], weight.at[pl.ds(start, rows), :], sem.at[k]))
    for c in copies:
        c.start()
    value = x[...].astype(f32)
    inverse = lax.rsqrt(jnp.mean(value * value, axis=-1, keepdims=True) + 1e-6)
    scale[...] = inverse
    act[...] = (value * inverse * gain[...]).astype(bf16)
    for c in copies:
        c.wait()
    pre[...] = dot(act[...], weight[:, : 2 * wide])
    kv[:, wide:] = dot(act[...], weight[:, 2 * wide :]).astype(bf16)
    for p in range(wide // 128):
        cols = slice(p * 128, p * 128 + 128)
        for which, out_gain in ((0, qgain), (1, kgain)):
            raw = pre[:, which * wide + p * 128 : which * wide + p * 128 + 128]
            raw = raw * lax.rsqrt(head_mean(raw * raw) + 1e-6) * out_gain[...]
            raw = raw * cos[...] + partner(raw) * sin[...]
            if which == 1:
                kv[:, cols] = raw.astype(bf16)
            else:
                raw = raw.astype(bf16).astype(f32) * HD**-0.5
                query[:, cols] = raw.astype(bf16)
                query_t[cols, :] = raw.T.astype(bf16)


def project(roles, x, gain, qgain, kgain, cos, sin, pieces, wide):
    count = len(pieces)
    rows = pieces[0].shape[0]
    tokens, width = x.shape
    shape = jax.ShapeDtypeStruct
    return pl.pallas_call(
        functools.partial(qkv_kernel, count, rows, wide),
        out_shape=(
            shape((tokens, width), bf16),
            shape((tokens, 1), f32),
            shape((tokens, 2 * wide), f32),
            shape((tokens, 2 * wide), bf16),
            shape((tokens, wide), bf16),
            shape((wide, tokens), bf16),
            shape((width, 3 * wide), bf16),
        ),
        in_specs=[pl.BlockSpec(memory_space=pltpu.SMEM)]
        + [pl.BlockSpec(memory_space=pltpu.VMEM)] * 6
        + [pl.BlockSpec(memory_space=pltpu.HBM)] * count,
        out_specs=(pl.BlockSpec(memory_space=pltpu.VMEM),) * 7,
        scratch_shapes=[pltpu.SemaphoreType.DMA((count,))],
        compiler_params=pltpu.CompilerParams(vmem_limit_bytes=24 << 20),
        cost_estimate=CHEAP,
        name="project",
    )(roles, x, gain, qgain, kgain, cos, sin, *pieces)


def mix_kernel(heads, gate, sums, cross, mixed, self_t, cross_t, lse, cross_lse):
    for p in range((heads + 1) // 2):
        both = []
        for h in range(2 * p, 2 * p + 2):
            if h >= heads:
                both.append(jnp.zeros_like(both[0]))
                continue
            rows = slice(h * HD, h * HD + HD)
            den, cross_den = sums[h, HD : HD + 1, :], cross[h, HD : HD + 1, :]
            lse[h : h + 1, :] = jnp.log(den)
            cross_lse[h : h + 1, :] = jnp.log(cross_den)
            own = sums[h, :HD, :] / den
            other = cross[h, :HD, :] / cross_den
            self_t[rows, :] = own
            cross_t[rows, :] = other
            both.append(own + gate[h] * other)
        mixed[:, p * 128 : p * 128 + 128] = jnp.concatenate(both, axis=0).T.astype(bf16)


def mix(gate, sums, cross, wide):
    heads, _, tokens = sums.shape
    shape = jax.ShapeDtypeStruct
    return pl.pallas_call(
        functools.partial(mix_kernel, heads),
        out_shape=(
            shape((tokens, wide), bf16),
            shape((heads * HD, tokens), f32),
            shape((heads * HD, tokens), f32),
            shape((heads, tokens), f32),
            shape((heads, tokens), f32),
        ),
        in_specs=[pl.BlockSpec(memory_space=pltpu.SMEM)] + [pl.BlockSpec(memory_space=pltpu.VMEM)] * 2,
        compiler_params=pltpu.CompilerParams(vmem_limit_bytes=SMALL_MIB << 20),
        name="mix",
        cost_estimate=CHEAP,
    )(gate, sums, cross)


def unmix_kernel(heads, count, gate, weight, self_t, cross_t, *rest):
    chunks, (tok, tok_t, ctok, ctok_t, delta, cdelta, cgate) = rest[:count], rest[count:]
    width = tok.shape[0]
    for p in range((heads + 1) // 2):
        cols = slice(p * 128, p * 128 + 128)
        value = jnp.concatenate([dot(grad[...], weight[:, cols]) for grad in chunks], axis=0)
        lane = lax.broadcasted_iota(jnp.int32, (width, 128), 1) // HD
        gates = jnp.where(lane == 0, gate[2 * p], gate[min(2 * p + 1, heads - 1)])
        tok[:, cols] = value.astype(bf16)
        ctok[:, cols] = (value * gates).astype(bf16)
        turned = value.T
        for h in range(2 * p, 2 * p + 2):
            rows = slice(h * HD, h * HD + HD)
            part = turned[(h % 2) * HD : (h % 2) * HD + HD, :]
            tok_t[rows, :] = part.astype(bf16)
            if h >= heads:
                ctok_t[rows, :] = part.astype(bf16)
                continue
            low = (part * gate[h]).astype(bf16)
            ctok_t[rows, :] = low
            delta[h : h + 1, :] = jnp.sum(part.astype(bf16).astype(f32) * self_t[rows, :], axis=0, keepdims=True)
            cdelta[h : h + 1, :] = jnp.sum(low.astype(f32) * cross_t[rows, :], axis=0, keepdims=True)
            cgate[h : h + 1, :] = jnp.sum(part * cross_t[rows, :], axis=0, keepdims=True)


def unmix(gate, chunks, weight, self_t, cross_t):
    tokens = self_t.shape[1]
    wide = weight.shape[1]
    heads = self_t.shape[0] // HD
    shape = jax.ShapeDtypeStruct
    return pl.pallas_call(
        functools.partial(unmix_kernel, heads, len(chunks)),
        out_shape=(shape((tokens, wide), bf16), shape((wide, tokens), bf16)) * 2 + (shape((heads, tokens), f32),) * 3,
        in_specs=[pl.BlockSpec(memory_space=pltpu.SMEM)]
        + [pl.BlockSpec(memory_space=pltpu.VMEM)] * (3 + len(chunks)),
        compiler_params=pltpu.CompilerParams(vmem_limit_bytes=SMALL_MIB << 20),
        name="unmix",
        cost_estimate=CHEAP,
    )(gate, weight, self_t, cross_t, *chunks)


def norm_back(raw, gain, grad, cos=None, sin=None):
    scale = lax.rsqrt(head_mean(raw * raw) + 1e-6)
    normed = raw * scale
    if cos is not None:
        grad = grad * cos - partner(grad) * sin
    gain_grad = jnp.sum(grad * normed, axis=0, keepdims=True)
    grad = grad * gain
    return scale * (grad - normed * head_mean(grad * normed)), gain_grad


def text_back_kernel(pre, gain, grad, out):
    wide = pre.shape[1] // 2
    for p in range(wide // 128):
        cols = slice(p * 128, p * 128 + 128)
        out[:, cols] = norm_back(pre[:, cols], gain[...], grad[:, cols])[0].astype(bf16)
    out[:, wide:] = grad[:, wide:].astype(bf16)


def text_back(pre, gain, grad):
    return pl.pallas_call(
        text_back_kernel,
        out_shape=jax.ShapeDtypeStruct(grad.shape, bf16),
        name="text_back",
        cost_estimate=CHEAP,
    )(pre, gain, grad)


def project_back_kernel(wide, starts, pre, qgain, kgain, cos, sin, dqt, *rest):
    kvs, (out, qgrad, kgrad) = rest[: len(starts)], rest[len(starts) :]
    tokens = pre.shape[0]
    total = [jnp.zeros((1, 128), f32), jnp.zeros((1, 128), f32)]
    summed = lambda cols: sum(kv[start : start + tokens, cols].astype(f32) for kv, start in zip(kvs, starts))
    for p in range(wide // 128):
        cols = slice(p * 128, p * 128 + 128)
        grads = (dqt[cols, :] * HD**-0.5).T, summed(cols)
        for which, gain in ((0, qgain), (1, kgain)):
            at = slice(which * wide + p * 128, which * wide + p * 128 + 128)
            value, extra = norm_back(pre[:, at], gain[...], grads[which], cos[...], sin[...])
            out[:, at] = value.astype(bf16)
            total[which] = total[which] + extra
    out[:, 2 * wide :] = summed(slice(wide, 2 * wide)).astype(bf16)
    qgrad[...] = total[0]
    kgrad[...] = total[1]


def project_back(pre, qgain, kgain, cos, sin, dqt, kvs, starts):
    tokens, wide = pre.shape[0], pre.shape[1] // 2
    shape = jax.ShapeDtypeStruct
    return pl.pallas_call(
        functools.partial(project_back_kernel, wide, tuple(starts)),
        out_shape=(shape((tokens, 3 * wide), bf16), shape((1, 128), f32), shape((1, 128), f32)),
        name="project_back",
        cost_estimate=CHEAP,
        compiler_params=pltpu.CompilerParams(vmem_limit_bytes=60 << 20),
    )(pre, qgain, kgain, cos, sin, dqt, *kvs)


def finish_kernel(count, x, scale, gain, *rest):
    grads, mids, out = rest[:count], rest[count : 2 * count], rest[2 * count]
    rows = grads[0].shape[0]
    for k in range(count):
        at = slice(k * rows, k * rows + rows)
        inverse = scale[at, :]
        normed = x[at, :].astype(f32) * inverse
        grad = grads[k][...].astype(f32) * gain[...]
        mean = jnp.mean(grad * normed, axis=-1, keepdims=True)
        out[at, :] = mids[k][...] + inverse * (grad - normed * mean)


def finish(grads, mids, x, scale, gain):
    return pl.pallas_call(
        functools.partial(finish_kernel, len(grads)),
        out_shape=jax.ShapeDtypeStruct(x.shape, f32),
        name="finish",
        cost_estimate=CHEAP,
        compiler_params=pltpu.CompilerParams(vmem_limit_bytes=60 << 20),
    )(x, scale, gain, *grads, *mids)


def per_device(
    seq_count,
    head_count,
    hidden_in,
    cond,
    captions,
    clip_lengths,
    ada_weight,
    norm_gains,
    qk_gains,
    w_query,
    w_key,
    w_value,
    w_out,
    cross_gate,
    w_text_key,
    w_text_value,
    w_gate,
    w_up,
    w_down,
    out_cotangent,
):
    local_rows, model_width = hidden_in.shape
    seq_index = lax.axis_index("seq")
    head_index = lax.axis_index("head")
    clips = clip_lengths.shape[0]
    cols = w_query.shape[1]
    heads = cols // HD
    wide = (cols + 127) // 128 * 128
    units = w_gate.shape[1]
    roles = seq_roles(seq_index, seq_count)
    pad = lambda v: jnp.pad(v, ((0, 0), (0, wide - cols))) if wide > cols else v
    cut = lambda v: v[:, :cols]

    spread = seq_count == 8
    core = lambda v: swap(v, "seq", 8, lambda i: i ^ 1)
    hold = lax.optimization_barrier
    axes = (("seq", seq_count), ("head", head_count))
    seq_hops, head_hops = hops("seq", seq_count), hops("head", head_count)
    finish_sum = lambda v: lax.psum_scatter(v, "seq", scatter_dimension=0, tiled=True)

    def hop(value, steps):
        for axis, bit in steps:
            value = value + swap(value, axis, dict(axes)[axis], lambda i: i ^ bit)
        return value

    clip_ends = jnp.cumsum(clip_lengths, dtype=jnp.int32)
    starts = clip_ends - clip_lengths
    text_rows = captions.reshape(-1, captions.shape[2])
    text_block = text_rows.shape[0] // seq_count
    text_ids = jnp.arange(clips, dtype=jnp.int32) * captions.shape[1]
    first_row = seq_index * local_rows
    place_info = jnp.concatenate([first_row[None], starts, clip_ends]).astype(jnp.int32)
    text_info = jnp.concatenate(
        [place_info, text_ids, text_ids + captions.shape[1], jnp.zeros((1,), jnp.int32)]
    )

    def self_info(which):
        return jnp.concatenate([place_info, starts, clip_ends, roles[which] * local_rows])

    places = first_row + jnp.arange(local_rows, dtype=jnp.int32)
    inside = (places[:, None] >= starts[None, :]) & (places[:, None] < clip_ends[None, :])
    position = places - jnp.sum(jnp.where(inside, starts[None, :], 0), axis=1, dtype=jnp.int32)
    lane = jnp.arange(128)
    frequency = 10000.0 ** (-(lane % (HD // 2)).astype(f32) / (HD // 2))
    angles = position.astype(f32)[:, None] * frequency[None, :]
    cos = jnp.cos(angles)
    sin = jnp.where(lane % HD < HD // 2, -1.0, 1.0)[None, :] * jnp.sin(angles)
    query_gain = jnp.tile(qk_gains[0], 2)[None, :]
    key_gain = jnp.tile(qk_gains[1], 2)[None, :]

    cond_act = jax.nn.silu(cond).astype(bf16)
    piece_width = ada_weight.shape[1]
    mod_piece = matmul(cond_act[None, :], ada_weight)
    mine = lax.broadcasted_iota(jnp.int32, (seq_count * head_count, 1), 0) == seq_index * head_count + head_index
    modulation = jnp.where(mine, mod_piece, 0.0)
    modulation, w_query = hold((modulation, w_query))
    qkv_block = jnp.concatenate([pad(w_query), pad(w_key), pad(w_value)], axis=1)
    out_block = pad(w_out.T)
    slab_width = text_rows.shape[1] // seq_count
    if spread:
        modulation = hop(modulation, seq_hops[:1])
        modulation, text_rows = hold((modulation, text_rows))
    own_text = lax.dynamic_slice_in_dim(text_rows, seq_index * slab_width, slab_width, 1)
    text_part = matmul(own_text, jnp.concatenate([pad(w_text_key), pad(w_text_value)], axis=1)).astype(bf16)

    def queries_keys(modulation, pieces):
        gain = norm_gains[0] * (1.0 + modulation.reshape(4, model_width)[0])
        return project(roles, hidden_in, gain[None, :], query_gain, key_gain, cos, sin, pieces, wide)

    def part_sums(group, blocks, before=None):
        return attend(self_info(jnp.array(group)), query_t, blocks, heads, clips, before)

    if spread:
        near = swap(qkv_block, "seq", 8, first_way)
        next_ = swap(qkv_block, "seq", 8, other_way)
        modulation = hop(modulation, head_hops[:1])
        text_pre = lax.psum(text_part, "seq")
        gate_w = lax.all_gather(w_gate, "seq", axis=0, tiled=True)
        near, next_, modulation = hold((near, next_, modulation))
        far = swap(near, "seq", 8, other_way)
        modulation = hop(modulation, head_hops[1:])
        modulation = hop(modulation, seq_hops[1:])
        qkv_pieces = [qkv_block, near, next_, far]
        qkv_pieces = qkv_pieces + [core(v) for v in qkv_pieces]
        modulation, qkv_pieces, out_block = hold((modulation, qkv_pieces, out_block))
        act_a, x_scale, pre, kv_own, queries, query_t, w_qkv = queries_keys(modulation, qkv_pieces)
        kv_own, modulation, out_block = hold((kv_own, modulation, out_block))
        near = swap(kv_own, "seq", 8, first_way)
        next_ = swap(kv_own, "seq", 8, other_way)
        kv_peer = core(kv_own)
        out_near = swap(out_block, "seq", 8, first_way)
        out_next = swap(out_block, "seq", 8, other_way)
        sums = part_sums((0, 4), [kv_own, kv_peer])
        near, next_, sums, out_near, out_next = hold((near, next_, sums, out_near, out_next))
        far = swap(near, "seq", 8, other_way)
        out_far = swap(out_near, "seq", 8, other_way)
        near_peer, next_peer = core(near), core(next_)
        out_peers = [core(out_block), core(out_near), core(out_next)]
        sums = part_sums((1, 2, 5, 6), [near, next_, near_peer, next_peer], sums)
        ud_block = jnp.concatenate([w_up, w_down.T], axis=1)
        far, sums, out_far, text_pre, ud_block = hold((far, sums, out_far, text_pre, ud_block))
        far_peer = core(far)
        ud_near = swap(ud_block, "seq", 8, first_way)
        ud_next = swap(ud_block, "seq", 8, other_way)
        out_t = place([out_block, out_near, out_next, out_far] + out_peers + [core(out_far)], roles)
        text_pre = text_pre.astype(f32)
        text_pieces = [text_norm(text_pre, key_gain)]
        cross_sums = attend(text_info, query_t, text_pieces, heads, clips)
        sums = part_sums((3, 7), [far, far_peer], sums)
        pieces = [kv_own, near, next_, far, kv_peer, near_peer, next_peer, far_peer]
    else:
        modulation = lax.psum(modulation, ("seq", "head"))
        text_pre = lax.psum(text_part, "seq").astype(f32)
        qkv_pieces = gather_pieces(qkv_block, seq_count)
        act_a, x_scale, pre, kv_own, queries, query_t, w_qkv = queries_keys(modulation, qkv_pieces)
        pieces = gather_pieces(kv_own, seq_count)
        text_pieces = [text_norm(text_pre, key_gain)]
        out_t = place(gather_pieces(out_block, seq_count), roles)
        sums = part_sums(tuple(range(seq_count)), pieces)
        cross_sums = attend(text_info, query_t, text_pieces, heads, clips)
        gate_w = lax.all_gather(w_gate, "seq", axis=0, tiled=True)
    scale_a, gate_a, scale_f, gate_f = jnp.split(modulation.reshape(-1), 4)
    gain_x = norm_gains[0] * (1.0 + scale_a)
    gate_local = jnp.tanh(cross_gate)
    mixed, self_t, cross_t, self_lse, cross_lse = mix(gate_local, sums, cross_sums, wide)
    attn_part = matmul(mixed, out_t, ROWS).astype(bf16)

    late = {}

    def split_weights(pieces):
        return place(pieces, roles, (units, units), 53)

    def fill_far(carry):
        far = swap(ud_near, "seq", 8, other_way)
        return [ud_near, ud_next, far, core(ud_block), core(ud_near), core(ud_next)]

    def fill_weights(carry):
        return [split_weights([ud_block] + carry + [core(carry[2])])]

    def fill_ready(carry):
        late["up"], late["down"] = carry[0]
        return []

    if not spread:
        weights = gather_pieces(jnp.concatenate([w_up, w_down.T], axis=1), seq_count)
        late["up"], late["down"] = split_weights(weights)
    chunk_count = 4
    chunk = local_rows // chunk_count
    rows_of = lambda v, k: v[k * chunk : (k + 1) * chunk]
    tanh_a, tanh_f = jnp.tanh(gate_a), jnp.tanh(gate_f)
    gain_a = tanh_a * norm_gains[1]
    gain_in = norm_gains[2] * (1.0 + scale_f)
    gain_f = tanh_f * norm_gains[3]
    kept = [{} for _ in range(chunk_count)]

    row = lambda v: v[None, :]

    def save(k, names, values):
        kept[k].update(zip(names, values))
        return values[-1]

    def feed_forward(k, end, total, got):
        tall, one, thin = (chunk, model_width), (chunk, 1), (chunk, units)
        outs = [(one, f32), (tall, f32), (tall, f32), (one, f32), (tall, bf16)]
        outs = outs + [(thin, f32), (thin, f32), (thin, bf16), (tall, bf16)]
        arrays = [total, got, rows_of(hidden_in, k), row(gain_a), row(gain_in), gate_w, late["up"], late["down"]]
        names = ["ra", "na", "mid", "rm", "act", "gate", "up", "units", "part"]
        return save(k, names, fused(forward_kernel, outs, [end], arrays, "feed_forward"))

    def feed_back(k, end, total, got):
        keep = kept[k]
        tall, thin = (chunk, model_width), (chunk, units)
        outs = [(tall, bf16), ((1, model_width), f32), (tall, bf16), (thin, bf16), (thin, bf16), (tall, bf16)]
        arrays = [total, got, keep["mid"], rows_of(out_cotangent, k), keep["gate"], keep["up"], row(gain_f)]
        arrays = arrays + [gate_w, late["up"], late["down"]]
        names = ["out", "uf", "dffn", "dgate", "dup", "part"]
        return save(k, names, fused(backward_kernel, outs, [end], arrays, "feed_back"))

    def attn_back(k, end, total, got):
        keep = kept[k]
        tall, line = (chunk, model_width), (1, model_width)
        outs = [(line, f32), (line, f32), (tall, f32), (tall, bf16)]
        arrays = [total, got, keep["mid"], keep["rm"], keep["na"], keep["ra"], rows_of(out_cotangent, k)]
        arrays = arrays + [row(gain_in), row(gain_a)]
        return save(k, ["sf", "ua", "dmid", "dattn"], fused(attn_back_kernel, outs, [end], arrays, "attn_back", 60))

    rows_all = lambda name: jnp.concatenate([keep[name] for keep in kept], axis=0)
    chunks_of = lambda name: [keep[name] for keep in kept]
    vec = lambda name: sum(keep[name][0] for keep in kept)
    def fill_down(carry):
        return [weight_grad(chunks_of("dffn"), chunks_of("units"))]

    def fill_gate(carry):
        low, carry = hold((chunks_of("dgate"), carry))
        down = scatter_start(carry[0], seq_index) if spread else carry[0]
        return [down, weight_grad(chunks_of("act"), low)]

    def fill_up(carry):
        late["gate_sum"] = finish_sum(carry[1])
        low, down = hold((chunks_of("dup"), carry[0]))
        down = scatter_first(down, seq_index) if spread else down
        return [down, weight_grad(chunks_of("act"), low)]

    def fill_last(carry):
        late["up_sum"] = finish_sum(carry[1])
        return [scatter_second(carry[0], seq_index) if spread else carry[0]]

    fills = {8 + chunk_count - 1: fill_down, 8 + chunk_count: fill_gate, 8 + chunk_count + 1: fill_up, 8 + chunk_count + 2: fill_last}
    first_parts = [rows_of(attn_part, k) for k in range(chunk_count)]
    if spread:
        fills.update({0: fill_far, 1: fill_weights, 2: fill_ready})
    grad_attn_chunks, (down_pair,) = run_ticks(
        first_parts, [feed_forward, feed_back, attn_back], head_index, head_count, fills
    )
    grad_attn_low = jnp.concatenate(grad_attn_chunks, axis=0)
    hidden_out = rows_all("out")
    down_grad = scatter_last(down_pair) if spread else finish_sum(down_pair).astype(f32)
    gate_grad, up_grad = late["gate_sum"], late["up_sum"]

    grad_self_tok, grad_self_t, grad_cross_tok, grad_cross_t, self_delta, cross_delta, gate_rows = unmix(
        gate_local, grad_attn_chunks, out_t, self_t, cross_t
    )
    cross_gate_part = jnp.sum(gate_rows, axis=1) * (1.0 - gate_local * gate_local)

    def back(group, parts, before=None):
        return attend_back(
            self_info(jnp.array(group)), query_t, grad_self_t, queries, grad_self_tok, self_lse, self_delta,
            [pieces[g] for g in group], heads, clips, bf16, parts, before,
        )

    def cross_back(before):
        return attend_back(
            text_info, query_t, grad_cross_t, queries, grad_cross_tok, cross_lse, cross_delta,
            text_pieces, heads, clips, f32, 1, before,
        )

    if spread:
        dq, _, kv_mine, kv_theirs = back((3, 2, 7, 6), 2)
        kv_got = core(kv_theirs)
        kv_mine, low = hold((kv_mine, grad_attn_low))
        out_part = matmul(low, mixed, COLS).astype(bf16)
        total = add_low(kv_mine, kv_got)
        total, dq = hold((total, dq))
        first = swap(total, "seq", 8, other_way)
        dq, text_dot, cross_kv = cross_back(dq)
        text_low = text_back(text_pre, key_gain, cross_kv)
        dq, text_low, gate_grad = hold((dq, text_low, gate_grad))
        dq, _, kv_mine, kv_theirs = back((1, 5), 2, dq)
        first, kv_mine, kv_theirs, up_grad = hold((first, kv_mine, kv_theirs, up_grad))
        total = kv_mine.astype(f32) + core(kv_theirs).astype(f32) + first[:local_rows].astype(f32)
        total = total.astype(bf16)
        second = swap(total, "seq", 8, first_way)
        dq, _, kv_mine, kv_theirs = back((0, 4), 2, dq)
        second, kv_mine, kv_theirs = hold((second, kv_mine, kv_theirs))
        kv_parts, kv_starts = [kv_mine, core(kv_theirs), first, second], (0, 0, local_rows, 0)
    else:
        dq, _, kv_all = back(tuple(range(seq_count)), 1)
        dq, text_dot, cross_kv = cross_back(dq)
        out_part = matmul(grad_attn_low, mixed, COLS).astype(bf16)
        text_low = text_back(text_pre, key_gain, cross_kv)
        kv_parts, kv_starts = [finish_sum(kv_all)], (0,)
    qkv_low, grad_query_gain, grad_key_gain = project_back(
        pre, query_gain, key_gain, cos, sin, dq, kv_parts, kv_starts
    )
    x_normed = hidden_in.astype(f32) * x_scale
    act_part = matmul(qkv_low, w_qkv, ROWS)
    sum_a = jnp.sum(act_part * x_normed, axis=0)
    act_low, qkv_low = hold((act_part.astype(bf16), qkv_low))
    fold = lambda v: v[0, :HD] + v[0, HD:]
    pair_gains = jnp.concatenate([fold(grad_query_gain), fold(grad_key_gain + text_dot / key_gain)])
    tail = jnp.stack([sum_a, jnp.pad(pair_gains, (0, model_width - 2 * HD))])
    tail = jnp.pad(tail, ((0, 14), (0, 0))).astype(bf16)
    small = jnp.concatenate([vec("ua"), vec("sf"), vec("uf"), cross_gate_part])

    def collect(k, end, total, got):
        total = jnp.where(end[0] == 1, got, total)
        if k == 0:
            late["tail"] = total[chunk:].astype(f32)
        return total[:chunk]

    def fill0(carry):
        part = matmul(act_a, qkv_low, COLS).astype(bf16)
        late["gate"] = gate_grad.astype(f32)
        late["qkv"] = scatter_start(part, seq_index) if spread else part
        if not spread:
            return [lax.psum(text_low, "seq")]
        return [scatter_start(text_low, seq_index)]

    def fill1(carry):
        if not spread:
            return carry
        return [scatter_first(carry[0], seq_index)]

    def fill2(carry):
        if not spread:
            return carry
        qkv, carry = hold((late["qkv"], carry))
        late["qkv"] = scatter_first(qkv, seq_index)
        return [scatter_second(carry[0], seq_index)]

    def fill3(carry):
        if not spread:
            late["down"] = down_grad.T
            return carry
        own = add_low(*carry[0])
        grad, own = hold((down_grad, own))
        late["down"] = grad.T
        return [[own, swap(own, "seq", 8, first_way), swap(own, "seq", 8, other_way)]]

    def fill4(carry):
        text = carry[0]
        values = jnp.concatenate([small, late["tail"][0], late["tail"][1, : 2 * HD]])
        values, text, up = hold((values, text, up_grad))
        late["up"] = up.astype(f32)
        if not spread:
            return [lax.psum(values, "seq"), text]
        qkv, text = hold((late["qkv"], text))
        late["qkv"] = scatter_second(qkv, seq_index)
        return [hop(values, seq_hops[:1]), text + [swap(text[1], "seq", 8, other_way)]]

    def fill5(carry):
        values, text = carry
        if not spread:
            return carry
        return [hop(values, seq_hops[1:]), text + [core(v) for v in text]]

    def fill6(carry):
        qkv = late["qkv"]
        qkv = scatter_last(qkv) if spread else finish_sum(qkv).astype(f32)
        text = place(carry[1], roles) if spread else carry[1]
        return [carry[0], matmul(own_text, text, COLS), qkv]

    parts = [rows_of(act_low, k) for k in range(chunk_count)]
    parts[0] = jnp.concatenate([parts[0], tail])
    fills = dict(enumerate([fill0, fill1, fill2, fill3, fill4, fill5, fill6]))
    act_chunks, (values, text_grad, own_qkv) = run_ticks(parts, [collect], head_index, head_count, fills)
    out_grad, act_chunks = hold((finish_sum(out_part), act_chunks))
    input_grad = finish(act_chunks, [keep["dmid"] for keep in kept], hidden_in, x_scale, gain_x[None, :])

    sum_ua, sum_sf, sum_uf = (values[k * model_width : (k + 1) * model_width] for k in range(3))
    values = values[3 * model_width :]
    cross_gate_grad, sum_sa, qk_sums = jnp.split(values, [heads, heads + model_width])
    qk_gains_grad = qk_sums.reshape(2, HD)
    norm_gains_grad = jnp.stack(
        [sum_sa * (1.0 + scale_a), sum_ua * tanh_a, sum_sf * (1.0 + scale_f), sum_uf * tanh_f]
    )
    mod_grad = jnp.concatenate(
        [
            sum_sa * norm_gains[0],
            sum_ua * norm_gains[1] * (1.0 - tanh_a * tanh_a),
            sum_sf * norm_gains[2],
            sum_uf * norm_gains[3] * (1.0 - tanh_f * tanh_f),
        ]
    )
    own_mod = lax.dynamic_slice_in_dim(
        mod_grad, (seq_index * head_count + head_index) * piece_width, piece_width
    )
    ada_grad = cond_act.astype(f32)[:, None] * own_mod[None, :]
    return (
        hidden_out,
        input_grad,
        ada_grad,
        norm_gains_grad,
        qk_gains_grad,
        cut(own_qkv[:, :wide]),
        cut(own_qkv[:, wide : 2 * wide]),
        cut(own_qkv[:, 2 * wide : 3 * wide]),
        cut(out_grad).astype(f32).T,
        cross_gate_grad,
        cut(text_grad[:, :wide]),
        cut(text_grad[:, wide:]),
        late["gate"],
        late["up"],
        late["down"],
    )


def solution(mesh):
    in_specs = (
        P("seq", None),
        P(),
        P(),
        P(),
        P(None, ("seq", "head")),
        P(),
        P(),
        P("seq", "head"),
        P("seq", "head"),
        P("seq", "head"),
        P("head", "seq"),
        P("head"),
        P("seq", "head"),
        P("seq", "head"),
        P("seq", "head"),
        P("seq", "head"),
        P("head", "seq"),
        P("seq", None),
    )
    out_specs = (
        P("seq", None),
        P("seq", None),
        P(None, ("seq", "head")),
        P(),
        P(),
        P("seq", "head"),
        P("seq", "head"),
        P("seq", "head"),
        P("head", "seq"),
        P("head"),
        P("seq", "head"),
        P("seq", "head"),
        P("seq", "head"),
        P("seq", "head"),
        P("head", "seq"),
    )
    body = functools.partial(per_device, mesh.shape["seq"], mesh.shape["head"])
    return jax.shard_map(body, mesh=mesh, in_specs=in_specs, out_specs=out_specs, check_vma=False)
```

time: 720 us -> 598 us (0.83)
  waiting for transfers between devices: 258 us -> 129 us
  Pallas kernels: 100 us -> 187 us
  other arithmetic: 101 us -> 38.2 us
  matrix products: 54.6 us -> 14.6 us
  local copies, waits for them, and re-layouts: 63.5 us -> 73.7 us
  starting transfers between devices: 119 us -> 129 us
    ppermute x48 -> x36, waiting for transfers between devices: 183 us -> 70.6 us  [the longest x12 29.9 us: run_ticks(): got = lax.ppermute(send, 'head', [(0, 1), (3, 2), (1, 0), (2, 3)])]
    pallas_call x16 -> x51, Pallas kernels: 100 us -> 187 us  [the longest x4 60.6 us: attend_back(): pl.pallas_call(functools.partial(bwd_kernel, heads, clips, count, tile, l...]
    convert_element_type x41 -> x13, other arithmetic: 45.5 us -> 13.1 us  [the longest x8 6.41 us: add_low(): return (a.astype(f32) + b.astype(f32)).astype(bf16)]
    reduce_sum x11 -> x1, other arithmetic: 32.4 us -> 0.12 us  [per_device(): jnp.sum(gate_rows, axis=1) * (1.0 - gate_local * gate_local)]
    unnamed x328 -> x392, local copies, waits for them, and re-layouts: 12.3 us -> 43.8 us
    dot_general x12 -> x5, matrix products: 32.9 us -> 11.7 us  [matmul(): return lax.dot_general(left, right, dims, preferred_element_type=f32)]
    ppermute x39 -> x57, waiting for transfers between devices: 74 us -> 52.8 us  [swap(): return lax.ppermute(value, axis, [(i, to(i)) for i in range(count)])]
    dot_general x6 -> x2, matrix products: 21.7 us -> 2.93 us  [matmul(): return jnp.dot(left, right, preferred_element_type=f32)]
  transfers between devices with their start and end apart: 95 -> 98, of which waited for: 40 -> 38; matrix products, arithmetic and copies ran while one was open for 22% -> 12% of each run, Pallas kernels for 13% -> 30%
where the time goes in v2:
time: 598 us; the launch traced here: 588 us
  Pallas kernels  187 us (31%)
  starting transfers between devices  129 us (22%)
  waiting for transfers between devices  129 us (22%)
  local copies, waits for them, and re-layouts  73.7 us (12%)
  other arithmetic  38.2 us (6%)
  between operations  16.7 us (3%)
  matrix products  14.6 us (2%)
    pallas_call x4, Pallas kernels, attend_back(): pl.pallas_call(functools.partial(bwd_kernel, heads, clips, count, tile, l...  60.6 us
    pallas_call x15, Pallas kernels, fused(): pl.pallas_call(functools.partial(kernel, **static) if static else kernel,...  53.5 us
    ppermute x57, waiting for transfers between devices, swap(): return lax.ppermute(value, axis, [(i, to(i)) for i in range(count)])  52.8 us
    ppermute x12, starting transfers between devices, run_ticks(): got = lax.ppermute(send, 'head', [(0, 1), (3, 2), (1, 0), (2, 3)])  47.6 us
    unnamed x392, local copies, waits for them, and re-layouts  43.8 us
    ppermute x57, starting transfers between devices, swap(): return lax.ppermute(value, axis, [(i, to(i)) for i in range(count)])  42.5 us
    ppermute x12, waiting for transfers between devices, run_ticks(): got = lax.ppermute(send, 'head', [(0, 1), (3, 2), (1, 0), (2, 3)])  29.9 us
    pallas_call x4, Pallas kernels, attend(): pl.pallas_call(functools.partial(fwd_kernel, heads, clips, count, tile, l...  28.8 us
  transfers between devices with their start and end apart: 98, of which 38 were waited for; matrix products, arithmetic and copies ran while one was open for 12% of the time, Pallas kernels for 30%

profile of v2, /device:TPU:0, one launch (start us, length us, event | category | flops | bytes accessed | tf_op | source)
XLA Modules:
  0.0 588.0 jit_solution(13636099994174709351)
XLA Ops:
  30.3 3.3 collective-permute-done.7.rest_3_
  45.2 6.3 %project.1 = (bf16[512,1536]{1,0:T(8,128)(2,1)S(1)}, f32[512,1]{1,0:T(8,128)S(1)}, f32[512,768]{1,0:T(8,128)S(1)}, bf16[512,768]{1,0:T(8,128)(2,1)S(1)}, bf16[51...) custom-call(s32[8]{0:T(128)S(1)} %stack.77.roles, ...), custom_call_target="tpu_custom_call" | custom-call | flops 1 | bytes 1 | tf_op jit(solution)/shard_map/project/pallas_call | solution.py:610
  64.2 6.3 %attend.4.rest_0_ = f32[6,80,512]{2,1,0:T(8,128)} custom-call(s32[19]{0:T(128)} %concatenate.59.info, bf16[384,512]{1,0:T(8,128)(2,1)} %copy-done.6, bf16[512,768]{1,0:T(8,128)(2,1)} %copy-done.27, bf16[512,768]{1,0:T(8,128)(2,1)} %copy-done.135), custom_call_target="tpu_custom_call" | custom-call | flops 1 | bytes 1 | tf_op jit(solution)/shard_map/attend/pallas_call | solution.py:122
  70.6 12.3 %collective-permute-done.15.rest_1_ = bf16[192,384]{1,0:T(8,128)(2,1)S(1)} collective-permute-done((bf16[192,384]{1,0:T(8,128)(2,1)S(1)}, bf16[192,384]{1,0:T(8,128)(2,1)S(1)}, u32[]{:S(2)}, u32[]{:S(2)}) %collective-permute-start.15) | collective-permute-done | bytes 147488 | tf_op jit(solution)/shard_map/ppermute | solution.py:248
  88.0 10.5 %attend.5.rest_0_ = f32[6,80,512]{2,1,0:T(8,128)} custom-call(s32[21]{0:T(128)} %concatenate.60.info, bf16[384,512]{1,0:T(8,128)(2,1)} %copy-done.6, f32[6,80,512]{2,1,0:T(8,128)} %attend.4.rest_0_, bf16[512,768]{1,0:T(8,128)(2,1)} %collective-permute-done.12.rest_1_, bf16[512,768]{1,0:T(8,128)(2,1)} %collective-permute-done.13.rest_2_.rest_1_, ...), custom_call_target="tpu_custom_call" | custom-call | flops 1 | bytes 1 | tf_op jit(solution)/shard_map/attend/pallas_call | solution.py:122
  111.6 5.2 attend.7.cross
  116.8 6.7 %attend.6.sums = f32[6,80,512]{2,1,0:T(8,128)} custom-call(s32[19]{0:T(128)} %concatenate.57.info, bf16[384,512]{1,0:T(8,128)(2,1)} %copy-done.6, f32[6,80,512]{2,1,0:T(8,128)} %attend.5.rest_0_, bf16[512,768]{1,0:T(8,128)(2,1)} %copy-done.134, bf16[512,768]{1,0:T(8,128)(2,1)} %collective-permute-done.21.rest_2_), custom_call_target="tpu_custom_call" | custom-call | flops 1 | bytes 1 | tf_op jit(solution)/shard_map/attend/pallas_call | solution.py:122
  130.1 3.5 collective-permute-start.26
  133.6 8.5 %collective-permute-done.26.refs_1_ = bf16[128,1536]{1,0:T(8,128)(2,1)S(1)} collective-permute-done((bf16[128,1536]{1,0:T(8,128)(2,1)S(1)}, bf16[128,1536]{1,0:T(8,128)(2,1)S(1)}, u32[]{:S(2)}, u32[]{:S(2)}) %collective-permute-start.26) | collective-permute-done | bytes 393248 | tf_op jit(solution)/shard_map/ppermute | solution.py:533
  142.1 4.3 collective-permute-done.29.rest_3_
  147.3 6.2 %collective-permute-start.34 = (bf16[128,1536]{1,0:T(8,128)(2,1)S(1)}, bf16[128,1536]{1,0:T(8,128)(2,1)S(1)}, u32[]{:S(2)}, u32[]{:S(2)}) collective-permute-start(bf16[128,1536]{1,0:T(8,128)(2,1)S(1)} %get-tuple-element.457.refs_0_), channel_id=1, source_target_pairs={{0,1},{3,2},{4,5},{7,6},{8,9},{11,10},{12,13},{15,14},{16,17},{19,... | collective-permute-start | bytes 1179656 | tf_op jit(solution)/shard_map/ppermute | solution.py:533
  153.5 6.1 %place.4 = (bf16[1536,1024]{1,0:T(8,128)(2,1)}, bf16[1536,1024]{1,0:T(8,128)(2,1)}) custom-call(s32[8]{0:T(128)S(1)} %stack.77.roles, bf16[192,2048]{1,0:T(8,128)(2,1)S(1)} %pad_maximum_fusion.3.rest_0_, bf16[192,2048]{1,0:T(8,128)(2,1)} %collective-permute-done.27.rest_1_, bf16[192,2048]{1,0:T(8,128)(2,1)} %collective-permute-done.28.rest_2_, ...), custom_call_target="tpu_custom_call" | custom-call | flops 1 | bytes 1 | tf_op jit(solution)/shard_map/place/pallas_call | solution.py:294
  167.5 6.5 %collective-permute-done.36.got.refs_1_ = bf16[128,1536]{1,0:T(8,128)(2,1)S(1)} collective-permute-done((bf16[128,1536]{1,0:T(8,128)(2,1)S(1)}, bf16[128,1536]{1,0:T(8,128)(2,1)S(1)}, u32[]{:S(2)}, u32[]{:S(2)}) %collective-permute-start.36) | collective-permute-done | bytes 393248 | tf_op jit(solution)/shard_map/ppermute | solution.py:529
  175.8 3.8 collective-permute-start.38
  203.6 3.4 feed_forward.5
  211.8 5.7 collective-permute-start.43
  233.5 4.2 collective-permute-start.46
  245.5 5.1 collective-permute-start.48
  251.3 3.3 feed_back.5
  257.3 11.8 %collective-permute-start.51 = (bf16[128,1536]{1,0:T(8,128)(2,1)S(1)}, bf16[128,1536]{1,0:T(8,128)(2,1)S(1)}, u32[]{:S(2)}, u32[]{:S(2)}) collective-permute-start(bf16[128,1536]{1,0:T(8,128)(2,1)S(1)} %get-tuple-element.555), channel_id=1, source_target_pairs={{0,1},{3,2},{1,0},{2,3},{4,5},{7,6},{5,4},{6,7},{8,9},{11,10},{9,8... | collective-permute-start | bytes 1179656 | tf_op jit(solution)/shard_map/ppermute | solution.py:529
  269.1 3.3 feed_back.6
  276.1 3.7 collective-permute-start.52
  280.6 3.3 feed_back.7
  284.6 4.6 collective-permute-done.52.got.refs_1_
  294.9 5.2 weight_grad.3
  300.1 3.5 attn_back.4
  308.7 3.6 attn_back.5
  312.3 5.2 weight_grad.4
  317.4 3.3 collective-permute-done.56.got
  327.6 5.3 weight_grad.5
  332.9 3.7 attn_back.6
  336.6 3.8 collective-permute-done.59.got
  349.7 3.5 attn_back.7
  353.2 5.0 collective-permute-done.61
  367.4 22.2 %attend_back.4 = (f32[384,512]{1,0:T(8,128)}, f32[1,128]{1,0:T(1,128)}, bf16[1024,768]{1,0:T(8,128)(2,1)}, bf16[1024,768]{1,0:T(8,128)(2,1)}) custom-call(s32[21]{0:T(128)} %concatenate.65.info, bf16[384,512]{1,0:T(8,128)(2,1)} %copy-done.6, bf16[384,512]{1,0:T(8,128)(2,1)} %copy-done.20, bf16[512,384]{1,0:T(8,128)(2,1)} %copy-done.12, ...), custom_call_target="tpu_custom_call" | custom-call | flops 1 | bytes 1 | tf_op jit(solution)/shard_map/attend_back/pallas_call | solution.py:202
  396.6 9.1 %attend_back.5 = (f32[384,512]{1,0:T(8,128)}, f32[1,128]{1,0:T(1,128)}, f32[512,768]{1,0:T(8,128)}) custom-call(s32[18]{0:T(128)} %concatenate.63.info, bf16[384,512]{1,0:T(8,128)(2,1)} %copy-done.6, bf16[384,512]{1,0:T(8,128)(2,1)} %copy-done.88, bf16[512,384]{1,0:T(8,128)(2,1)} %copy-done.12, bf16[512,384]{1,0:T(8,128)(2,1)} %copy-done.87, ...), custom_call_target="tpu_custom_call" | custom-call | flops 1 | bytes 1 | tf_op jit(solution)/shard_map/attend_back/pallas_call | solution.py:202
  405.7 3.9 text_back.1
  409.6 14.6 %attend_back.6 = (f32[384,512]{1,0:T(8,128)}, f32[1,128]{1,0:T(1,128)}, bf16[512,768]{1,0:T(8,128)(2,1)}, bf16[512,768]{1,0:T(8,128)(2,1)}) custom-call(s32[19]{0:T(128)} %concatenate.68.info, bf16[384,512]{1,0:T(8,128)(2,1)} %copy-done.6, bf16[384,512]{1,0:T(8,128)(2,1)} %copy-done.20, bf16[512,384]{1,0:T(8,128)(2,1)} %copy-done.12, ...), custom_call_target="tpu_custom_call" | custom-call | flops 1 | bytes 1 | tf_op jit(solution)/shard_map/attend_back/pallas_call | solution.py:202
  433.8 14.8 %attend_back.7 = (f32[384,512]{1,0:T(8,128)}, f32[1,128]{1,0:T(1,128)}, bf16[512,768]{1,0:T(8,128)(2,1)}, bf16[512,768]{1,0:T(8,128)(2,1)}) custom-call(s32[19]{0:T(128)} %concatenate.59.info, bf16[384,512]{1,0:T(8,128)(2,1)} %copy-done.6, bf16[384,512]{1,0:T(8,128)(2,1)} %copy-done.20, bf16[512,384]{1,0:T(8,128)(2,1)} %copy-done.12, ...), custom_call_target="tpu_custom_call" | custom-call | flops 1 | bytes 1 | tf_op jit(solution)/shard_map/attend_back/pallas_call | solution.py:202
  453.7 6.5 %project_back.1 = (bf16[512,1152]{1,0:T(8,128)(2,1)}, f32[1,128]{1,0:T(1,128)}, f32[1,128]{1,0:T(1,128)}) custom-call(f32[512,768]{1,0:T(8,128)} %copy-done.48, f32[1,128]{1,0:T(1,128)} %copy-done.123, f32[1,128]{1,0:T(1,128)} %copy-done.115, f32[512,128]{1,0:T(8,128)} %copy-done.29, f32[512,128]{1,0:T(8,128)} %copy-done.28, ...), custom_call_target="tpu_custom_call" | custom-call | flops 1 | bytes 1 | tf_op jit(solution)/shard_map/project_back/pallas_call | solution.py:759
  460.1 4.8 fusion.33
  477.6 6.7 %collective-permute-done.67.refs_1_ = bf16[144,1536]{1,0:T(8,128)(2,1)S(1)} collective-permute-done((bf16[144,1536]{1,0:T(8,128)(2,1)S(1)}, bf16[144,1536]{1,0:T(8,128)(2,1)S(1)}, u32[]{:S(2)}, u32[]{:S(2)}) %collective-permute-start.67) | collective-permute-done | bytes 442400 | tf_op jit(solution)/shard_map/ppermute | solution.py:533
  486.1 7.4 %collective-permute-start.70 = (bf16[128,1536]{1,0:T(8,128)(2,1)S(1)}, bf16[128,1536]{1,0:T(8,128)(2,1)S(1)}, u32[]{:S(2)}, u32[]{:S(2)}) collective-permute-start(bf16[128,1536]{1,0:T(8,128)(2,1)S(1)} %get-tuple-element.704.refs_0_), channel_id=1, source_target_pairs={{0,1},{3,2},{4,5},{7,6},{8,9},{11,10},{12,13},{15,14},{16,17},{19,... | collective-permute-start | bytes 1179656 | tf_op jit(solution)/shard_map/ppermute | solution.py:533
  507.7 4.9 collective-permute-done.72
  518.6 4.9 collective-permute-done.75
  540.4 8.2 %collective-permute-done.80 = bf16[128,1536]{1,0:T(8,128)(2,1)S(1)} collective-permute-done((bf16[128,1536]{1,0:T(8,128)(2,1)S(1)}, bf16[128,1536]{1,0:T(8,128)(2,1)S(1)}, u32[]{:S(2)}, u32[]{:S(2)}) %collective-permute-start.80) | collective-permute-done | bytes 393248 | tf_op jit(solution)/shard_map/ppermute | solution.py:535
  559.0 5.8 collective-permute-done.85
  575.3 5.7 finish.1
  (732 shorter events, 271.9 us)
Async XLA Ops:
  7.2 94.1 %all-reduce.4.cloned.1.call-start = ((), (), s32[]{:S(2)}) async-start(), calls=%async_computation.3 | async-start | bytes 1572864 | tf_op jit(solution)/shard_map/psum | solution.py:887
  11.7 13.5 %collective-permute-start = (bf16[192,1152]{1,0:T(8,128)(2,1)S(1)}, bf16[192,1152]{1,0:T(8,128)(2,1)S(1)}, u32[]{:S(2)}, u32[]{:S(2)}) collective-permute-start(bf16[192,1152]{1,0:T(8,128)(2,1)S(1)} %constant_dynamic-update-slice_fusion.rest_0_), channel_id=1, source_target_pairs={{0,8},{4,20},{8,0},{12,28},{16,24},{20,4},{24,16},{28,12},{1,9},{5... | collective-permute-start | bytes 1327112 | tf_op jit(solution)/shard_map/ppermute | solution.py:248
  16.3 27.0 %collective-permute-start.8 = (bf16[192,1152]{1,0:T(8,128)(2,1)S(1)}, bf16[192,1152]{1,0:T(8,128)(2,1)}, u32[]{:S(2)}, u32[]{:S(2)}) collective-permute-start(bf16[192,1152]{1,0:T(8,128)(2,1)S(1)} %constant_dynamic-update-slice_fusion.rest_0_), channel_id=1, source_target_pairs={{0,4},{4,0},{8,12},{12,8},{16,20},{20,16},{24,28},{28,24},{1,5},{5... | collective-permute-start | bytes 1327112 | tf_op jit(solution)/shard_map/ppermute | solution.py:248
  26.9 16.4 %collective-permute-start.9 = (bf16[192,1152]{1,0:T(8,128)(2,1)S(1)}, bf16[192,1152]{1,0:T(8,128)(2,1)}, u32[]{:S(2)}, u32[]{:S(2)}) collective-permute-start(bf16[192,1152]{1,0:T(8,128)(2,1)S(1)} %collective-permute-done.rest_1_), channel_id=1, source_target_pairs={{0,4},{4,0},{8,12},{12,8},{16,20},{20,16},{24,28},{28,24},{1,5},{5... | collective-permute-start | bytes 1327112 | tf_op jit(solution)/shard_map/ppermute | solution.py:248
  30.3 13.0 %collective-permute-start.10 = (bf16[192,1152]{1,0:T(8,128)(2,1)}, bf16[192,1152]{1,0:T(8,128)(2,1)}, u32[]{:S(2)}, u32[]{:S(2)}) collective-permute-start(bf16[192,1152]{1,0:T(8,128)(2,1)} %collective-permute-done.1.rest_2_), channel_id=1, source_target_pairs={{0,4},{4,0},{8,12},{12,8},{16,20},{20,16},{24,28},{28,24},{1,5},{5... | collective-permute-start | bytes 1327112 | tf_op jit(solution)/shard_map/ppermute | solution.py:248
  43.1 145.9 %all-gather.2.cloned.1.call-start = ((), (), s32[]{:S(2)}) async-start(), calls=%async_computation.4 | async-start | bytes 3538944 | tf_op jit(solution)/shard_map/all_gather | solution.py:888
  57.9 25.0 %collective-permute-start.12 = (bf16[512,768]{1,0:T(8,128)(2,1)S(1)}, bf16[512,768]{1,0:T(8,128)(2,1)}, u32[]{:S(2)}, u32[]{:S(2)}) collective-permute-start(bf16[512,768]{1,0:T(8,128)(2,1)S(1)} %get-tuple-element.430.rest_0_.rest_1_), channel_id=1, source_target_pairs={{0,8},{4,20},{8,0},{12,28},{16,24},{20,4},{24,16},{28,12},{1,9},{5... | collective-permute-start | bytes 2359304 | tf_op jit(solution)/shard_map/ppermute | solution.py:248
  59.7 23.2 %collective-permute-start.13 = (bf16[512,768]{1,0:T(8,128)(2,1)S(1)}, bf16[512,768]{1,0:T(8,128)(2,1)}, u32[]{:S(2)}, u32[]{:S(2)}) collective-permute-start(bf16[512,768]{1,0:T(8,128)(2,1)S(1)} %get-tuple-element.430.rest_0_.rest_1_), channel_id=1, source_target_pairs={{0,16},{4,12},{8,24},{12,4},{16,0},{20,28},{24,8},{28,20},{1,17},{... | collective-permute-start | bytes 2359304 | tf_op jit(solution)/shard_map/ppermute | solution.py:248
  60.7 348.9 %reduce-scatter.6.cloned.1.call-start = ((), (), s32[]{:S(2)}) async-start(), calls=%async_computation.6 | async-start | bytes 3538944 | tf_op jit(solution)/shard_map/reduce_scatter | solution.py:829
  61.4 21.5 %collective-permute-start.15 = (bf16[192,384]{1,0:T(8,128)(2,1)S(1)}, bf16[192,384]{1,0:T(8,128)(2,1)S(1)}, u32[]{:S(2)}, u32[]{:S(2)}) collective-permute-start(bf16[192,384]{1,0:T(8,128)(2,1)S(1)} %bitcast.85), channel_id=1, source_target_pairs={{0,8},{4,20},{8,0},{12,28},{16,24},{20,4},{24,16},{28,12},{1,9},{5... | collective-permute-start | bytes 442376 | tf_op jit(solution)/shard_map/ppermute | solution.py:248
  61.7 21.2 %collective-permute-start.16 = (bf16[192,384]{1,0:T(8,128)(2,1)S(1)}, bf16[192,384]{1,0:T(8,128)(2,1)S(1)}, u32[]{:S(2)}, u32[]{:S(2)}) collective-permute-start(bf16[192,384]{1,0:T(8,128)(2,1)S(1)} %bitcast.86), channel_id=1, source_target_pairs={{0,16},{4,12},{8,24},{12,4},{16,0},{20,28},{24,8},{28,20},{1,17},{... | collective-permute-start | bytes 442376 | tf_op jit(solution)/shard_map/ppermute | solution.py:248
  83.5 17.8 %collective-permute-start.17 = (bf16[512,768]{1,0:T(8,128)(2,1)}, bf16[512,768]{1,0:T(8,128)(2,1)S(1)}, u32[]{:S(2)}, u32[]{:S(2)}) collective-permute-start(bf16[512,768]{1,0:T(8,128)(2,1)} %collective-permute-done.12.rest_1_), channel_id=1, source_target_pairs={{0,16},{4,12},{8,24},{12,4},{16,0},{20,28},{24,8},{28,20},{1,17},{... | collective-permute-start | bytes 2359304 | tf_op jit(solution)/shard_map/ppermute | solution.py:248
  85.0 16.3 %collective-permute-start.20 = (bf16[192,384]{1,0:T(8,128)(2,1)S(1)}, bf16[192,384]{1,0:T(8,128)(2,1)S(1)}, u32[]{:S(2)}, u32[]{:S(2)}) collective-permute-start(bf16[192,384]{1,0:T(8,128)(2,1)S(1)} %collective-permute-done.15.rest_1_), channel_id=1, source_target_pairs={{0,16},{4,12},{8,24},{12,4},{16,0},{20,28},{24,8},{28,20},{1,17},{... | collective-permute-start | bytes 442376 | tf_op jit(solution)/shard_map/ppermute | solution.py:248
  101.4 25.6 %collective-permute-start.27 = (bf16[192,2048]{1,0:T(8,128)(2,1)S(1)}, bf16[192,2048]{1,0:T(8,128)(2,1)}, u32[]{:S(2)}, u32[]{:S(2)}) collective-permute-start(bf16[192,2048]{1,0:T(8,128)(2,1)S(1)} %pad_maximum_fusion.3.rest_0_), channel_id=1, source_target_pairs={{0,8},{4,20},{8,0},{12,28},{16,24},{20,4},{24,16},{28,12},{1,9},{5... | collective-permute-start | bytes 2359304 | tf_op jit(solution)/shard_map/ppermute | solution.py:248
  102.4 26.0 %collective-permute-start.28 = (bf16[192,2048]{1,0:T(8,128)(2,1)S(1)}, bf16[192,2048]{1,0:T(8,128)(2,1)}, u32[]{:S(2)}, u32[]{:S(2)}) collective-permute-start(bf16[192,2048]{1,0:T(8,128)(2,1)S(1)} %pad_maximum_fusion.3.rest_0_), channel_id=1, source_target_pairs={{0,16},{4,12},{8,24},{12,4},{16,0},{20,28},{24,8},{28,20},{1,17},{... | collective-permute-start | bytes 2359304 | tf_op jit(solution)/shard_map/ppermute | solution.py:248
  103.8 19.8 %collective-permute-start.23 = (bf16[192,384]{1,0:T(8,128)(2,1)S(1)}, bf16[192,384]{1,0:T(8,128)(2,1)S(1)}, u32[]{:S(2)}, u32[]{:S(2)}) collective-permute-start(bf16[192,384]{1,0:T(8,128)(2,1)S(1)} %collective-permute-done.15.rest_1_), channel_id=1, source_target_pairs={{0,4},{4,0},{8,12},{12,8},{16,20},{20,16},{24,28},{28,24},{1,5},{5... | collective-permute-start | bytes 442376 | tf_op jit(solution)/shard_map/ppermute | solution.py:248
  104.5 19.3 %collective-permute-start.24 = (bf16[192,384]{1,0:T(8,128)(2,1)S(1)}, bf16[192,384]{1,0:T(8,128)(2,1)S(1)}, u32[]{:S(2)}, u32[]{:S(2)}) collective-permute-start(bf16[192,384]{1,0:T(8,128)(2,1)S(1)} %collective-permute-done.16.rest_2_), channel_id=1, source_target_pairs={{0,4},{4,0},{8,12},{12,8},{16,20},{20,16},{24,28},{28,24},{1,5},{5... | collective-permute-start | bytes 442376 | tf_op jit(solution)/shard_map/ppermute | solution.py:248
  104.6 19.2 %collective-permute-start.25 = (bf16[192,384]{1,0:T(8,128)(2,1)S(1)}, bf16[192,384]{1,0:T(8,128)(2,1)S(1)}, u32[]{:S(2)}, u32[]{:S(2)}) collective-permute-start(bf16[192,384]{1,0:T(8,128)(2,1)S(1)} %collective-permute-done.20.rest_3_), channel_id=1, source_target_pairs={{0,4},{4,0},{8,12},{12,8},{16,20},{20,16},{24,28},{28,24},{1,5},{5... | collective-permute-start | bytes 442376 | tf_op jit(solution)/shard_map/ppermute | solution.py:248
  127.0 19.4 %collective-permute-start.29 = (bf16[192,2048]{1,0:T(8,128)(2,1)}, bf16[192,2048]{1,0:T(8,128)(2,1)}, u32[]{:S(2)}, u32[]{:S(2)}) collective-permute-start(bf16[192,2048]{1,0:T(8,128)(2,1)} %collective-permute-done.27.rest_1_), channel_id=1, source_target_pairs={{0,16},{4,12},{8,24},{12,4},{16,0},{20,28},{24,8},{28,20},{1,17},{... | collective-permute-start | bytes 2359304 | tf_op jit(solution)/shard_map/ppermute | solution.py:248
  128.4 18.0 %collective-permute-start.31 = (bf16[192,2048]{1,0:T(8,128)(2,1)}, bf16[192,2048]{1,0:T(8,128)(2,1)}, u32[]{:S(2)}, u32[]{:S(2)}) collective-permute-start(bf16[192,2048]{1,0:T(8,128)(2,1)} %collective-permute-done.27.rest_1_), channel_id=1, source_target_pairs={{0,4},{4,0},{8,12},{12,8},{16,20},{20,16},{24,28},{28,24},{1,5},{5... | collective-permute-start | bytes 2359304 | tf_op jit(solution)/shard_map/ppermute | solution.py:248
  128.4 17.9 %collective-permute-start.32 = (bf16[192,2048]{1,0:T(8,128)(2,1)}, bf16[192,2048]{1,0:T(8,128)(2,1)}, u32[]{:S(2)}, u32[]{:S(2)}) collective-permute-start(bf16[192,2048]{1,0:T(8,128)(2,1)} %collective-permute-done.28.rest_2_), channel_id=1, source_target_pairs={{0,4},{4,0},{8,12},{12,8},{16,20},{20,16},{24,28},{28,24},{1,5},{5... | collective-permute-start | bytes 2359304 | tf_op jit(solution)/shard_map/ppermute | solution.py:248
  146.6 12.9 %collective-permute-start.33 = (bf16[128,1536]{1,0:T(8,128)(2,1)S(1)}, bf16[128,1536]{1,0:T(8,128)(2,1)S(1)}, u32[]{:S(2)}, u32[]{:S(2)}) collective-permute-start(bf16[128,1536]{1,0:T(8,128)(2,1)S(1)} %relay.18.refs_2_), channel_id=1, source_target_pairs={{1,2},{2,1},{5,6},{6,5},{9,10},{10,9},{13,14},{14,13},{17,18},{18,... | collective-permute-start | bytes 1179656 | tf_op jit(solution)/shard_map/ppermute | solution.py:527
  147.3 14.7 %collective-permute-start.34 = (bf16[128,1536]{1,0:T(8,128)(2,1)S(1)}, bf16[128,1536]{1,0:T(8,128)(2,1)S(1)}, u32[]{:S(2)}, u32[]{:S(2)}) collective-permute-start(bf16[128,1536]{1,0:T(8,128)(2,1)S(1)} %get-tuple-element.457.refs_0_), channel_id=1, source_target_pairs={{0,1},{3,2},{4,5},{7,6},{8,9},{11,10},{12,13},{15,14},{16,17},{19,... | collective-permute-start | bytes 1179656 | tf_op jit(solution)/shard_map/ppermute | solution.py:533
  175.8 23.6 %collective-permute-start.38 = (bf16[128,1536]{1,0:T(8,128)(2,1)}, bf16[128,1536]{1,0:T(8,128)(2,1)}, u32[]{:S(2)}, u32[]{:S(2)}) collective-permute-start(bf16[128,1536]{1,0:T(8,128)(2,1)} %get-tuple-element.478), channel_id=1, source_target_pairs={{0,1},{3,2},{1,0},{2,3},{4,5},{7,6},{5,4},{6,7},{8,9},{11,10},{9,8... | collective-permute-start | bytes 1179656 | tf_op jit(solution)/shard_map/ppermute | solution.py:529
  179.6 19.9 %collective-permute-start.39 = (bf16[128,1536]{1,0:T(8,128)(2,1)}, bf16[128,1536]{1,0:T(8,128)(2,1)}, u32[]{:S(2)}, u32[]{:S(2)}) collective-permute-start(bf16[128,1536]{1,0:T(8,128)(2,1)} %get-tuple-element.483.refs_2_), channel_id=1, source_target_pairs={{1,2},{2,1},{5,6},{6,5},{9,10},{10,9},{13,14},{14,13},{17,18},{18,... | collective-permute-start | bytes 1179656 | tf_op jit(solution)/shard_map/ppermute | solution.py:527
  211.8 12.7 %collective-permute-start.43 = (bf16[128,1536]{1,0:T(8,128)(2,1)S(1)}, bf16[128,1536]{1,0:T(8,128)(2,1)S(1)}, u32[]{:S(2)}, u32[]{:S(2)}) collective-permute-start(bf16[128,1536]{1,0:T(8,128)(2,1)S(1)} %get-tuple-element.497), channel_id=1, source_target_pairs={{0,1},{3,2},{1,0},{2,3},{4,5},{7,6},{5,4},{6,7},{8,9},{11,10},{9,8... | collective-permute-start | bytes 1179656 | tf_op jit(solution)/shard_map/ppermute | solution.py:529
  256.6 15.9 %collective-permute-start.50 = (bf16[128,1536]{1,0:T(8,128)(2,1)S(1)}, bf16[128,1536]{1,0:T(8,128)(2,1)S(1)}, u32[]{:S(2)}, u32[]{:S(2)}) collective-permute-start(bf16[128,1536]{1,0:T(8,128)(2,1)S(1)} %get-tuple-element.569.refs_2_), channel_id=1, source_target_pairs={{1,2},{2,1},{5,6},{6,5},{9,10},{10,9},{13,14},{14,13},{17,18},{18,... | collective-permute-start | bytes 1179656 | tf_op jit(solution)/shard_map/ppermute | solution.py:527
  257.3 17.9 %collective-permute-start.51 = (bf16[128,1536]{1,0:T(8,128)(2,1)S(1)}, bf16[128,1536]{1,0:T(8,128)(2,1)S(1)}, u32[]{:S(2)}, u32[]{:S(2)}) collective-permute-start(bf16[128,1536]{1,0:T(8,128)(2,1)S(1)} %get-tuple-element.555), channel_id=1, source_target_pairs={{0,1},{3,2},{1,0},{2,3},{4,5},{7,6},{5,4},{6,7},{8,9},{11,10},{9,8... | collective-permute-start | bytes 1179656 | tf_op jit(solution)/shard_map/ppermute | solution.py:529
  276.1 13.1 %collective-permute-start.52 = (bf16[128,1536]{1,0:T(8,128)(2,1)S(1)}, bf16[128,1536]{1,0:T(8,128)(2,1)S(1)}, u32[]{:S(2)}, u32[]{:S(2)}) collective-permute-start(bf16[128,1536]{1,0:T(8,128)(2,1)S(1)} %get-tuple-element.573), channel_id=1, source_target_pairs={{0,1},{3,2},{1,0},{2,3},{4,5},{7,6},{5,4},{6,7},{8,9},{11,10},{9,8... | collective-permute-start | bytes 1179656 | tf_op jit(solution)/shard_map/ppermute | solution.py:529
  290.7 12.9 %collective-permute-start.54 = (bf16[128,1536]{1,0:T(8,128)(2,1)S(1)}, bf16[128,1536]{1,0:T(8,128)(2,1)S(1)}, u32[]{:S(2)}, u32[]{:S(2)}) collective-permute-start(bf16[128,1536]{1,0:T(8,128)(2,1)S(1)} %get-tuple-element.588), channel_id=1, source_target_pairs={{0,1},{3,2},{1,0},{2,3},{4,5},{7,6},{5,4},{6,7},{8,9},{11,10},{9,8... | collective-permute-start | bytes 1179656 | tf_op jit(solution)/shard_map/ppermute | solution.py:529
  306.5 14.3 %collective-permute-start.58 = (bf16[4,192,1024]{2,1,0:T(8,128)(2,1)}, bf16[4,192,1024]{2,1,0:T(8,128)(2,1)S(1)}, u32[]{:S(2)}, u32[]{:S(2)}) collective-permute-start(bf16[4,192,1024]{2,1,0:T(8,128)(2,1)} %dynamic-slice_bitcast_fusion.1), channel_id=1, source_target_pairs={{0,4},{4,0},{8,12},{12,8},{16,20},{20,16},{24,28},{28,24},{1,5},{5... | collective-permute-start | bytes 4718600 | tf_op jit(solution)/shard_map/ppermute | solution.py:248
  306.7 14.0 %collective-permute-start.56 = (bf16[128,1536]{1,0:T(8,128)(2,1)S(1)}, bf16[128,1536]{1,0:T(8,128)(2,1)S(1)}, u32[]{:S(2)}, u32[]{:S(2)}) collective-permute-start(bf16[128,1536]{1,0:T(8,128)(2,1)S(1)} %get-tuple-element.626.total), channel_id=1, source_target_pairs={{1,0},{2,3},{5,4},{6,7},{9,8},{10,11},{13,12},{14,15},{17,16},{18,... | collective-permute-start | bytes 1179656 | tf_op jit(solution)/shard_map/ppermute | solution.py:535
  308.0 12.7 %collective-permute-start.57 = (bf16[128,1536]{1,0:T(8,128)(2,1)S(1)}, bf16[128,1536]{1,0:T(8,128)(2,1)S(1)}, u32[]{:S(2)}, u32[]{:S(2)}) collective-permute-start(bf16[128,1536]{1,0:T(8,128)(2,1)S(1)} %get-tuple-element.632.refs_0_), channel_id=1, source_target_pairs={{1,2},{2,1},{5,6},{6,5},{9,10},{10,9},{13,14},{14,13},{17,18},{18,... | collective-permute-start | bytes 1179656 | tf_op jit(solution)/shard_map/ppermute | solution.py:527
  321.5 106.4 %reduce-scatter.8.cloned.1.call-start = ((), (), s32[]{:S(2)}) async-start(), calls=%async_computation.7 | async-start | bytes 3538944 | tf_op jit(solution)/shard_map/reduce_scatter | solution.py:829
  326.2 14.3 %collective-permute-start.60 = (bf16[2,192,1024]{2,1,0:T(8,128)(2,1)}, bf16[2,192,1024]{2,1,0:T(8,128)(2,1)S(1)}, u32[]{:S(2)}, u32[]{:S(2)}) collective-permute-start(bf16[2,192,1024]{2,1,0:T(8,128)(2,1)} %pad_maximum_fusion.4), channel_id=1, source_target_pairs={{0,16},{4,12},{8,24},{12,4},{16,0},{20,28},{24,8},{28,20},{1,17},{... | collective-permute-start | bytes 2359304 | tf_op jit(solution)/shard_map/ppermute | solution.py:248
  326.3 14.2 %collective-permute-start.59 = (bf16[128,1536]{1,0:T(8,128)(2,1)S(1)}, bf16[128,1536]{1,0:T(8,128)(2,1)S(1)}, u32[]{:S(2)}, u32[]{:S(2)}) collective-permute-start(bf16[128,1536]{1,0:T(8,128)(2,1)S(1)} %relay.30.total), channel_id=1, source_target_pairs={{1,0},{2,3},{5,4},{6,7},{9,8},{10,11},{13,12},{14,15},{17,16},{18,... | collective-permute-start | bytes 1179656 | tf_op jit(solution)/shard_map/ppermute | solution.py:535
  341.3 228.6 %reduce-scatter.4.cloned.1.call-start = ((), (), s32[]{:S(2)}) async-start(), calls=%async_computation.5 | async-start | bytes 1327104 | tf_op jit(solution)/shard_map/reduce_scatter | solution.py:829
  343.9 14.3 %collective-permute-start.61 = (bf16[192,1024]{1,0:T(8,128)(2,1)}, bf16[192,1024]{1,0:T(8,128)(2,1)S(1)}, u32[]{:S(2)}, u32[]{:S(2)}) collective-permute-start(bf16[192,1024]{1,0:T(8,128)(2,1)} %get-tuple-element.817), channel_id=1, source_target_pairs={{0,8},{4,20},{8,0},{12,28},{16,24},{20,4},{24,16},{28,12},{1,9},{5... | collective-permute-start | bytes 1179656 | tf_op jit(solution)/shard_map/ppermute | solution.py:248
  393.7 32.1 %collective-permute-start.63 = (bf16[1024,768]{1,0:T(8,128)(2,1)S(1)}, bf16[1024,768]{1,0:T(8,128)(2,1)S(1)}, u32[]{:S(2)}, u32[]{:S(2)}) collective-permute-start(bf16[1024,768]{1,0:T(8,128)(2,1)S(1)} %add_convert_fusion), channel_id=1, source_target_pairs={{0,16},{4,12},{8,24},{12,4},{16,0},{20,28},{24,8},{28,20},{1,17},{... | collective-permute-start | bytes 4718600 | tf_op jit(solution)/shard_map/ppermute | solution.py:248
  432.7 15.8 %collective-permute-start.65 = (bf16[512,768]{1,0:T(8,128)(2,1)}, bf16[512,768]{1,0:T(8,128)(2,1)}, u32[]{:S(2)}, u32[]{:S(2)}) collective-permute-start(bf16[512,768]{1,0:T(8,128)(2,1)} %add_convert_fusion.1), channel_id=1, source_target_pairs={{0,8},{4,20},{8,0},{12,28},{16,24},{20,4},{24,16},{28,12},{1,9},{5... | collective-permute-start | bytes 2359304 | tf_op jit(solution)/shard_map/ppermute | solution.py:248
  452.3 25.3 %collective-permute-start.68 = (bf16[4,64,768]{2,1,0:T(8,128)(2,1)}, bf16[4,64,768]{2,1,0:T(8,128)(2,1)S(1)}, u32[]{:S(2)}, u32[]{:S(2)}) collective-permute-start(bf16[4,64,768]{2,1,0:T(8,128)(2,1)} %dynamic-slice_bitcast_fusion.2), channel_id=1, source_target_pairs={{0,4},{4,0},{8,12},{12,8},{16,20},{20,16},{24,28},{28,24},{1,5},{5... | collective-permute-start | bytes 1179656 | tf_op jit(solution)/shard_map/ppermute | solution.py:248
  470.3 42.3 %collective-permute-start.74 = (bf16[4,192,1152]{2,1,0:T(8,128)(2,1)}, bf16[4,192,1152]{2,1,0:T(8,128)(2,1)}, u32[]{:S(2)}, u32[]{:S(2)}) collective-permute-start(bf16[4,192,1152]{2,1,0:T(8,128)(2,1)} %dynamic-slice_bitcast_fusion), channel_id=1, source_target_pairs={{0,4},{4,0},{8,12},{12,8},{16,20},{20,16},{24,28},{28,24},{1,5},{5... | collective-permute-start | bytes 5308424 | tf_op jit(solution)/shard_map/ppermute | solution.py:248
  471.3 13.0 %collective-permute-start.67 = (bf16[144,1536]{1,0:T(8,128)(2,1)S(1)}, bf16[144,1536]{1,0:T(8,128)(2,1)S(1)}, u32[]{:S(2)}, u32[]{:S(2)}) collective-permute-start(bf16[144,1536]{1,0:T(8,128)(2,1)S(1)} %pad_maximum_fusion.5.refs_0_), channel_id=1, source_target_pairs={{0,1},{3,2},{4,5},{7,6},{8,9},{11,10},{12,13},{15,14},{16,17},{19,... | collective-permute-start | bytes 1327112 | tf_op jit(solution)/shard_map/ppermute | solution.py:533
  484.4 16.7 %collective-permute-start.69 = (bf16[144,1536]{1,0:T(8,128)(2,1)S(1)}, bf16[144,1536]{1,0:T(8,128)(2,1)S(1)}, u32[]{:S(2)}, u32[]{:S(2)}) collective-permute-start(bf16[144,1536]{1,0:T(8,128)(2,1)S(1)} %relay.31.refs_2_), channel_id=1, source_target_pairs={{1,2},{2,1},{5,6},{6,5},{9,10},{10,9},{13,14},{14,13},{17,18},{18,... | collective-permute-start | bytes 1327112 | tf_op jit(solution)/shard_map/ppermute | solution.py:527
  486.1 15.0 %collective-permute-start.70 = (bf16[128,1536]{1,0:T(8,128)(2,1)S(1)}, bf16[128,1536]{1,0:T(8,128)(2,1)S(1)}, u32[]{:S(2)}, u32[]{:S(2)}) collective-permute-start(bf16[128,1536]{1,0:T(8,128)(2,1)S(1)} %get-tuple-element.704.refs_0_), channel_id=1, source_target_pairs={{0,1},{3,2},{4,5},{7,6},{8,9},{11,10},{12,13},{15,14},{16,17},{19,... | collective-permute-start | bytes 1179656 | tf_op jit(solution)/shard_map/ppermute | solution.py:533
  517.4 19.6 %collective-permute-start.83 = (bf16[2,192,1152]{2,1,0:T(8,128)(2,1)}, bf16[2,192,1152]{2,1,0:T(8,128)(2,1)S(1)}, u32[]{:S(2)}, u32[]{:S(2)}) collective-permute-start(bf16[2,192,1152]{2,1,0:T(8,128)(2,1)} %pad_maximum_fusion.2), channel_id=1, source_target_pairs={{0,16},{4,12},{8,24},{12,4},{16,0},{20,28},{24,8},{28,20},{1,17},{... | collective-permute-start | bytes 2654216 | tf_op jit(solution)/shard_map/ppermute | solution.py:248
  534.9 13.7 %collective-permute-start.80 = (bf16[128,1536]{1,0:T(8,128)(2,1)S(1)}, bf16[128,1536]{1,0:T(8,128)(2,1)S(1)}, u32[]{:S(2)}, u32[]{:S(2)}) collective-permute-start(bf16[128,1536]{1,0:T(8,128)(2,1)S(1)} %get-tuple-element.771), channel_id=1, source_target_pairs={{1,0},{2,3},{5,4},{6,7},{9,8},{10,11},{13,12},{14,15},{17,16},{18,... | collective-permute-start | bytes 1179656 | tf_op jit(solution)/shard_map/ppermute | solution.py:535
  550.9 13.9 %collective-permute-start.85 = (bf16[128,1536]{1,0:T(8,128)(2,1)S(1)}, bf16[128,1536]{1,0:T(8,128)(2,1)S(1)}, u32[]{:S(2)}, u32[]{:S(2)}) collective-permute-start(bf16[128,1536]{1,0:T(8,128)(2,1)S(1)} %relay.35), channel_id=1, source_target_pairs={{1,0},{2,3},{5,4},{6,7},{9,8},{10,11},{13,12},{14,15},{17,16},{18,... | collective-permute-start | bytes 1179656 | tf_op jit(solution)/shard_map/ppermute | solution.py:535
  (245 other events, 1872.9 us)
Sparse Core Ops, SparseCore 0:
  43.2 58.1 all-reduce.3
  103.2 40.2 all-gather.1
  320.9 51.2 reduce-scatter.5
  375.8 52.0 reduce-scatter.7
  496.8 38.0 reduce-scatter.3
